TPU v7x, 32 devices: a whole 2x2x4 slice. The times are simulated.
32 devices in a mesh: groups: 2 (over x), attn: 16 (over z, y, core).
Axes of the slice: x: 2, y: 2, z: 4, core: 2. Of those that a mesh axis runs over, the one named last changes fastest.
Arguments:
- queries: bfloat16 [384, 6144], P(('groups', 'attn')), parts along dimension 0, may hold values from -64 to 64
- residual: bfloat16 [384, 6144], P(('groups', 'attn')), parts along dimension 0, may hold values from -6 to 6
- new_keys: bfloat16 [384, 1024], P(('groups', 'attn')), parts along dimension 0, may hold values from -6 to 6
- new_values: bfloat16 [384, 1024], P(('groups', 'attn')), parts along dimension 0, may hold values from -6 to 6
- key_pool: bfloat16 [3072, 16, 1024], P(('groups', 'attn')), parts along dimension 0, may hold values from -4 to 4
- value_pool: bfloat16 [3072, 16, 1024], P(('groups', 'attn')), parts along dimension 0, may hold values from -6 to 6
- page_table: int32 [384, 8], P(('groups', 'attn')), parts along dimension 0, may hold values from 0 to 95, as said below
- lengths: int32 [384], P(('groups', 'attn')), parts along dimension 0, may hold values from 2 to 127
- migrate: int32 [64], P(('groups', 'attn')), parts along dimension 0, may hold values from 0 to 11, as said below
- chosen: int32 [384, 2], P(('groups', 'attn')), parts along dimension 0, may hold values from 0 to 7, as said below
- router_weight: bfloat16 [6144, 8], replicated, may hold values from -0.078125 to 0.078125
- w_gate: bfloat16 [6144, 2048], P(None, 'attn'), may hold values from -0.078125 to 0.078125
- w_up: bfloat16 [6144, 2048], P(None, 'attn'), may hold values from -0.078125 to 0.078125
- w_down: bfloat16 [2048, 6144], P('attn'), may hold values from -0.1875 to 0.1875
Outputs:
- mixed: bfloat16 [384, 6144], P(('groups', 'attn')), parts along dimension 0
- moved_keys: bfloat16 [64, 128, 1024], P(('groups', 'attn')), parts along dimension 0
- moved_values: bfloat16 [64, 128, 1024], P(('groups', 'attn')), parts along dimension 0
There are 2 independent parts, one for each index of `groups`. A program takes and returns all parts, laid end to end along the dimension named above; an argument that names none is the same for every part. Nothing has to cross between parts.
Inputs may be any that keep to these rules, and one draw needn't show every extreme that they name: `page_table`: the 8 entries of the 12 requests of one device name every page 0 to 95 of that device once. `migrate`: the 2 entries of one device are different slots of its requests. `chosen`: A request names two different experts. Of the requests of one device at most 5 name expert e, for each e < 2, and for each such e some device has exactly 5.
All inputs are finite; a program needn't handle non-finite values.
Results may differ from a plain program's by a relative error of at most 0.0065.
Values may be sent and summed in bfloat16 or wider, within the bound.
No kernel may reach another device: no remote copies, remote signals or barrier semaphores. Data moves between devices by JAX's collectives and lax.ppermute only.
A program may use at most 192 MiB of HBM per device.

v0:
```python
import math

import jax
import jax.numpy as jnp
from jax import lax
from jax.sharding import PartitionSpec as P

HEAD_DIM = 128
CAP = 5
EXP_ON = 2


def passed_along(array, axis, by):
    length = lax.axis_size(axis)
    return lax.ppermute(array, axis, [(i, (i + by) % length) for i in range(length)])


def build_sequence(pool_pages, table_rows, lengths_here, fresh_rows):
    gathered = jnp.take(pool_pages, table_rows, axis=0)
    sequence = gathered.reshape(table_rows.shape[0], -1, pool_pages.shape[-1])
    positions = jnp.arange(sequence.shape[1], dtype=jnp.int32)[None, :, None]
    boundary = lengths_here[:, None, None]
    sequence = jnp.where(positions < boundary, sequence, jnp.zeros_like(sequence))
    return jnp.where(positions == boundary, fresh_rows[:, None, :], sequence)


def attend(query_rows, key_rows, value_rows, lengths_here):
    row_count = query_rows.shape[0]
    kv_count = key_rows.shape[-1] // HEAD_DIM
    group_size = query_rows.shape[-1] // key_rows.shape[-1]
    position_count = key_rows.shape[1]
    query_split = query_rows.reshape(row_count, kv_count, group_size, HEAD_DIM)
    key_split = key_rows.reshape(row_count, position_count, kv_count, HEAD_DIM)
    value_split = value_rows.reshape(row_count, position_count, kv_count, HEAD_DIM)
    scores = jnp.einsum(
        "rkgd,rskd->rkgs", query_split, key_split, preferred_element_type=jnp.float32
    ) / math.sqrt(HEAD_DIM)
    positions = jnp.arange(position_count, dtype=jnp.int32)
    visible = positions[None, None, None, :] <= lengths_here[:, None, None, None]
    scores = jnp.where(visible, scores, -jnp.inf)
    highest = jnp.max(scores, axis=-1, keepdims=True)
    exponent = jnp.where(visible, jnp.exp(scores - highest), 0.0)
    probs = (exponent / jnp.sum(exponent, axis=-1, keepdims=True)).astype(jnp.bfloat16)
    attended = jnp.einsum("rkgs,rskd->rkgd", probs, value_split, preferred_element_type=jnp.float32)
    return attended.reshape(row_count, -1).astype(jnp.bfloat16)


def gate_weights(normed, router_weight, chosen):
    logits = jnp.dot(normed, router_weight, preferred_element_type=jnp.float32)
    first_logit = jnp.take_along_axis(logits, chosen[:, 0:1], axis=1)[:, 0]
    second_logit = jnp.take_along_axis(logits, chosen[:, 1:2], axis=1)[:, 0]
    first_weight = 1.0 / (1.0 + jnp.exp(second_logit - first_logit))
    second_weight = 1.0 / (1.0 + jnp.exp(first_logit - second_logit))
    stacked = []
    for expert in range(EXP_ON):
        stacked.append(
            jnp.where(chosen[:, 0] == expert, first_weight, 0.0)
            + jnp.where(chosen[:, 1] == expert, second_weight, 0.0)
        )
    return jnp.stack(stacked, axis=0)


def slot_table(chosen, slot_count):
    expert_ids = jnp.arange(EXP_ON, dtype=jnp.int32)[:, None]
    wanted = (chosen[None, :, 0] == expert_ids) | (chosen[None, :, 1] == expert_ids)
    position_of = jnp.cumsum(wanted.astype(jnp.int32), axis=1) - 1
    slot_ids = jnp.arange(slot_count, dtype=jnp.int32)[None, :, None]
    selector = wanted[:, None, :] & (position_of[:, None, :] == slot_ids)
    return (wanted, position_of, selector)


def unpack(expert_sums, wanted, position_of, weights_here):
    accumulated = jnp.zeros((wanted.shape[1], expert_sums.shape[-1]), jnp.float32)
    for expert in range(expert_sums.shape[0]):
        index_rows = jnp.clip(position_of[expert], 0, expert_sums.shape[1] - 1)
        picked = jnp.take(expert_sums[expert], index_rows, axis=0)
        factor = jnp.where(wanted[expert], weights_here[expert], 0.0)
        accumulated = accumulated + factor[:, None] * picked
    return accumulated


def body(
    queries,
    residual,
    new_keys,
    new_values,
    key_pool,
    value_pool,
    page_table,
    lengths,
    migrate,
    chosen,
    router_weight,
    w_gate,
    w_up,
    w_down,
):
    device_count = lax.axis_size("attn")
    model_width = residual.shape[1]
    key_seq = build_sequence(key_pool, page_table, lengths, new_keys)
    value_seq = build_sequence(value_pool, page_table, lengths, new_values)
    leave_keys = jnp.take(key_seq, migrate, axis=0)
    leave_values = jnp.take(value_seq, migrate, axis=0)
    arrived_keys, arrived_values = passed_along((leave_keys, leave_values), "attn", 1)
    attended = attend(queries, key_seq, value_seq, lengths)
    state = residual.astype(jnp.float32) + attended.astype(jnp.float32)
    normed = (state * lax.rsqrt(jnp.mean(state * state, axis=1, keepdims=True) + 1e-05)).astype(
        jnp.bfloat16
    )
    weights_here = gate_weights(normed, router_weight, chosen)
    wanted, position_of, selector = slot_table(chosen, CAP)
    packed = jnp.einsum(
        "ecr,rd->ecd", selector.astype(jnp.bfloat16), normed, preferred_element_type=jnp.float32
    ).astype(jnp.bfloat16)
    per_expert = device_count // EXP_ON
    outgoing = jnp.repeat(packed, per_expert, axis=0)
    rows_in = lax.all_to_all(outgoing, "attn", split_axis=0, concat_axis=0, tiled=True)
    flat_rows = rows_in.reshape(-1, model_width)
    gate_part = jnp.dot(flat_rows, w_gate, preferred_element_type=jnp.float32)
    up_part = jnp.dot(flat_rows, w_up, preferred_element_type=jnp.float32)
    hidden_units = (jax.nn.silu(gate_part) * up_part).astype(jnp.bfloat16)
    expert_out = jnp.dot(hidden_units, w_down, preferred_element_type=jnp.float32)
    partial_sums = expert_out.reshape(rows_in.shape[0], rows_in.shape[1], model_width)
    arrived_sums = lax.all_to_all(
        partial_sums.astype(jnp.bfloat16), "attn", split_axis=0, concat_axis=0, tiled=True
    ).astype(partial_sums.dtype)
    expert_sums = arrived_sums.reshape(EXP_ON, per_expert, CAP, model_width).sum(axis=1)
    addition = unpack(expert_sums, wanted, position_of, weights_here)
    mixed = (state + addition).astype(jnp.bfloat16)
    return (mixed, arrived_keys, arrived_values)


def solution(mesh):
    placed = (
        P(("groups", "attn"), None),
        P(("groups", "attn"), None),
        P(("groups", "attn"), None),
        P(("groups", "attn"), None),
        P(("groups", "attn"), None, None),
        P(("groups", "attn"), None, None),
        P(("groups", "attn"), None),
        P(("groups", "attn")),
        P(("groups", "attn")),
        P(("groups", "attn"), None),
        P(),
        P(None, "attn"),
        P(None, "attn"),
        P("attn", None),
    )
    return jax.shard_map(
        body,
        mesh=mesh,
        in_specs=placed,
        out_specs=(
            P(("groups", "attn"), None),
            P(("groups", "attn"), None, None),
            P(("groups", "attn"), None, None),
        ),
        check_vma=False,
    )
```

profile of v0, /device:TPU:13, one launch (start us, length us, event | category | flops | bytes accessed | tf_op | source)
XLA Modules:
  0.0 163.1 jit_solution(12127568732852339962)
XLA Ops:
  2.5 2.5 %gather_fusion = bf16[96,16,1024]{2,1,0:T(8,128)(2,1)} fusion(bf16[96,16,1024]{2,1,0:T(8,128)(2,1)S(1)} %copy-done, s32[1024]{0:T(1024)S(1)} %pad_clamp_fusion.3), kind=kCustom, calls=%fused_computation.clone | custom fusion | bytes 6291840 | tf_op jit(solution)/shard_map/jit(_take)/gather | solution.py:19
  5.1 4.5 %gather_fusion.1 = bf16[96,16,1024]{2,1,0:T(8,128)(2,1)} fusion(bf16[96,16,1024]{2,1,0:T(8,128)(2,1)} %param.27, s32[1024]{0:T(1024)S(1)} %pad_clamp_fusion.3), kind=kCustom, calls=%fused_computation.4.clone | custom fusion | bytes 6291840 | tf_op jit(solution)/shard_map/jit(_take)/gather | solution.py:19
  9.6 3.2 %broadcast_select_fusion.1 = (bf16[12,8,16,1024]{3,2,1,0:T(8,128)(2,1)S(1)}, bf16[12,8,16,1024]{3,2,1,0:T(8,128)(2,1)S(1)}) fusion(bf16[12,8,16,1024]{3,2,1,0:T(8,128)(2,1)} %bitcast.98, pred[12,8]{1,0:T(8,128)(4,1)S(1)} %copy.21, bf16[12,8,16,1024]{3,2,1,0:T(8,128)(2,1)} %bitcast.99), kind=kLoop, calls=%fused_computation.25 | loop fusion | flops 3145728 | bytes 12583008 | tf_op jit(solution)/shard_map/jit(_take)/select_n | solution.py:19
  12.8 2.9 %copy.30 = bf16[192,8,8,128]{3,2,1,0:T(8,128)(2,1)} copy(bf16[192,8,8,128]{3,1,2,0:T(8,128)(2,1)S(1)} %bitcast.95) | data formatting | bytes 6291456
  16.4 2.6 %copy.28 = bf16[192,8,8,128]{3,2,1,0:T(8,128)(2,1)} copy(bf16[192,8,8,128]{3,1,2,0:T(8,128)(2,1)S(1)} %bitcast.94) | data formatting | bytes 6291456
  20.5 8.5 %fusion.2 = (bf16[12,128,8,128]{3,2,1,0:T(8,128)(2,1)}, bf16[12,128,8,128]{3,2,1,0:T(8,128)(2,1)}) fusion(pred[12,128]{1,0:T(8,128)(4,1)S(1)} %get-tuple-element.38, pred[12,128]{1,0:T(8,128)(4,1)S(1)} %get-tuple-element.37, bf16[12,8,128]{2,1,0:T(8,128)(2,1)} %slice.60, bf16[12,8,128]{2,1,0:T(8,128)(2,1)} %slice.61, bf16[12,128,8,128]{3,2,1,0:T(8,128)(2,1)} %bitcast.97, ...), kind=kLoop, calls=%fused_computation.14 | loop fusion | flops 6291456 | bytes 12635136 | tf_op jit(solution)/shard_map/jit(_where)/select_n | solution.py:24
  29.0 4.5 %fusion.53 = (f32[12,8,6]{2,1,0:T(8,128)S(1)}, f32[12,8,6,128]{3,2,1,0:T(8,128)}) fusion(pred[12,128]{1,0:T(8,128)(4,1)S(1)} %get-tuple-element.36, bf16[12,8,6,128]{3,2,1,0:T(8,128)(2,1)S(1)} %reshape.208, bf16[12,128,8,128]{3,2,1,0:T(8,128)(2,1)} %get-tuple-element.20), kind=kOutput, calls=%fused_computation.107 | convolution fusion | flops 19243136 | bytes 3591936 | tf_op jit(solution)/shard_map/sub | solution.py:42
  33.5 3.8 %fusion.24 = f32[12,8,6,128]{3,2,1,0:T(8,128)} fusion(bf16[12,128,8,128]{3,2,1,0:T(8,128)(2,1)} %get-tuple-element.21, f32[12,8,6,128]{3,2,1,0:T(8,128)} %get-tuple-element.40, f32[12,8,6]{2,1,0:T(8,128)S(1)} %get-tuple-element.39), kind=kOutput, calls=%fused_computation.33 | convolution fusion | flops 19169280 | bytes 3737856 | tf_op jit(solution)/shard_map/rkgs,rskd->rkgd/dot_general | solution.py:44
  38.4 1.2 multiply_reduce_fusion
  39.6 1.7 %multiply_convert_fusion = bf16[12,6144]{1,0:T(8,128)(2,1)} fusion(f32[12]{0:T(128)S(1)} %add_rsqrt_fusion, f32[12,6144]{1,0:T(8,128)S(1)} %reshape.217, bf16[12,6144]{1,0:T(8,128)(2,1)} %param.23), kind=kLoop, calls=%fused_computation.43 | loop fusion | flops 294912 | bytes 589872 | tf_op jit(solution)/shard_map/convert_element_type | solution.py:107
  45.0 1.3 broadcast_in_dim.134
  46.4 6.6 %all-to-all-start = ((bf16[16,5,6144]{2,1,0:T(8,128)(2,1)}), bf16[16,5,6144]{2,1,0:T(8,128)(2,1)}, u32[]{:S(2)}, u32[]{:S(2)}) async-start(bf16[16,5,6144]{2,1,0:T(8,128)(2,1)} %bitcast.100), calls=%async_computation | async-start | bytes 3145728 | tf_op jit(solution)/shard_map/all_to_all | solution.py:117
  53.6 5.0 %fusion.3 = (bf16[12,128,1024]{2,1,0:T(8,128)(2,1)}, bf16[12,128,1024]{2,1,0:T(8,128)(2,1)}) fusion(bf16[12,8,16,1024]{3,2,1,0:T(8,128)(2,1)} %copy-done.2, pred[12,128]{1,0:T(8,128)(4,1)S(1)} %get-tuple-element.38, pred[12,128]{1,0:T(8,128)(4,1)S(1)} %get-tuple-element.37, bf16[12,1024]{1,0:T(8,128)(2,1)} %param.25, bf16[12,8,16,1024]{3,2,1,0:T(8,128)(2,1)} %copy-done.1, ...), kind=kLoop, calls=%fused_computation.17 | loop fusion | flops 6291456 | bytes 12635136 | tf_op jit(solution)/shard_map/jit(_where)/select_n | solution.py:24
  58.5 3.3 %gather_fusion.6 = bf16[2,128,1024]{2,1,0:T(8,128)(2,1)} fusion(bf16[12,128,1024]{2,1,0:T(8,128)(2,1)} %get-tuple-element.19, s32[1024]{0:T(1024)S(1)} %pad_clamp_fusion), kind=kCustom, calls=%fused_computation.3.clone | custom fusion | bytes 1048584 | tf_op jit(solution)/shard_map/jit(_take)/gather | solution.py:102
  61.8 3.3 %gather_fusion.7 = bf16[2,128,1024]{2,1,0:T(8,128)(2,1)} fusion(bf16[12,128,1024]{2,1,0:T(8,128)(2,1)} %get-tuple-element.18, s32[1024]{0:T(1024)S(1)} %pad_clamp_fusion), kind=kCustom, calls=%fused_computation.7.clone | custom fusion | bytes 1048584 | tf_op jit(solution)/shard_map/jit(_take)/gather | solution.py:103
  65.1 24.1 %all-to-all-done = bf16[16,5,6144]{2,1,0:T(8,128)(2,1)} async-done(((bf16[16,5,6144]{2,1,0:T(8,128)(2,1)}), bf16[16,5,6144]{2,1,0:T(8,128)(2,1)}, u32[]{:S(2)}, u32[]{:S(2)}) %all-to-all-start) | async-done | bytes 983072 | tf_op jit(solution)/shard_map/all_to_all | solution.py:117
  89.2 2.4 %reshape.211 = bf16[80,6144]{1,0:T(8,128)(2,1)} reshape(bf16[16,5,6144]{2,1,0:T(8,128)(2,1)} %all-to-all-done) | data formatting | bytes 1966080 | tf_op jit(solution)/shard_map/reshape | solution.py:118
  91.6 2.1 %fusion.57 = f32[80,128]{1,0:T(8,128)S(1)} fusion(bf16[80,6144]{1,0:T(8,128)(2,1)} %reshape.211, bf16[6144,128]{1,0:T(8,128)(2,1)} %param.33), kind=kOutput, calls=%fused_computation.109 | convolution fusion | flops 125829120 | bytes 2596864 | tf_op jit(solution)/shard_map/dot_general | solution.py:119
  93.7 4.0 %convolution_convert_fusion = bf16[80,6144]{1,0:T(8,128)(2,1)} fusion(bf16[128,6144]{1,0:T(8,128)(2,1)} %param.35, bf16[80,6144]{1,0:T(8,128)(2,1)} %reshape.211, bf16[6144,128]{1,0:T(8,128)(2,1)} %param.34, f32[80,128]{1,0:T(8,128)S(1)} %fusion.57), kind=kOutput, calls=%fused_computation.9 | convolution fusion | flops 252211200 | bytes 5152768 | tf_op jit(solution)/shard_map/dot_general | solution.py:122
  97.7 2.4 %convert_element_type.49 = bf16[16,5,6144]{2,1,0:T(8,128)(2,1)} reshape(bf16[80,6144]{1,0:T(8,128)(2,1)} %convolution_convert_fusion) | data formatting | bytes 1966080 | tf_op jit(solution)/shard_map/convert_element_type | solution.py:125
  100.1 5.1 %all-to-all-start.1 = ((bf16[16,5,6144]{2,1,0:T(8,128)(2,1)}), bf16[16,5,6144]{2,1,0:T(8,128)(2,1)}, u32[]{:S(2)}, u32[]{:S(2)}) async-start(bf16[16,5,6144]{2,1,0:T(8,128)(2,1)} %convert_element_type.49), calls=%async_computation.1 | async-start | bytes 3145728 | tf_op jit(solution)/shard_map/all_to_all | solution.py:124
  105.2 2.3 %broadcast_select_fusion.2 = (bf16[2,128,1024]{2,1,0:T(8,128)(2,1)}, bf16[2,128,1024]{2,1,0:T(8,128)(2,1)}) fusion(bf16[2,128,1024]{2,1,0:T(8,128)(2,1)} %gather_fusion.7, pred[2]{0:T(512)(128)(4,1)S(1)} %compare_and_fusion.1, bf16[2,128,1024]{2,1,0:T(8,128)(2,1)} %gather_fusion.6), kind=kLoop, calls=%fused_computation.36 | loop fusion | flops 524288 | bytes 2097154 | tf_op jit(solution)/shard_map/jit(_take)/select_n | solution.py:103
  107.5 1.4 collective-permute-start
  112.4 33.0 %collective-permute-done = bf16[2,128,1024]{2,1,0:T(8,128)(2,1)} collective-permute-done((bf16[2,128,1024]{2,1,0:T(8,128)(2,1)}, bf16[2,128,1024]{2,1,0:T(8,128)(2,1)}, u32[]{:S(2)}, u32[]{:S(2)}) %collective-permute-start) | collective-permute-done | bytes 524320 | tf_op jit(solution)/shard_map/ppermute | solution.py:15
  145.5 5.6 %collective-permute-done.1 = bf16[2,128,1024]{2,1,0:T(8,128)(2,1)} collective-permute-done((bf16[2,128,1024]{2,1,0:T(8,128)(2,1)}, bf16[2,128,1024]{2,1,0:T(8,128)(2,1)}, u32[]{:S(2)}, u32[]{:S(2)}) %collective-permute-start.1) | collective-permute-done | bytes 524320 | tf_op jit(solution)/shard_map/ppermute | solution.py:15
  151.1 1.6 %all-to-all-done.1 = bf16[16,5,6144]{2,1,0:T(8,128)(2,1)} async-done(((bf16[16,5,6144]{2,1,0:T(8,128)(2,1)}), bf16[16,5,6144]{2,1,0:T(8,128)(2,1)}, u32[]{:S(2)}, u32[]{:S(2)}) %all-to-all-start.1) | async-done | bytes 983072 | tf_op jit(solution)/shard_map/all_to_all | solution.py:124
  152.7 1.8 %convert_reduce_fusion = f32[2,5,6144]{2,1,0:T(8,128)S(1)} fusion(bf16[16,5,6144]{2,1,0:T(8,128)(2,1)} %all-to-all-done.1), kind=kLoop, calls=%fused_computation.15 | loop fusion | flops 921600 | bytes 1228800 | tf_op jit(solution)/shard_map/reduce_sum | solution.py:127
  154.5 1.4 gather_fusion.4
  155.9 1.4 gather_fusion.5
  157.3 2.1 %fusion.30 = bf16[12,6144]{1,0:T(8,128)(2,1)} fusion(f32[12,6144]{1,0:T(8,128)} %gather_fusion.5, f32[12,6144]{1,0:T(8,128)} %gather_fusion.4, f32[12]{0:T(128)S(1)} %copy-done.14, f32[12]{0:T(128)} %get-tuple-element.11, pred[12]{0:T(512)(128)(4,1)S(1)} %copy-done.13, pred[12]{0:T(512)(128)(4,1)S(1)} %copy-done.12, f32[12,6144]{1,0:T(8,128)} %copy-done.3, ...), kind=kLoop, calls=%fused_computation.41 | loop fusion | flops 663552 | bytes 1179768 | tf_op jit(solution)/shard_map/convert_element_type | solution.py:129
  159.4 1.9 %copy.49 = bf16[2,128,1024]{2,1,0:T(8,128)(2,1)} copy(bf16[2,128,1024]{2,1,0:T(8,128)(2,1)} %collective-permute-done) | data formatting | bytes 1048576
  161.3 1.9 %copy.50 = bf16[2,128,1024]{2,1,0:T(8,128)(2,1)} copy(bf16[2,128,1024]{2,1,0:T(8,128)(2,1)} %collective-permute-done.1) | data formatting | bytes 1048576
  (73 shorter events, 13.1 us)
Async XLA Ops:
  0.6 1.9 %copy-start = (bf16[96,16,1024]{2,1,0:T(8,128)(2,1)S(1)}, bf16[96,16,1024]{2,1,0:T(8,128)(2,1)}, u32[]{:S(2)}) copy-start(bf16[96,16,1024]{2,1,0:T(8,128)(2,1)} %param.26) | copy-start | bytes 9437188
  12.8 2.9 %copy-start.2 = (bf16[12,8,16,1024]{3,2,1,0:T(8,128)(2,1)}, bf16[12,8,16,1024]{3,2,1,0:T(8,128)(2,1)S(1)}, u32[]{:S(2)}) copy-start(bf16[12,8,16,1024]{3,2,1,0:T(8,128)(2,1)S(1)} %get-tuple-element.23) | copy-start | bytes 9437188
  12.8 3.6 %copy-start.1 = (bf16[12,8,16,1024]{3,2,1,0:T(8,128)(2,1)}, bf16[12,8,16,1024]{3,2,1,0:T(8,128)(2,1)S(1)}, u32[]{:S(2)}) copy-start(bf16[12,8,16,1024]{3,2,1,0:T(8,128)(2,1)S(1)} %get-tuple-element.22) | copy-start | bytes 9437188
  16.4 2.6 %copy-start.17 = (s32[12]{0:T(128)S(1)}, s32[12]{0:T(128)}, u32[]{:S(2)}) copy-start(s32[12]{0:T(128)} %param.29) | copy-start | bytes 148
  16.4 2.7 %copy-start.7 = (bf16[12,1024]{1,0:T(8,128)(2,1)S(1)}, bf16[12,1024]{1,0:T(8,128)(2,1)}, u32[]{:S(2)}) copy-start(bf16[12,1024]{1,0:T(8,128)(2,1)} %param.24) | copy-start | bytes 73732
  16.4 3.3 %copy-start.8 = (bf16[12,1024]{1,0:T(8,128)(2,1)S(1)}, bf16[12,1024]{1,0:T(8,128)(2,1)}, u32[]{:S(2)}) copy-start(bf16[12,1024]{1,0:T(8,128)(2,1)} %param.25) | copy-start | bytes 73732
  16.4 3.9 %copy-start.6 = (bf16[12,6144]{1,0:T(8,128)(2,1)S(1)}, bf16[12,6144]{1,0:T(8,128)(2,1)}, u32[]{:S(2)}) copy-start(bf16[12,6144]{1,0:T(8,128)(2,1)} %param.22) | copy-start | bytes 442372
  33.5 7.8 %copy-start.10 = (s32[12,2]{0,1:T(2,128)S(1)}, s32[12,2]{0,1:T(2,128)}, u32[]{:S(2)}) copy-start(s32[12,2]{0,1:T(2,128)} %param.31) | copy-start | bytes 292
  38.3 8.0 %copy-start.3 = (f32[12,6144]{1,0:T(8,128)}, f32[12,6144]{1,0:T(8,128)S(1)}, u32[]{:S(2)}) copy-start(f32[12,6144]{1,0:T(8,128)S(1)} %reshape.217) | copy-start | bytes 884740
  46.4 42.8 %all-to-all-start = ((bf16[16,5,6144]{2,1,0:T(8,128)(2,1)}), bf16[16,5,6144]{2,1,0:T(8,128)(2,1)}, u32[]{:S(2)}, u32[]{:S(2)}) async-start(bf16[16,5,6144]{2,1,0:T(8,128)(2,1)} %bitcast.100), calls=%async_computation | async-start | bytes 3145728 | tf_op jit(solution)/shard_map/all_to_all | solution.py:117
  53.6 11.5 %copy-start.18 = (s32[2]{0:T(128)S(1)}, s32[2]{0:T(128)}, u32[]{:S(2)}) copy-start(s32[2]{0:T(128)} %param.30) | copy-start | bytes 28
  100.1 9.0 %copy-start.15 = (s32[12,1,1]{0,2,1:T(1,128)S(1)}, s32[12,1,1]{0,2,1:T(1,128)}, u32[]{:S(2)}) copy-start(s32[12,1,1]{0,2,1:T(1,128)} %get-tuple-element.26) | copy-start | bytes 148
  100.1 9.0 %copy-start.16 = (s32[12,1,1]{0,2,1:T(1,128)S(1)}, s32[12,1,1]{0,2,1:T(1,128)}, u32[]{:S(2)}) copy-start(s32[12,1,1]{0,2,1:T(1,128)} %get-tuple-element.27) | copy-start | bytes 148
  100.1 9.0 %copy-start.5 = (bf16[12,6144]{1,0:T(8,128)(2,1)S(1)}, bf16[12,6144]{1,0:T(8,128)(2,1)}, u32[]{:S(2)}) copy-start(bf16[12,6144]{1,0:T(8,128)(2,1)} %multiply_convert_fusion) | copy-start | bytes 442372
  100.1 9.0 %copy-start.9 = (bf16[6144,8]{0,1:T(8,128)(2,1)S(1)}, bf16[6144,8]{0,1:T(8,128)(2,1)}, u32[]{:S(2)}) copy-start(bf16[6144,8]{0,1:T(8,128)(2,1)} %param.32) | copy-start | bytes 294916
  100.1 11.2 %copy-start.11 = (pred[2,12]{1,0:T(4,128)(4,1)S(1)}, pred[2,12]{1,0:T(4,128)(4,1)}, u32[]{:S(2)}) copy-start(pred[2,12]{1,0:T(4,128)(4,1)} %get-tuple-element.15) | copy-start | bytes 76
  100.1 52.6 %all-to-all-start.1 = ((bf16[16,5,6144]{2,1,0:T(8,128)(2,1)}), bf16[16,5,6144]{2,1,0:T(8,128)(2,1)}, u32[]{:S(2)}, u32[]{:S(2)}) async-start(bf16[16,5,6144]{2,1,0:T(8,128)(2,1)} %convert_element_type.49), calls=%async_computation.1 | async-start | bytes 3145728 | tf_op jit(solution)/shard_map/all_to_all | solution.py:124
  107.5 37.9 %collective-permute-start = (bf16[2,128,1024]{2,1,0:T(8,128)(2,1)}, bf16[2,128,1024]{2,1,0:T(8,128)(2,1)}, u32[]{:S(2)}, u32[]{:S(2)}) collective-permute-start(bf16[2,128,1024]{2,1,0:T(8,128)(2,1)} %get-tuple-element.33), channel_id=1, source_target_pairs={{0,1},{1,2},{2,3},{3,4},{4,5},{5,6},{6,7},{7,8},{8,9},{9,10},{10,1... | collective-permute-start | bytes 1572872 | tf_op jit(solution)/shard_map/ppermute | solution.py:15
  108.9 42.1 %collective-permute-start.1 = (bf16[2,128,1024]{2,1,0:T(8,128)(2,1)}, bf16[2,128,1024]{2,1,0:T(8,128)(2,1)}, u32[]{:S(2)}, u32[]{:S(2)}) collective-permute-start(bf16[2,128,1024]{2,1,0:T(8,128)(2,1)} %get-tuple-element.32), channel_id=1, source_target_pairs={{0,1},{1,2},{2,3},{3,4},{4,5},{5,6},{6,7},{7,8},{8,9},{9,10},{10,1... | collective-permute-start | bytes 1572872 | tf_op jit(solution)/shard_map/ppermute | solution.py:15
  154.5 2.8 %copy-start.12 = (pred[12]{0:T(512)(128)(4,1)S(1)}, pred[12]{0:T(512)(128)(4,1)}, u32[]{:S(2)}) copy-start(pred[12]{0:T(512)(128)(4,1)} %get-tuple-element.6) | copy-start | bytes 40
  154.5 2.8 %copy-start.13 = (pred[12]{0:T(512)(128)(4,1)S(1)}, pred[12]{0:T(512)(128)(4,1)}, u32[]{:S(2)}) copy-start(pred[12]{0:T(512)(128)(4,1)} %get-tuple-element.30) | copy-start | bytes 40
  155.9 1.4 copy-start.4
  155.9 1.4 copy-start.14
where the time goes:
time: 164 us; the launch traced here: 163 us
  waiting for transfers between devices  64.4 us (39%)
  local copies, waits for them, and re-layouts  36.5 us (22%)
  other arithmetic  32.5 us (20%)
  matrix products  15.6 us (10%)
  starting transfers between devices  13.2 us (8%)
    ppermute x2, waiting for transfers between devices, passed_along(): lax.ppermute(array, axis, [(i, (i + by) % length) for i in range(length)])  38.6 us
    all_to_all x1, waiting for transfers between devices, body(): lax.all_to_all(outgoing, 'attn', split_axis=0, concat_axis=0, tiled=True)  24.1 us
    select_n x2, other arithmetic, build_sequence(): return jnp.where(positions == boundary, fresh_rows[:, None, :], sequence)  13.5 us
    unnamed x44, local copies, waits for them, and re-layouts  10 us
    gather x2, local copies, waits for them, and re-layouts, build_sequence(): gathered = jnp.take(pool_pages, table_rows, axis=0)  6.98 us
    all_to_all x1, starting transfers between devices, body(): lax.all_to_all(outgoing, 'attn', split_axis=0, concat_axis=0, tiled=True)  6.56 us
    all_to_all x1, starting transfers between devices, body(): lax.all_to_all(partial_sums.astype(jnp.bfloat16), 'attn', split_axis=0, c...  5.06 us
    sub x1, matrix products, attend(): exponent = jnp.where(visible, jnp.exp(scores - highest), 0.0)  4.47 us
  transfers between devices with their start and end apart: 4, of which 4 were waited for; matrix products, arithmetic and copies ran while one was open for 11% of the time, Pallas kernels for 0%

commit v1 on v0

v1 whole, which is shorter than its diff:
```python
import math

import jax
import jax.numpy as jnp
from jax import lax
from jax.experimental import pallas as pl
from jax.experimental.pallas import tpu as pltpu
from jax.sharding import PartitionSpec as P

HEAD_DIM = 128
CAP = 5
EXP_ON = 2
F32 = jnp.float32
BF16 = jnp.bfloat16

SMEM = pl.BlockSpec(memory_space=pltpu.SMEM)
VMEM = pl.BlockSpec(memory_space=pltpu.VMEM)
ANY = pl.BlockSpec(memory_space=pl.ANY)


def exchanged(array, mask):
    length = lax.axis_size("attn")
    return lax.ppermute(array, "attn", [(i, i ^ mask) for i in range(length)])


def migrate_kernel(table, lengths, migrate, new_keys, new_values, key_pool, value_pool,
                   out_keys, out_values, fresh, sems):
    moves, positions, _ = out_keys.shape
    page = key_pool.shape[1]
    pages = positions // page
    sides = ((key_pool, out_keys), (value_pool, out_values))
    for m in range(moves):
        request = migrate[m]
        for p in range(pages):
            number = table[request, p]
            for side, (pool, out) in enumerate(sides):
                pltpu.make_async_copy(
                    pool.at[number], out.at[m, pl.ds(p * page, page)], sems.at[side, m]
                ).start()
    fresh[0] = new_keys[...].astype(F32)
    fresh[1] = new_values[...].astype(F32)
    for m in range(moves):
        request = migrate[m]
        length = lengths[request]
        for side, (pool, out) in enumerate(sides):
            pltpu.make_async_copy(out.at[m], out.at[m], sems.at[side, m]).wait()
            row = fresh[side, pl.ds(request, 1), :]
            for p in range(pages):
                block = out[m, pl.ds(p * page, page), :].astype(F32)
                at = lax.broadcasted_iota(jnp.int32, block.shape, 0) + p * page
                block = jnp.where(at < length, block, jnp.where(at == length, row, 0.0))
                out[m, pl.ds(p * page, page), :] = block.astype(BF16)


def leaving(page_table, lengths, migrate, new_keys, new_values, key_pool, value_pool):
    rows, width = new_keys.shape
    moves = migrate.shape[0]
    positions = page_table.shape[1] * key_pool.shape[1]
    shape = jax.ShapeDtypeStruct((moves, positions, width), BF16)
    return pl.pallas_call(
        migrate_kernel,
        out_shape=(shape, shape),
        in_specs=[SMEM] * 3 + [VMEM] * 2 + [ANY] * 2,
        out_specs=(VMEM, VMEM),
        scratch_shapes=[pltpu.VMEM((2, rows, width), F32), pltpu.SemaphoreType.DMA((2, moves))],
        compiler_params=pltpu.CompilerParams(vmem_limit_bytes=8 << 20),
        cost_estimate=pl.CostEstimate(flops=0, bytes_accessed=4 << 20, transcendentals=0),
    )(page_table, lengths, migrate, new_keys, new_values, key_pool, value_pool)


def attend_kernel(table, lengths, chosen, mine, queries, residual, new_keys, new_values,
                  key_pool, value_pool, state_out, normed_out, own_out, away_out,
                  keys, values, heads_q, heads_r, fresh, sems):
    rows, width = queries.shape
    page = key_pool.shape[1]
    positions = keys.shape[1]
    pages = positions // page
    kv_width = keys.shape[2]
    kv_heads = kv_width // HEAD_DIM
    heads = width // HEAD_DIM
    group = heads // kv_heads
    for r in range(rows):
        for p in range(pages):
            number = table[r, p]
            at = pl.ds(p * page, page)
            pltpu.make_async_copy(key_pool.at[number], keys.at[r, at], sems.at[0, r]).start()
            pltpu.make_async_copy(value_pool.at[number], values.at[r, at], sems.at[1, r]).start()
    fresh[0] = new_keys[...].astype(F32)
    fresh[1] = new_values[...].astype(F32)
    for h in range(heads):
        cols = slice(h * HEAD_DIM, (h + 1) * HEAD_DIM)
        heads_q[pl.ds(h, rows, stride=heads), :] = queries[:, cols].astype(F32)
        heads_r[pl.ds(h, rows, stride=heads), :] = residual[:, cols].astype(F32)
    own_out[...] = jnp.zeros_like(own_out)
    away_out[...] = jnp.zeros_like(away_out)
    head_of = lax.broadcasted_iota(jnp.int32, (heads, HEAD_DIM), 0)
    at_of = lax.broadcasted_iota(jnp.int32, (heads, positions), 1)
    in_group = [(head_of >= g * group) & (head_of < (g + 1) * group) for g in range(kv_heads)]
    expert = mine[0]
    taken = [jnp.int32(0), jnp.int32(0)]
    for r in range(rows):
        length = lengths[r]
        first = pl.multiple_of(length // page * page, page)
        tail = pl.ds(first, page)
        here = lax.broadcasted_iota(jnp.int32, (page, kv_width), 0) == length - first
        for side, buffer in enumerate((keys, values)):
            pltpu.make_async_copy(buffer.at[r], buffer.at[r], sems.at[side, r]).wait()
            block = buffer[r, tail, :].astype(F32)
            block = jnp.where(here, fresh[side, r:r + 1, :], block)
            buffer[r, tail, :] = block.astype(BF16)
        query = heads_q[r * heads:(r + 1) * heads, :]
        spread = jnp.concatenate(
            [jnp.where(inside, query, 0.0).astype(BF16) for inside in in_group], axis=1
        )
        scores = lax.dot_general(
            spread, keys[r], (((1,), (1,)), ((), ())), preferred_element_type=F32
        ) * (1.0 / math.sqrt(HEAD_DIM))
        visible = at_of <= length
        scores = jnp.where(visible, scores, -jnp.inf)
        highest = jnp.max(scores, axis=1, keepdims=True)
        exponent = jnp.where(visible, jnp.exp(scores - highest), 0.0)
        probs = (exponent / jnp.sum(exponent, axis=1, keepdims=True)).astype(BF16)
        mixed = jnp.dot(probs, values[r], preferred_element_type=F32)
        attended = mixed[:, :HEAD_DIM]
        for g in range(1, kv_heads):
            attended = jnp.where(
                in_group[g], mixed[:, g * HEAD_DIM:(g + 1) * HEAD_DIM], attended
            )
        state = heads_r[r * heads:(r + 1) * heads, :] + attended.astype(BF16).astype(F32)
        state_out[r] = state
        square = jnp.sum(jnp.sum(state * state, axis=1, keepdims=True), axis=0, keepdims=True)
        normed = (state * lax.rsqrt(square / width + 1e-05)).astype(BF16)
        normed_out[r] = normed
        for side, (out, number) in enumerate(((own_out, expert), (away_out, 1 - expert))):
            wanted = (chosen[r, 0] == number) | (chosen[r, 1] == number)
            slot = jnp.minimum(taken[side], CAP - 1)

            @pl.when(wanted)
            def _():
                out[slot] = normed

            taken[side] = taken[side] + wanted.astype(jnp.int32)


def attended(page_table, lengths, chosen, mine, queries, residual, new_keys, new_values,
             key_pool, value_pool):
    rows, width = queries.shape
    heads = width // HEAD_DIM
    kv_width = new_keys.shape[1]
    positions = page_table.shape[1] * key_pool.shape[1]
    packed = jax.ShapeDtypeStruct((CAP, heads, HEAD_DIM), BF16)
    return pl.pallas_call(
        attend_kernel,
        out_shape=(
            jax.ShapeDtypeStruct((rows, heads, HEAD_DIM), F32),
            jax.ShapeDtypeStruct((rows, heads, HEAD_DIM), BF16),
            packed,
            packed,
        ),
        in_specs=[SMEM] * 4 + [VMEM] * 4 + [ANY] * 2,
        out_specs=(VMEM,) * 4,
        scratch_shapes=[
            pltpu.VMEM((rows, positions, kv_width), BF16),
            pltpu.VMEM((rows, positions, kv_width), BF16),
            pltpu.VMEM((rows * heads, HEAD_DIM), F32),
            pltpu.VMEM((rows * heads, HEAD_DIM), F32),
            pltpu.VMEM((2, rows, kv_width), F32),
            pltpu.SemaphoreType.DMA((2, rows)),
        ],
        compiler_params=pltpu.CompilerParams(vmem_limit_bytes=16 << 20),
        cost_estimate=pl.CostEstimate(
            flops=400_000_000, bytes_accessed=36 << 20, transcendentals=1 << 17
        ),
    )(page_table, lengths, chosen, mine, queries, residual, new_keys, new_values,
      key_pool, value_pool)


def expert_kernel(kept_rows, given_rows, w_gate, w_up, w_down, kept, given, split, flat, back):
    block, heads, _ = kept_rows.shape
    half = block * heads
    split[:half] = kept_rows[...].astype(F32).reshape(half, HEAD_DIM)
    split[half:] = given_rows[...].astype(F32).reshape(half, HEAD_DIM)
    for h in range(heads):
        cols = slice(h * HEAD_DIM, (h + 1) * HEAD_DIM)
        flat[:, cols] = split[pl.ds(h, 2 * block, stride=heads), :].astype(BF16)
    gate = jnp.dot(flat[...], w_gate[...], preferred_element_type=F32)
    up = jnp.dot(flat[...], w_up[...], preferred_element_type=F32)
    hidden = (gate / (1.0 + jnp.exp(-gate)) * up).astype(BF16)
    wide = 4
    for first in range(0, heads, wide):
        cols = slice(first * HEAD_DIM, (first + wide) * HEAD_DIM)
        part = jnp.dot(hidden, w_down[:, cols], preferred_element_type=F32)
        for h in range(wide):
            back[pl.ds(first + h, 2 * block, stride=heads), :] = part[
                :, h * HEAD_DIM:(h + 1) * HEAD_DIM
            ]
    kept[...] = back[:half].reshape(block, heads, HEAD_DIM)
    given[...] = back[half:].reshape(block, heads, HEAD_DIM).astype(BF16)


def expert_parts(kept_rows, given_rows, w_gate, w_up, w_down):
    total, heads, _ = kept_rows.shape
    block = 8 * CAP
    if total % block:
        block = CAP
    rows = pl.BlockSpec((block, heads, HEAD_DIM), lambda i: (i, 0, 0))

    def fixed(array):
        return pl.BlockSpec(array.shape, lambda i: (0, 0))

    return pl.pallas_call(
        expert_kernel,
        grid=(total // block,),
        out_shape=(
            jax.ShapeDtypeStruct(kept_rows.shape, F32),
            jax.ShapeDtypeStruct(kept_rows.shape, BF16),
        ),
        in_specs=[rows, rows, fixed(w_gate), fixed(w_up), fixed(w_down)],
        out_specs=(rows, rows),
        scratch_shapes=[
            pltpu.VMEM((2 * block * heads, HEAD_DIM), F32),
            pltpu.VMEM((2 * block, heads * HEAD_DIM), BF16),
            pltpu.VMEM((2 * block * heads, HEAD_DIM), F32),
        ],
        compiler_params=pltpu.CompilerParams(vmem_limit_bytes=32 << 20),
        cost_estimate=pl.CostEstimate(
            flops=400_000_000, bytes_accessed=8 << 20, transcendentals=10240
        ),
    )(kept_rows, given_rows, w_gate, w_up, w_down)


def finish_kernel(chosen, mine, weights, state, own, away, mixed, rows_split):
    rows, heads, _ = state.shape
    expert = mine[0]
    taken = [jnp.int32(0), jnp.int32(0)]
    for r in range(rows):
        total = state[r]
        for side, (sums, number) in enumerate(((own, expert), (away, 1 - expert))):
            wanted = (chosen[r, 0] == number) | (chosen[r, 1] == number)
            slot = jnp.minimum(taken[side], CAP - 1)
            factor = jnp.where(wanted, weights[number, r], 0.0)
            total = total + factor * sums[slot].astype(F32)
            taken[side] = taken[side] + wanted.astype(jnp.int32)
        rows_split[r * heads:(r + 1) * heads, :] = total
    for h in range(heads):
        mixed[:, h * HEAD_DIM:(h + 1) * HEAD_DIM] = rows_split[
            pl.ds(h, rows, stride=heads), :
        ].astype(BF16)


def finished(chosen, mine, weights, state, own, away):
    rows, heads, _ = state.shape
    return pl.pallas_call(
        finish_kernel,
        out_shape=jax.ShapeDtypeStruct((rows, heads * HEAD_DIM), BF16),
        in_specs=[SMEM] * 3 + [VMEM] * 3,
        out_specs=VMEM,
        scratch_shapes=[pltpu.VMEM((rows * heads, HEAD_DIM), F32)],
        compiler_params=pltpu.CompilerParams(vmem_limit_bytes=8 << 20),
    )(chosen, mine, weights, state, own, away)


def gate_weights(normed, router_weight, chosen):
    rows, heads, _ = normed.shape
    router = router_weight.reshape(heads, HEAD_DIM, -1)
    logits = jnp.einsum("rhd,hde->re", normed, router, preferred_element_type=F32)
    numbers = jnp.arange(logits.shape[1], dtype=jnp.int32)[None, :]
    first = chosen[:, 0:1]
    second = chosen[:, 1:2]
    first_logit = jnp.sum(jnp.where(numbers == first, logits, 0.0), axis=1, keepdims=True)
    second_logit = jnp.sum(jnp.where(numbers == second, logits, 0.0), axis=1, keepdims=True)
    first_weight = 1.0 / (1.0 + jnp.exp(second_logit - first_logit))
    second_weight = 1.0 / (1.0 + jnp.exp(first_logit - second_logit))
    experts = jnp.arange(EXP_ON, dtype=jnp.int32)[None, :]
    weights = jnp.where(first == experts, first_weight, 0.0) + jnp.where(
        second == experts, second_weight, 0.0
    )
    return weights.T


def body(
    queries,
    residual,
    new_keys,
    new_values,
    key_pool,
    value_pool,
    page_table,
    lengths,
    migrate,
    chosen,
    router_weight,
    w_gate,
    w_up,
    w_down,
):
    length = lax.axis_size("attn")
    swap = length // 2
    masks = list(range(2, swap, 2))
    mine = (lax.axis_index("attn") // (length // EXP_ON)).astype(jnp.int32).reshape(1)
    along = [(i, (i + 1) % length) for i in range(length)]
    leave_keys, leave_values = leaving(
        page_table, lengths, migrate, new_keys, new_values, key_pool, value_pool
    )
    arrived_keys = lax.ppermute(leave_keys, "attn", along)
    arrived_values = lax.ppermute(leave_values, "attn", along)
    state, normed, own, away = attended(
        page_table, lengths, chosen, mine, queries, residual, new_keys, new_values,
        key_pool, value_pool,
    )
    weights = gate_weights(normed, router_weight, chosen)
    swapped = exchanged(away, swap)
    blocks = [own] + [exchanged(own, mask) for mask in masks]
    blocks += [swapped] + [exchanged(swapped, mask) for mask in masks]
    mine_rows = jnp.concatenate(blocks)
    other_rows = exchanged(mine_rows, 1)
    kept, given = expert_parts(mine_rows, other_rows, w_gate, w_up, w_down)
    summed = (kept + exchanged(given, 1).astype(F32)).astype(BF16)
    count = len(masks) + 1
    parts = [summed[i * CAP:(i + 1) * CAP] for i in range(2 * count)]
    back = parts[count].astype(F32)
    for i, mask in enumerate(masks):
        back = back + exchanged(parts[count + 1 + i], mask).astype(F32)
    away_sums = exchanged(back.astype(BF16), swap)
    own_sums = parts[0].astype(F32)
    for i, mask in enumerate(masks):
        own_sums = own_sums + exchanged(parts[1 + i], mask).astype(F32)
    mixed = finished(chosen, mine, weights, state, own_sums, away_sums)
    return (mixed, arrived_keys, arrived_values)


def solution(mesh):
    placed = (
        P(("groups", "attn"), None),
        P(("groups", "attn"), None),
        P(("groups", "attn"), None),
        P(("groups", "attn"), None),
        P(("groups", "attn"), None, None),
        P(("groups", "attn"), None, None),
        P(("groups", "attn"), None),
        P(("groups", "attn")),
        P(("groups", "attn")),
        P(("groups", "attn"), None),
        P(),
        P(None, "attn"),
        P(None, "attn"),
        P("attn", None),
    )
    return jax.shard_map(
        body,
        mesh=mesh,
        in_specs=placed,
        out_specs=(
            P(("groups", "attn"), None),
            P(("groups", "attn"), None, None),
            P(("groups", "attn"), None, None),
        ),
        check_vma=False,
    )
```

time: 164 us -> 85.9 us (0.52)
  the two profiles are of different devices: /device:TPU:13 before, /device:TPU:0 now
where the time goes in v1:
time: 85.9 us; the launch traced here: 85.5 us
  starting transfers between devices  26.9 us (31%)
  Pallas kernels  24.6 us (29%)
  waiting for transfers between devices  21.5 us (25%)
  local copies, waits for them, and re-layouts  11.1 us (13%)
  between operations  0.86 us (1%)
    ppermute x16, starting transfers between devices, exchanged(): return lax.ppermute(array, 'attn', [(i, i ^ mask) for i in range(length)])  26 us
    ppermute x16, waiting for transfers between devices, exchanged(): return lax.ppermute(array, 'attn', [(i, i ^ mask) for i in range(length)])  21.5 us
    pallas_call x1, Pallas kernels, attended(): pl.pallas_call(attend_kernel, out_shape=(jax.ShapeDtypeStruct((rows, head...  18.3 us
    unnamed x47, local copies, waits for them, and re-layouts  11.1 us
    pallas_call x1, Pallas kernels, leaving(): pl.pallas_call(migrate_kernel, out_shape=(shape, shape), in_specs=[SMEM]...  2.44 us
    pallas_call x1, Pallas kernels, expert_parts(): pl.pallas_call(expert_kernel, grid=(total // block,), out_shape=(jax.Shap...  2.36 us
  transfers between devices with their start and end apart: 18, of which 9 were waited for; matrix products, arithmetic and copies ran while one was open for 1% of the time, Pallas kernels for 3%

profile of v1, /device:TPU:0, one launch (start us, length us, event | category | flops | bytes accessed | tf_op | source)
XLA Modules:
  0.0 85.5 jit_solution(15525041856453753903)
XLA Ops:
  0.7 0.8 copy.17.table
  1.5 0.8 copy.20.chosen
  2.2 1.9 %copy-done.1 = bf16[96,16,1024]{2,1,0:T(8,128)(2,1)S(1)} copy-done((bf16[96,16,1024]{2,1,0:T(8,128)(2,1)S(1)}, bf16[96,16,1024]{2,1,0:T(8,128)(2,1)}, u32[]{:S(2)}) %copy-start.1) | copy-done | bytes 3145752
  4.1 1.9 %copy-done.3 = bf16[96,16,1024]{2,1,0:T(8,128)(2,1)S(1)} copy-done((bf16[96,16,1024]{2,1,0:T(8,128)(2,1)S(1)}, bf16[96,16,1024]{2,1,0:T(8,128)(2,1)}, u32[]{:S(2)}) %copy-start.3) | copy-done | bytes 3145752
  6.0 0.9 %copy-done.8 = bf16[12,6144]{1,0:T(8,128)(2,1)S(1)} copy-done((bf16[12,6144]{1,0:T(8,128)(2,1)S(1)}, bf16[12,6144]{1,0:T(8,128)(2,1)}, u32[]{:S(2)}) %copy-start.8) | copy-done | bytes 147480
  6.9 0.9 %copy-done.9 = bf16[12,6144]{1,0:T(8,128)(2,1)S(1)} copy-done((bf16[12,6144]{1,0:T(8,128)(2,1)S(1)}, bf16[12,6144]{1,0:T(8,128)(2,1)}, u32[]{:S(2)}) %copy-start.9) | copy-done | bytes 147480
  7.9 0.8 copy-done.10
  8.6 0.8 copy-done.12
  9.4 0.7 copy-done.14
  10.0 18.3 %shard_map.157 = (f32[12,48,128]{2,1,0:T(8,128)S(1)}, bf16[12,48,128]{2,1,0:T(8,128)(2,1)S(1)}, bf16[5,48,128]{2,1,0:T(8,128)(2,1)S(1)}, bf16[5,48,128]{2,1,0:T(8,128)(2,1)S(1)}) custom-call(s32[12,8]{1,0:T(8,128)S(1)} %copy.17.table, s32[12]{0:T(128)S(1)} %copy-done.14, s32[12,2]{1,0:T(8,128)S(1)} %copy.20.chosen, s32[1]{0:T(128)} %bitcast.mine, ...), custom_call_target="tpu_custom_call" | custom-call | flops 400000000 | bytes 37748736 | tf_op jit(solution)/shard_map/pallas_call | solution.py:152
  28.4 4.0 %collective-permute-start.2 = (bf16[5,48,128]{2,1,0:T(8,128)(2,1)S(1)}, bf16[5,48,128]{2,1,0:T(8,128)(2,1)S(1)}, u32[]{:S(2)}, u32[]{:S(2)}) collective-permute-start(bf16[5,48,128]{2,1,0:T(8,128)(2,1)S(1)} %get-tuple-element.13), channel_id=1, source_target_pairs={{0,6},{1,7},{2,4},{3,5},{4,2},{5,3},{6,0},{7,1},{8,14},{9,15},{10,... | collective-permute-start | bytes 184328 | tf_op jit(solution)/shard_map/ppermute | solution.py:23
  33.0 2.9 %collective-permute-start.3 = (bf16[5,48,128]{2,1,0:T(8,128)(2,1)S(1)}, bf16[5,48,128]{2,1,0:T(8,128)(2,1)S(1)}, u32[]{:S(2)}, u32[]{:S(2)}) collective-permute-start(bf16[5,48,128]{2,1,0:T(8,128)(2,1)S(1)} %get-tuple-element.14), channel_id=1, source_target_pairs={{0,8},{1,9},{2,10},{3,11},{4,12},{5,13},{6,14},{7,15},{8,0},{9,1},... | collective-permute-start | bytes 184328 | tf_op jit(solution)/shard_map/ppermute | solution.py:23
  35.9 2.9 %collective-permute-done.3 = bf16[5,48,128]{2,1,0:T(8,128)(2,1)S(1)} collective-permute-done((bf16[5,48,128]{2,1,0:T(8,128)(2,1)S(1)}, bf16[5,48,128]{2,1,0:T(8,128)(2,1)S(1)}, u32[]{:S(2)}, u32[]{:S(2)}) %collective-permute-start.3) | collective-permute-done | bytes 61472 | tf_op jit(solution)/shard_map/ppermute | solution.py:23
  38.8 2.2 %collective-permute-start.6 = (bf16[5,48,128]{2,1,0:T(8,128)(2,1)S(1)}, bf16[5,48,128]{2,1,0:T(8,128)(2,1)S(1)}, u32[]{:S(2)}, u32[]{:S(2)}) collective-permute-start(bf16[5,48,128]{2,1,0:T(8,128)(2,1)S(1)} %collective-permute-done.3), channel_id=1, source_target_pairs={{0,6},{1,7},{2,4},{3,5},{4,2},{5,3},{6,0},{7,1},{8,14},{9,15},{10,... | collective-permute-start | bytes 184328 | tf_op jit(solution)/shard_map/ppermute | solution.py:23
  41.6 0.7 collective-permute-start.4
  42.4 3.4 %collective-permute-done.4 = bf16[5,48,128]{2,1,0:T(8,128)(2,1)S(1)} collective-permute-done((bf16[5,48,128]{2,1,0:T(8,128)(2,1)S(1)}, bf16[5,48,128]{2,1,0:T(8,128)(2,1)S(1)}, u32[]{:S(2)}, u32[]{:S(2)}) %collective-permute-start.4) | collective-permute-done | bytes 61472 | tf_op jit(solution)/shard_map/ppermute | solution.py:23
  46.0 1.9 %collective-permute-done.7.given_rows = bf16[40,48,128]{2,1,0:T(8,128)(2,1)S(1)} collective-permute-done((bf16[40,48,128]{2,1,0:T(8,128)(2,1)S(1)}, bf16[40,48,128]{2,1,0:T(8,128)(2,1)S(1)}, u32[]{:S(2)}, u32[]{:S(2)}) %collective-permute-start.7) | collective-permute-done | bytes 491552 | tf_op jit(solution)/shard_map/ppermute | solution.py:23
  47.9 2.4 %shard_map.158 = (f32[40,48,128]{2,1,0:T(8,128)S(1)}, bf16[40,48,128]{2,1,0:T(8,128)(2,1)S(1)}) custom-call(bf16[40,48,128]{2,1,0:T(8,128)(2,1)S(1)} %constant_dynamic-update-slice_fusion.kept_rows, bf16[40,48,128]{2,1,0:T(8,128)(2,1)S(1)} %collective-permute-done.7.given_rows, bf16[6144,128]{1,0:T(8,128)(2,1)S(1)} %copy-done.5, ...), custom_call_target="tpu_custom_call" | custom-call | flops 400000000 | bytes 8388608 | tf_op jit(solution)/shard_map/pallas_call | solution.py:211
  50.5 2.4 %shard_map.160 = (bf16[2,128,1024]{2,1,0:T(8,128)(2,1)S(1)}, bf16[2,128,1024]{2,1,0:T(8,128)(2,1)S(1)}) custom-call(s32[12,8]{1,0:T(8,128)S(1)} %copy.17.table, s32[12]{0:T(128)S(1)} %copy-done.15, s32[2]{0:T(128)S(1)} %copy-done.16, bf16[12,1024]{1,0:T(8,128)(2,1)S(1)} %copy-done.11, bf16[12,1024]{1,0:T(8,128)(2,1)S(1)} %copy-done.13, ...), custom_call_target="tpu_custom_call" | custom-call | bytes 4194304 | tf_op jit(solution)/shard_map/pallas_call | solution.py:60
  54.0 2.3 %collective-permute-start.12 = (bf16[5,48,128]{2,1,0:T(8,128)(2,1)S(1)}, bf16[5,48,128]{2,1,0:T(8,128)(2,1)S(1)}, u32[]{:S(2)}, u32[]{:S(2)}) collective-permute-start(bf16[5,48,128]{2,1,0:T(8,128)(2,1)S(1)} %get-tuple-element.23), channel_id=1, source_target_pairs={{0,2},{1,3},{2,0},{3,1},{4,6},{5,7},{6,4},{7,5},{8,10},{9,11},{10,... | collective-permute-start | bytes 184328 | tf_op jit(solution)/shard_map/ppermute | solution.py:23
  56.2 1.2 %collective-permute-start.14 = (bf16[5,48,128]{2,1,0:T(8,128)(2,1)S(1)}, bf16[5,48,128]{2,1,0:T(8,128)(2,1)S(1)}, u32[]{:S(2)}, u32[]{:S(2)}) collective-permute-start(bf16[5,48,128]{2,1,0:T(8,128)(2,1)S(1)} %get-tuple-element.24), channel_id=1, source_target_pairs={{0,6},{1,7},{2,4},{3,5},{4,2},{5,3},{6,0},{7,1},{8,14},{9,15},{10,... | collective-permute-start | bytes 184328 | tf_op jit(solution)/shard_map/ppermute | solution.py:23
  58.1 7.9 %collective-permute-done.12 = bf16[5,48,128]{2,1,0:T(8,128)(2,1)S(1)} collective-permute-done((bf16[5,48,128]{2,1,0:T(8,128)(2,1)S(1)}, bf16[5,48,128]{2,1,0:T(8,128)(2,1)S(1)}, u32[]{:S(2)}, u32[]{:S(2)}) %collective-permute-start.12) | collective-permute-done | bytes 61472 | tf_op jit(solution)/shard_map/ppermute | solution.py:23
  65.9 5.2 %collective-permute-start.11 = (bf16[5,48,128]{2,1,0:T(8,128)(2,1)S(1)}, bf16[5,48,128]{2,1,0:T(8,128)(2,1)S(1)}, u32[]{:S(2)}, u32[]{:S(2)}) collective-permute-start(bf16[5,48,128]{2,1,0:T(8,128)(2,1)S(1)} %get-tuple-element.26), channel_id=1, source_target_pairs={{0,6},{1,7},{2,4},{3,5},{4,2},{5,3},{6,0},{7,1},{8,14},{9,15},{10,... | collective-permute-start | bytes 184328 | tf_op jit(solution)/shard_map/ppermute | solution.py:23
  71.3 0.8 collective-permute-start.10
  72.2 1.5 %collective-permute-start.9 = (bf16[5,48,128]{2,1,0:T(8,128)(2,1)S(1)}, bf16[5,48,128]{2,1,0:T(8,128)(2,1)S(1)}, u32[]{:S(2)}, u32[]{:S(2)}) collective-permute-start(bf16[5,48,128]{2,1,0:T(8,128)(2,1)S(1)} %get-tuple-element.28), channel_id=1, source_target_pairs={{0,2},{1,3},{2,0},{3,1},{4,6},{5,7},{6,4},{7,5},{8,10},{9,11},{10,... | collective-permute-start | bytes 184328 | tf_op jit(solution)/shard_map/ppermute | solution.py:23
  73.9 1.9 %collective-permute-done.10 = bf16[5,48,128]{2,1,0:T(8,128)(2,1)S(1)} collective-permute-done((bf16[5,48,128]{2,1,0:T(8,128)(2,1)S(1)}, bf16[5,48,128]{2,1,0:T(8,128)(2,1)S(1)}, u32[]{:S(2)}, u32[]{:S(2)}) %collective-permute-start.10) | collective-permute-done | bytes 61472 | tf_op jit(solution)/shard_map/ppermute | solution.py:23
  75.7 0.7 collective-permute-done.9
  76.5 3.2 %collective-permute-start.15 = (bf16[5,48,128]{2,1,0:T(8,128)(2,1)S(1)}, bf16[5,48,128]{2,1,0:T(8,128)(2,1)S(1)}, u32[]{:S(2)}, u32[]{:S(2)}) collective-permute-start(bf16[5,48,128]{2,1,0:T(8,128)(2,1)S(1)} %get-tuple-element.21), channel_id=1, source_target_pairs={{0,8},{1,9},{2,10},{3,11},{4,12},{5,13},{6,14},{7,15},{8,0},{9,1},... | collective-permute-start | bytes 184328 | tf_op jit(solution)/shard_map/ppermute | solution.py:23
  79.7 2.7 %collective-permute-done.15.away = bf16[5,48,128]{2,1,0:T(8,128)(2,1)S(1)} collective-permute-done((bf16[5,48,128]{2,1,0:T(8,128)(2,1)S(1)}, bf16[5,48,128]{2,1,0:T(8,128)(2,1)S(1)}, u32[]{:S(2)}, u32[]{:S(2)}) %collective-permute-start.15) | collective-permute-done | bytes 61472 | tf_op jit(solution)/shard_map/ppermute | solution.py:23
  82.4 1.5 %shard_map.159 = bf16[12,6144]{1,0:T(8,128)(2,1)} custom-call(s32[12,2]{1,0:T(8,128)S(1)} %copy.20.chosen, s32[1]{0:T(128)} %bitcast.mine, f32[2,12]{1,0:T(2,128)S(1)} %fusion.2.weights, f32[12,48,128]{2,1,0:T(8,128)S(1)} %get-tuple-element.12.state, f32[5,48,128]{2,1,0:T(8,128)S(1)} %get-tuple-element.22.own, ...), custom_call_target="tpu_custom_call" | custom-call | tf_op jit(solution)/shard_map/pallas_call | solution.py:253
  83.9 0.8 copy.35
  84.7 0.8 copy.36
  (63 shorter events, 3.8 us)
Async XLA Ops:
  0.6 57.3 %copy-start = (bf16[6144,8]{0,1:T(8,128)(2,1)S(1)}, bf16[6144,8]{0,1:T(8,128)(2,1)}, u32[]{:S(2)}) copy-start(bf16[6144,8]{0,1:T(8,128)(2,1)} %param.24) | copy-start | bytes 294916
  2.2 1.9 %copy-start.1 = (bf16[96,16,1024]{2,1,0:T(8,128)(2,1)S(1)}, bf16[96,16,1024]{2,1,0:T(8,128)(2,1)}, u32[]{:S(2)}) copy-start(bf16[96,16,1024]{2,1,0:T(8,128)(2,1)} %key_pool.3) | copy-start | bytes 9437188
  4.1 1.9 %copy-start.3 = (bf16[96,16,1024]{2,1,0:T(8,128)(2,1)S(1)}, bf16[96,16,1024]{2,1,0:T(8,128)(2,1)}, u32[]{:S(2)}) copy-start(bf16[96,16,1024]{2,1,0:T(8,128)(2,1)} %value_pool.3) | copy-start | bytes 9437188
  6.0 0.9 %copy-start.8 = (bf16[12,6144]{1,0:T(8,128)(2,1)S(1)}, bf16[12,6144]{1,0:T(8,128)(2,1)}, u32[]{:S(2)}) copy-start(bf16[12,6144]{1,0:T(8,128)(2,1)} %queries.1) | copy-start | bytes 442372
  10.0 37.8 %copy-start.5 = (bf16[6144,128]{1,0:T(8,128)(2,1)S(1)}, bf16[6144,128]{1,0:T(8,128)(2,1)}, u32[]{:S(2)}) copy-start(bf16[6144,128]{1,0:T(8,128)(2,1)} %w_gate.1) | copy-start | bytes 4718596
  10.0 37.8 %copy-start.6 = (bf16[6144,128]{1,0:T(8,128)(2,1)S(1)}, bf16[6144,128]{1,0:T(8,128)(2,1)}, u32[]{:S(2)}) copy-start(bf16[6144,128]{1,0:T(8,128)(2,1)} %w_up.1) | copy-start | bytes 4718596
  10.0 37.8 %copy-start.7 = (bf16[128,6144]{1,0:T(8,128)(2,1)S(1)}, bf16[128,6144]{1,0:T(8,128)(2,1)}, u32[]{:S(2)}) copy-start(bf16[128,6144]{1,0:T(8,128)(2,1)} %w_down.1) | copy-start | bytes 4718596
  28.4 14.0 %collective-permute-start.2 = (bf16[5,48,128]{2,1,0:T(8,128)(2,1)S(1)}, bf16[5,48,128]{2,1,0:T(8,128)(2,1)S(1)}, u32[]{:S(2)}, u32[]{:S(2)}) collective-permute-start(bf16[5,48,128]{2,1,0:T(8,128)(2,1)S(1)} %get-tuple-element.13), channel_id=1, source_target_pairs={{0,6},{1,7},{2,4},{3,5},{4,2},{5,3},{6,0},{7,1},{8,14},{9,15},{10,... | collective-permute-start | bytes 184328 | tf_op jit(solution)/shard_map/ppermute | solution.py:23
  32.4 9.9 %collective-permute-start.1 = (bf16[5,48,128]{2,1,0:T(8,128)(2,1)S(1)}, bf16[5,48,128]{2,1,0:T(8,128)(2,1)S(1)}, u32[]{:S(2)}, u32[]{:S(2)}) collective-permute-start(bf16[5,48,128]{2,1,0:T(8,128)(2,1)S(1)} %get-tuple-element.13), channel_id=1, source_target_pairs={{0,4},{1,5},{2,6},{3,7},{4,0},{5,1},{6,2},{7,3},{8,12},{9,13},{10,... | collective-permute-start | bytes 184328 | tf_op jit(solution)/shard_map/ppermute | solution.py:23
  32.8 8.7 %collective-permute-start = (bf16[5,48,128]{2,1,0:T(8,128)(2,1)S(1)}, bf16[5,48,128]{2,1,0:T(8,128)(2,1)S(1)}, u32[]{:S(2)}, u32[]{:S(2)}) collective-permute-start(bf16[5,48,128]{2,1,0:T(8,128)(2,1)S(1)} %get-tuple-element.13), channel_id=1, source_target_pairs={{0,2},{1,3},{2,0},{3,1},{4,6},{5,7},{6,4},{7,5},{8,10},{9,11},{10,... | collective-permute-start | bytes 184328 | tf_op jit(solution)/shard_map/ppermute | solution.py:23
  33.0 5.8 %collective-permute-start.3 = (bf16[5,48,128]{2,1,0:T(8,128)(2,1)S(1)}, bf16[5,48,128]{2,1,0:T(8,128)(2,1)S(1)}, u32[]{:S(2)}, u32[]{:S(2)}) collective-permute-start(bf16[5,48,128]{2,1,0:T(8,128)(2,1)S(1)} %get-tuple-element.14), channel_id=1, source_target_pairs={{0,8},{1,9},{2,10},{3,11},{4,12},{5,13},{6,14},{7,15},{8,0},{9,1},... | collective-permute-start | bytes 184328 | tf_op jit(solution)/shard_map/ppermute | solution.py:23
  38.8 7.0 %collective-permute-start.6 = (bf16[5,48,128]{2,1,0:T(8,128)(2,1)S(1)}, bf16[5,48,128]{2,1,0:T(8,128)(2,1)S(1)}, u32[]{:S(2)}, u32[]{:S(2)}) collective-permute-start(bf16[5,48,128]{2,1,0:T(8,128)(2,1)S(1)} %collective-permute-done.3), channel_id=1, source_target_pairs={{0,6},{1,7},{2,4},{3,5},{4,2},{5,3},{6,0},{7,1},{8,14},{9,15},{10,... | collective-permute-start | bytes 184328 | tf_op jit(solution)/shard_map/ppermute | solution.py:23
  41.0 4.8 %collective-permute-start.5 = (bf16[5,48,128]{2,1,0:T(8,128)(2,1)S(1)}, bf16[5,48,128]{2,1,0:T(8,128)(2,1)S(1)}, u32[]{:S(2)}, u32[]{:S(2)}) collective-permute-start(bf16[5,48,128]{2,1,0:T(8,128)(2,1)S(1)} %collective-permute-done.3), channel_id=1, source_target_pairs={{0,4},{1,5},{2,6},{3,7},{4,0},{5,1},{6,2},{7,3},{8,12},{9,13},{10,... | collective-permute-start | bytes 184328 | tf_op jit(solution)/shard_map/ppermute | solution.py:23
  41.6 4.2 %collective-permute-start.4 = (bf16[5,48,128]{2,1,0:T(8,128)(2,1)S(1)}, bf16[5,48,128]{2,1,0:T(8,128)(2,1)S(1)}, u32[]{:S(2)}, u32[]{:S(2)}) collective-permute-start(bf16[5,48,128]{2,1,0:T(8,128)(2,1)S(1)} %collective-permute-done.3), channel_id=1, source_target_pairs={{0,2},{1,3},{2,0},{3,1},{4,6},{5,7},{6,4},{7,5},{8,10},{9,11},{10,... | collective-permute-start | bytes 184328 | tf_op jit(solution)/shard_map/ppermute | solution.py:23
  42.3 8.1 %copy-start.11 = (bf16[12,1024]{1,0:T(8,128)(2,1)S(1)}, bf16[12,1024]{1,0:T(8,128)(2,1)}, u32[]{:S(2)}) copy-start(bf16[12,1024]{1,0:T(8,128)(2,1)} %new_keys.3) | copy-start | bytes 73732
  42.3 8.1 %copy-start.13 = (bf16[12,1024]{1,0:T(8,128)(2,1)S(1)}, bf16[12,1024]{1,0:T(8,128)(2,1)}, u32[]{:S(2)}) copy-start(bf16[12,1024]{1,0:T(8,128)(2,1)} %new_values.3) | copy-start | bytes 73732
  42.4 8.1 %copy-start.4 = (bf16[96,16,1024]{2,1,0:T(8,128)(2,1)S(1)}, bf16[96,16,1024]{2,1,0:T(8,128)(2,1)}, u32[]{:S(2)}) copy-start(bf16[96,16,1024]{2,1,0:T(8,128)(2,1)} %value_pool.3) | copy-start | bytes 9437188
  45.9 4.6 %copy-start.2 = (bf16[96,16,1024]{2,1,0:T(8,128)(2,1)S(1)}, bf16[96,16,1024]{2,1,0:T(8,128)(2,1)}, u32[]{:S(2)}) copy-start(bf16[96,16,1024]{2,1,0:T(8,128)(2,1)} %key_pool.3) | copy-start | bytes 9437188
  45.9 4.6 %copy-start.15 = (s32[12]{0:T(128)S(1)}, s32[12]{0:T(128)}, u32[]{:S(2)}) copy-start(s32[12]{0:T(128)} %lengths.3) | copy-start | bytes 148
  45.9 4.6 %copy-start.16 = (s32[2]{0:T(128)S(1)}, s32[2]{0:T(128)}, u32[]{:S(2)}) copy-start(s32[2]{0:T(128)} %migrate.1) | copy-start | bytes 28
  45.9 1.9 %collective-permute-start.7 = (bf16[40,48,128]{2,1,0:T(8,128)(2,1)S(1)}, bf16[40,48,128]{2,1,0:T(8,128)(2,1)S(1)}, u32[]{:S(2)}, u32[]{:S(2)}) collective-permute-start(bf16[40,48,128]{2,1,0:T(8,128)(2,1)S(1)} %constant_dynamic-update-slice_fusion.kept_rows), channel_id=1, source_target_pairs={{0,1},{1,0},{2,3},{3,2},{4,5},{5,4},{6,7},{7,6},{8,9},{9,8},{10,11... | collective-permute-start | bytes 1474568 | tf_op jit(solution)/shard_map/ppermute | solution.py:23
  50.2 3.6 %copy-start.17 = (s32[12,2]{0,1:T(2,128)S(1)}, s32[12,2]{0,1:T(2,128)}, u32[]{:S(2)}) copy-start(s32[12,2]{0,1:T(2,128)} %param.23) | copy-start | bytes 292
  50.2 3.6 %collective-permute-start.8 = (bf16[40,48,128]{2,1,0:T(8,128)(2,1)S(1)}, bf16[40,48,128]{2,1,0:T(8,128)(2,1)S(1)}, u32[]{:S(2)}, u32[]{:S(2)}) collective-permute-start(bf16[40,48,128]{2,1,0:T(8,128)(2,1)S(1)} %get-tuple-element.16), channel_id=1, source_target_pairs={{0,1},{1,0},{2,3},{3,2},{4,5},{5,4},{6,7},{7,6},{8,9},{9,8},{10,11... | collective-permute-start | bytes 1474568 | tf_op jit(solution)/shard_map/ppermute | solution.py:23
  52.9 26.7 %collective-permute-start.16 = (bf16[2,128,1024]{2,1,0:T(8,128)(2,1)S(1)}, bf16[2,128,1024]{2,1,0:T(8,128)(2,1)S(1)}, u32[]{:S(2)}, u32[]{:S(2)}) collective-permute-start(bf16[2,128,1024]{2,1,0:T(8,128)(2,1)S(1)} %get-tuple-element.17), channel_id=1, source_target_pairs={{0,1},{1,2},{2,3},{3,4},{4,5},{5,6},{6,7},{7,8},{8,9},{9,10},{10,1... | collective-permute-start | bytes 1572872 | tf_op jit(solution)/shard_map/ppermute | solution.py:305
  53.3 26.3 %collective-permute-start.17 = (bf16[2,128,1024]{2,1,0:T(8,128)(2,1)S(1)}, bf16[2,128,1024]{2,1,0:T(8,128)(2,1)S(1)}, u32[]{:S(2)}, u32[]{:S(2)}) collective-permute-start(bf16[2,128,1024]{2,1,0:T(8,128)(2,1)S(1)} %get-tuple-element.18), channel_id=1, source_target_pairs={{0,1},{1,2},{2,3},{3,4},{4,5},{5,6},{6,7},{7,8},{8,9},{9,10},{10,1... | collective-permute-start | bytes 1572872 | tf_op jit(solution)/shard_map/ppermute | solution.py:306
  54.0 12.0 %collective-permute-start.12 = (bf16[5,48,128]{2,1,0:T(8,128)(2,1)S(1)}, bf16[5,48,128]{2,1,0:T(8,128)(2,1)S(1)}, u32[]{:S(2)}, u32[]{:S(2)}) collective-permute-start(bf16[5,48,128]{2,1,0:T(8,128)(2,1)S(1)} %get-tuple-element.23), channel_id=1, source_target_pairs={{0,2},{1,3},{2,0},{3,1},{4,6},{5,7},{6,4},{7,5},{8,10},{9,11},{10,... | collective-permute-start | bytes 184328 | tf_op jit(solution)/shard_map/ppermute | solution.py:23
  56.2 15.1 %collective-permute-start.14 = (bf16[5,48,128]{2,1,0:T(8,128)(2,1)S(1)}, bf16[5,48,128]{2,1,0:T(8,128)(2,1)S(1)}, u32[]{:S(2)}, u32[]{:S(2)}) collective-permute-start(bf16[5,48,128]{2,1,0:T(8,128)(2,1)S(1)} %get-tuple-element.24), channel_id=1, source_target_pairs={{0,6},{1,7},{2,4},{3,5},{4,2},{5,3},{6,0},{7,1},{8,14},{9,15},{10,... | collective-permute-start | bytes 184328 | tf_op jit(solution)/shard_map/ppermute | solution.py:23
  57.4 14.8 %collective-permute-start.13 = (bf16[5,48,128]{2,1,0:T(8,128)(2,1)S(1)}, bf16[5,48,128]{2,1,0:T(8,128)(2,1)S(1)}, u32[]{:S(2)}, u32[]{:S(2)}) collective-permute-start(bf16[5,48,128]{2,1,0:T(8,128)(2,1)S(1)} %get-tuple-element.25), channel_id=1, source_target_pairs={{0,4},{1,5},{2,6},{3,7},{4,0},{5,1},{6,2},{7,3},{8,12},{9,13},{10,... | collective-permute-start | bytes 184328 | tf_op jit(solution)/shard_map/ppermute | solution.py:23
  65.9 7.9 %collective-permute-start.11 = (bf16[5,48,128]{2,1,0:T(8,128)(2,1)S(1)}, bf16[5,48,128]{2,1,0:T(8,128)(2,1)S(1)}, u32[]{:S(2)}, u32[]{:S(2)}) collective-permute-start(bf16[5,48,128]{2,1,0:T(8,128)(2,1)S(1)} %get-tuple-element.26), channel_id=1, source_target_pairs={{0,6},{1,7},{2,4},{3,5},{4,2},{5,3},{6,0},{7,1},{8,14},{9,15},{10,... | collective-permute-start | bytes 184328 | tf_op jit(solution)/shard_map/ppermute | solution.py:23
  71.3 4.4 %collective-permute-start.10 = (bf16[5,48,128]{2,1,0:T(8,128)(2,1)S(1)}, bf16[5,48,128]{2,1,0:T(8,128)(2,1)S(1)}, u32[]{:S(2)}, u32[]{:S(2)}) collective-permute-start(bf16[5,48,128]{2,1,0:T(8,128)(2,1)S(1)} %get-tuple-element.27), channel_id=1, source_target_pairs={{0,4},{1,5},{2,6},{3,7},{4,0},{5,1},{6,2},{7,3},{8,12},{9,13},{10,... | collective-permute-start | bytes 184328 | tf_op jit(solution)/shard_map/ppermute | solution.py:23
  72.2 4.2 %collective-permute-start.9 = (bf16[5,48,128]{2,1,0:T(8,128)(2,1)S(1)}, bf16[5,48,128]{2,1,0:T(8,128)(2,1)S(1)}, u32[]{:S(2)}, u32[]{:S(2)}) collective-permute-start(bf16[5,48,128]{2,1,0:T(8,128)(2,1)S(1)} %get-tuple-element.28), channel_id=1, source_target_pairs={{0,2},{1,3},{2,0},{3,1},{4,6},{5,7},{6,4},{7,5},{8,10},{9,11},{10,... | collective-permute-start | bytes 184328 | tf_op jit(solution)/shard_map/ppermute | solution.py:23
  76.5 5.9 %collective-permute-start.15 = (bf16[5,48,128]{2,1,0:T(8,128)(2,1)S(1)}, bf16[5,48,128]{2,1,0:T(8,128)(2,1)S(1)}, u32[]{:S(2)}, u32[]{:S(2)}) collective-permute-start(bf16[5,48,128]{2,1,0:T(8,128)(2,1)S(1)} %get-tuple-element.21), channel_id=1, source_target_pairs={{0,8},{1,9},{2,10},{3,11},{4,12},{5,13},{6,14},{7,15},{8,0},{9,1},... | collective-permute-start | bytes 184328 | tf_op jit(solution)/shard_map/ppermute | solution.py:23
  (4 other events, 3.1 us)

commit v2 on v1

v2 whole, which is shorter than its diff:
```python
import math

import jax
import jax.numpy as jnp
from jax import lax
from jax.experimental import pallas as pl
from jax.experimental.pallas import tpu as pltpu
from jax.sharding import PartitionSpec as P

HEAD_DIM = 128
CAP = 5
EXP_ON = 2
F32 = jnp.float32
BF16 = jnp.bfloat16

SMEM = pl.BlockSpec(memory_space=pltpu.SMEM)
VMEM = pl.BlockSpec(memory_space=pltpu.VMEM)
ANY = pl.BlockSpec(memory_space=pl.ANY)
HBM = pl.BlockSpec(memory_space=pltpu.HBM)


def in_hbm(array):
    return pltpu.with_memory_space_constraint(array, pltpu.HBM)


def exchanged(array, mask):
    length = lax.axis_size("attn")
    return lax.ppermute(array, "attn", [(i, i ^ mask) for i in range(length)])


def stage_kernel(table_at, lengths_at, migrate_at, chosen_at, mine, queries_at, residual_at,
                 new_keys_at, new_values_at, key_pool_at, value_pool_at,
                 plan, key_pool, value_pool, heads_q, heads_r, moved_keys, moved_values,
                 table, lengths, migrate, chosen, queries, residual, new_keys, new_values,
                 fresh, small_sems, row_sems, pool_sems):
    pages, rows = table.shape
    page = key_pool.shape[1]
    moves = moved_keys.shape[0]
    heads = heads_q.shape[0] // rows
    small = [
        pltpu.make_async_copy(source, target, small_sems.at[i])
        for i, (source, target) in enumerate(
            ((table_at, table), (lengths_at, lengths), (migrate_at, migrate), (chosen_at, chosen))
        )
    ]
    wide = [
        pltpu.make_async_copy(source, target, row_sems.at[i])
        for i, (source, target) in enumerate(
            ((queries_at, queries), (residual_at, residual),
             (new_keys_at, new_keys), (new_values_at, new_values))
        )
    ]
    pool = []
    cut = key_pool.shape[0] // POOL_CUTS
    for c in range(POOL_CUTS):
        part = pl.ds(c * cut, cut)
        for side, (source, target) in enumerate(
            ((key_pool_at, key_pool), (value_pool_at, value_pool))
        ):
            pool.append(
                pltpu.make_async_copy(source.at[part], target.at[part], pool_sems.at[side, c])
            )
    for copy in wide[:2] + small + wide[2:] + pool:
        copy.start()
    for copy, target, source in zip(wide[:2], (heads_q, heads_r), (queries, residual)):
        copy.wait()
        for h in range(heads):
            target[pl.ds(h, rows, stride=heads), :] = source[
                :, h * HEAD_DIM:(h + 1) * HEAD_DIM
            ].astype(F32)
    for copy in small:
        copy.wait()
    expert = mine[0]
    other = 1 - expert
    taken_own, taken_away = jnp.int32(0), jnp.int32(0)
    own_slots, away_slots = [], []
    for r in range(rows):
        for p in range(pages):
            plan[p, r] = table[p, r]
        plan[pages, r] = lengths[r]
        first, second = chosen[0, r], chosen[1, r]
        own = ((first == expert) | (second == expert)).astype(jnp.int32)
        away = ((first == other) | (second == other)).astype(jnp.int32)
        own_slots.append(jnp.where(own == 1, taken_own, -1))
        away_slots.append(jnp.where(away == 1, taken_away, -1))
        plan[pages + 1, r] = own_slots[r]
        plan[pages + 2, r] = away_slots[r]
        taken_own = taken_own + own
        taken_away = taken_away + away
    behind = taken_away
    for r in range(rows):
        is_away = away_slots[r] >= 0
        plan[pages + 3, jnp.where(is_away, away_slots[r], behind)] = jnp.int32(r)
        behind = behind + jnp.where(is_away, 0, 1)
    plan[pages + 4, 0] = taken_away
    for copy, side in zip(wide[2:], (0, 1)):
        copy.wait()
        fresh[side] = (new_keys, new_values)[side][...].astype(F32)
    for copy in pool:
        copy.wait()
    inside = lax.broadcasted_iota(jnp.int32, (page, key_pool.shape[2]), 0)
    for r in range(rows):
        length = lengths[r]
        last = length // page
        number = table[last, r]
        here = inside == length - last * page
        for side, buffer in enumerate((key_pool, value_pool)):
            block = buffer[number].astype(F32)
            buffer[number] = jnp.where(here, fresh[side, r:r + 1, :], block).astype(BF16)
    for m in range(moves):
        request = migrate[m]
        length = lengths[request]
        for p in range(pages):
            number = table[p, request]
            kept = inside + p * page <= length
            for buffer, out in ((key_pool, moved_keys), (value_pool, moved_values)):
                block = jnp.where(kept, buffer[number].astype(F32), 0.0)
                out[m, p * page:(p + 1) * page, :] = block.astype(BF16)


POOL_CUTS = 3


def staged(page_table, lengths, migrate, chosen, mine, queries, residual, new_keys, new_values,
           key_pool, value_pool):
    rows, width = queries.shape
    heads = width // HEAD_DIM
    kv_width = new_keys.shape[1]
    moves = migrate.shape[0]
    pages = page_table.shape[1]
    moved = jax.ShapeDtypeStruct((moves, pages * key_pool.shape[1], kv_width), BF16)
    split = jax.ShapeDtypeStruct((rows * heads, HEAD_DIM), F32)
    return pl.pallas_call(
        stage_kernel,
        out_shape=(
            jax.ShapeDtypeStruct((pages + 5, rows), jnp.int32),
            jax.ShapeDtypeStruct(key_pool.shape, BF16),
            jax.ShapeDtypeStruct(value_pool.shape, BF16),
            split, split, moved, moved,
        ),
        in_specs=[HBM] * 4 + [SMEM] + [HBM] * 6,
        out_specs=(SMEM,) + (VMEM,) * 6,
        scratch_shapes=[
            pltpu.SMEM((pages, rows), jnp.int32),
            pltpu.SMEM(lengths.shape, jnp.int32),
            pltpu.SMEM(migrate.shape, jnp.int32),
            pltpu.SMEM((2, rows), jnp.int32),
            pltpu.VMEM(queries.shape, BF16),
            pltpu.VMEM(queries.shape, BF16),
            pltpu.VMEM(new_keys.shape, BF16),
            pltpu.VMEM(new_keys.shape, BF16),
            pltpu.VMEM((2, rows, kv_width), F32),
            pltpu.SemaphoreType.DMA((4,)),
            pltpu.SemaphoreType.DMA((4,)),
            pltpu.SemaphoreType.DMA((2, POOL_CUTS)),
        ],
        compiler_params=pltpu.CompilerParams(vmem_limit_bytes=16 << 20),
        cost_estimate=pl.CostEstimate(flops=0, bytes_accessed=8 << 20, transcendentals=0),
    )(*[in_hbm(a) for a in (page_table.T, lengths, migrate, chosen.T)], mine,
      *[in_hbm(a) for a in (queries, residual, new_keys, new_values, key_pool, value_pool)])


def attend_pair(plan, pair, key_pool, value_pool, heads_q, heads_r, state_out, normed_out):
    page = key_pool.shape[1]
    kv_heads = key_pool.shape[2] // HEAD_DIM
    rows, heads, _ = state_out.shape
    group = heads // kv_heads
    pages = plan.shape[0] - 5
    positions = pages * page
    head_of = lax.broadcasted_iota(jnp.int32, (heads, HEAD_DIM), 0)
    at_of = lax.broadcasted_iota(jnp.int32, (heads, positions), 1)
    in_group = [(head_of >= g * group) & (head_of < (g + 1) * group) for g in range(kv_heads)]
    both = [plan[pages + 3, 2 * pair + i] for i in range(2)]
    starts = [pl.multiple_of(r * heads, 8) for r in both]
    numbers = [[plan[p, r] for p in range(pages)] for r in both]
    queries = [heads_q[pl.ds(start, heads), :] for start in starts]
    spread = [
        jnp.concatenate(
            [jnp.where(inside, query, 0.0).astype(BF16) for inside in in_group], axis=1
        )
        for query in queries
    ]
    scores = [
        lax.dot_general(
            rows_q, jnp.concatenate([key_pool[n] for n in number], axis=0),
            (((1,), (1,)), ((), ())), preferred_element_type=F32,
        ) * (1.0 / math.sqrt(HEAD_DIM))
        for rows_q, number in zip(spread, numbers)
    ]
    visible = [at_of <= plan[pages, r] for r in both]
    scores = [jnp.where(seen, score, -jnp.inf) for seen, score in zip(visible, scores)]
    highest = [jnp.max(score, axis=1, keepdims=True) for score in scores]
    exponent = [
        jnp.where(seen, jnp.exp(score - high), 0.0)
        for seen, score, high in zip(visible, scores, highest)
    ]
    sums = [jnp.sum(e, axis=1, keepdims=True) for e in exponent]
    probs = [(e / s).astype(BF16) for e, s in zip(exponent, sums)]
    mixed = [
        jnp.dot(
            prob, jnp.concatenate([value_pool[n] for n in number], axis=0),
            preferred_element_type=F32,
        )
        for prob, number in zip(probs, numbers)
    ]
    states = []
    for start, mix in zip(starts, mixed):
        attended = mix[:, :HEAD_DIM]
        for g in range(1, kv_heads):
            attended = jnp.where(in_group[g], mix[:, g * HEAD_DIM:(g + 1) * HEAD_DIM], attended)
        states.append(heads_r[pl.ds(start, heads), :] + attended.astype(BF16).astype(F32))
    squares = [
        jnp.sum(jnp.sum(state * state, axis=1, keepdims=True), axis=0, keepdims=True)
        for state in states
    ]
    normed = [
        (state * lax.rsqrt(square / (heads * HEAD_DIM) + 1e-05)).astype(BF16)
        for state, square in zip(states, squares)
    ]
    for r, state, rows_n in zip(both, states, normed):
        state_out[r] = state
        normed_out[r] = rows_n
    return both, normed


def away_kernel(plan, key_pool, value_pool, heads_q, heads_r,
                state_out, normed_out, own_out, away_out):
    pages = plan.shape[0] - 5
    own_out[...] = jnp.zeros_like(own_out)
    away_out[...] = jnp.zeros_like(away_out)

    def step(pair, carry):
        both, normed = attend_pair(
            plan, pair, key_pool, value_pool, heads_q, heads_r, state_out, normed_out
        )
        for r, rows_n in zip(both, normed):
            for row, out in ((pages + 1, own_out), (pages + 2, away_out)):
                slot = plan[row, r]

                @pl.when(slot >= 0)
                def _():
                    out[jnp.clip(slot, 0, CAP - 1)] = rows_n

        return carry

    lax.fori_loop(0, (plan[pages + 4, 0] + 1) // 2, step, 0)


def rest_kernel(plan, key_pool, value_pool, heads_q, heads_r, state_in, normed_in, own_in,
                state_out, normed_out, own_out):
    pages = plan.shape[0] - 5
    rows = state_out.shape[0]
    state_out[...] = state_in[...]
    normed_out[...] = normed_in[...]
    own_out[...] = own_in[...]

    def step(pair, carry):
        both, normed = attend_pair(
            plan, pair, key_pool, value_pool, heads_q, heads_r, state_out, normed_out
        )
        for r, rows_n in zip(both, normed):
            slot = plan[pages + 1, r]

            @pl.when(slot >= 0)
            def _():
                own_out[jnp.clip(slot, 0, CAP - 1)] = rows_n

        return carry

    lax.fori_loop((plan[pages + 4, 0] + 1) // 2, rows // 2, step, 0)


def attend_shapes(rows, heads):
    packed = jax.ShapeDtypeStruct((CAP, heads, HEAD_DIM), BF16)
    return (
        jax.ShapeDtypeStruct((rows, heads, HEAD_DIM), F32),
        jax.ShapeDtypeStruct((rows, heads, HEAD_DIM), BF16),
        packed,
        packed,
    )


def attended_away(plan, key_pool, value_pool, heads_q, heads_r):
    rows = plan.shape[1]
    heads = heads_q.shape[0] // rows
    return pl.pallas_call(
        away_kernel,
        out_shape=attend_shapes(rows, heads),
        in_specs=[SMEM] + [VMEM] * 4,
        out_specs=(VMEM,) * 4,
        compiler_params=pltpu.CompilerParams(vmem_limit_bytes=8 << 20),
        cost_estimate=pl.CostEstimate(
            flops=1 << 27, bytes_accessed=8 << 20, transcendentals=1 << 15
        ),
    )(plan, key_pool, value_pool, heads_q, heads_r)


def attended_rest(plan, key_pool, value_pool, heads_q, heads_r, state, normed, own):
    rows, heads, _ = state.shape
    return pl.pallas_call(
        rest_kernel,
        out_shape=attend_shapes(rows, heads)[:3],
        in_specs=[SMEM] + [VMEM] * 7,
        out_specs=(VMEM,) * 3,
        compiler_params=pltpu.CompilerParams(vmem_limit_bytes=8 << 20),
        cost_estimate=pl.CostEstimate(
            flops=1 << 28, bytes_accessed=24 << 20, transcendentals=1 << 16
        ),
    )(plan, key_pool, value_pool, heads_q, heads_r, state, normed, own)


def expert_kernel(kept_rows, given_rows, w_gate, w_up, w_down, arrived_keys, arrived_values,
                  kept, given, moved_keys, moved_values, split, flat, back, sems):
    copies = [
        pltpu.make_async_copy(arrived_keys, moved_keys, sems.at[0]),
        pltpu.make_async_copy(arrived_values, moved_values, sems.at[1]),
    ]

    @pl.when(pl.program_id(0) == 0)
    def _():
        for copy in copies:
            copy.start()

    block, heads, _ = kept_rows.shape
    half = block * heads
    split[:half] = kept_rows[...].astype(F32).reshape(half, HEAD_DIM)
    split[half:] = given_rows[...].astype(F32).reshape(half, HEAD_DIM)
    for h in range(heads):
        cols = slice(h * HEAD_DIM, (h + 1) * HEAD_DIM)
        flat[:, cols] = split[pl.ds(h, 2 * block, stride=heads), :].astype(BF16)
    gate = jnp.dot(flat[...], w_gate[...], preferred_element_type=F32)
    up = jnp.dot(flat[...], w_up[...], preferred_element_type=F32)
    hidden = (gate / (1.0 + jnp.exp(-gate)) * up).astype(BF16)
    wide = 4
    for first in range(0, heads, wide):
        cols = slice(first * HEAD_DIM, (first + wide) * HEAD_DIM)
        part = jnp.dot(hidden, w_down[:, cols], preferred_element_type=F32)
        for h in range(wide):
            back[pl.ds(first + h, 2 * block, stride=heads), :] = part[
                :, h * HEAD_DIM:(h + 1) * HEAD_DIM
            ]
    kept[...] = back[:half].reshape(block, heads, HEAD_DIM)
    given[...] = back[half:].reshape(block, heads, HEAD_DIM).astype(BF16)

    @pl.when(pl.program_id(0) == pl.num_programs(0) - 1)
    def _():
        for copy in copies:
            copy.wait()


def expert_parts(kept_rows, given_rows, w_gate, w_up, w_down, arrived_keys, arrived_values):
    total, heads, _ = kept_rows.shape
    block = 8 * CAP
    if total % block:
        block = CAP
    rows = pl.BlockSpec((block, heads, HEAD_DIM), lambda i: (i, 0, 0))

    def fixed(array):
        return pl.BlockSpec(array.shape, lambda i: (0, 0))

    return pl.pallas_call(
        expert_kernel,
        grid=(total // block,),
        out_shape=(
            jax.ShapeDtypeStruct(kept_rows.shape, F32),
            jax.ShapeDtypeStruct(kept_rows.shape, BF16),
            jax.ShapeDtypeStruct(arrived_keys.shape, BF16),
            jax.ShapeDtypeStruct(arrived_values.shape, BF16),
        ),
        in_specs=[rows, rows, fixed(w_gate), fixed(w_up), fixed(w_down), ANY, ANY],
        out_specs=(rows, rows, HBM, HBM),
        scratch_shapes=[
            pltpu.VMEM((2 * block * heads, HEAD_DIM), F32),
            pltpu.VMEM((2 * block, heads * HEAD_DIM), BF16),
            pltpu.VMEM((2 * block * heads, HEAD_DIM), F32),
            pltpu.SemaphoreType.DMA((2,)),
        ],
        compiler_params=pltpu.CompilerParams(vmem_limit_bytes=32 << 20),
        cost_estimate=pl.CostEstimate(
            flops=400_000_000, bytes_accessed=8 << 20, transcendentals=10240
        ),
    )(kept_rows, given_rows, w_gate, w_up, w_down, arrived_keys, arrived_values)


def finish_kernel(plan, mine, weights, state, own, away, mixed, rows_split):
    rows, heads, _ = state.shape
    pages = plan.shape[0] - 5
    expert = mine[0]
    for r in range(rows):
        total = state[r]
        for row, sums, number in ((pages + 1, own, expert), (pages + 2, away, 1 - expert)):
            slot = plan[row, r]
            factor = jnp.where(slot >= 0, weights[number, r], 0.0)
            total = total + factor * sums[jnp.clip(slot, 0, CAP - 1)].astype(F32)
        rows_split[r * heads:(r + 1) * heads, :] = total
    for h in range(heads):
        mixed[:, h * HEAD_DIM:(h + 1) * HEAD_DIM] = rows_split[
            pl.ds(h, rows, stride=heads), :
        ].astype(BF16)


def finished(plan, mine, weights, state, own, away):
    rows, heads, _ = state.shape
    return pl.pallas_call(
        finish_kernel,
        out_shape=jax.ShapeDtypeStruct((rows, heads * HEAD_DIM), BF16),
        in_specs=[SMEM] * 3 + [VMEM] * 3,
        out_specs=VMEM,
        scratch_shapes=[pltpu.VMEM((rows * heads, HEAD_DIM), F32)],
        compiler_params=pltpu.CompilerParams(vmem_limit_bytes=8 << 20),
    )(plan, mine, weights, state, own, away)


def gate_weights(normed, router_weight, chosen):
    rows, heads, _ = normed.shape
    router = router_weight.reshape(heads, HEAD_DIM, -1)
    logits = jnp.einsum("rhd,hde->re", normed, router, preferred_element_type=F32)
    numbers = jnp.arange(logits.shape[1], dtype=jnp.int32)[None, :]
    first = chosen[:, 0:1]
    second = chosen[:, 1:2]
    first_logit = jnp.sum(jnp.where(numbers == first, logits, 0.0), axis=1, keepdims=True)
    second_logit = jnp.sum(jnp.where(numbers == second, logits, 0.0), axis=1, keepdims=True)
    first_weight = 1.0 / (1.0 + jnp.exp(second_logit - first_logit))
    second_weight = 1.0 / (1.0 + jnp.exp(first_logit - second_logit))
    experts = jnp.arange(EXP_ON, dtype=jnp.int32)[None, :]
    weights = jnp.where(first == experts, first_weight, 0.0) + jnp.where(
        second == experts, second_weight, 0.0
    )
    return weights.T


def body(
    queries,
    residual,
    new_keys,
    new_values,
    key_pool,
    value_pool,
    page_table,
    lengths,
    migrate,
    chosen,
    router_weight,
    w_gate,
    w_up,
    w_down,
):
    length = lax.axis_size("attn")
    swap = length // 2
    masks = list(range(2, swap, 2))
    mine = (lax.axis_index("attn") // (length // EXP_ON)).astype(jnp.int32).reshape(1)
    along = [(i, (i + 1) % length) for i in range(length)]
    plan, keys, values, heads_q, heads_r, leave_keys, leave_values = staged(
        page_table, lengths, migrate, chosen, mine, queries, residual, new_keys, new_values,
        key_pool, value_pool,
    )
    arrived_keys = lax.ppermute(leave_keys, "attn", along)
    arrived_values = lax.ppermute(leave_values, "attn", along)
    state, normed, own, away = attended_away(plan, keys, values, heads_q, heads_r)
    swapped = exchanged(away, swap)
    state, normed, own = attended_rest(
        plan, keys, values, heads_q, heads_r, state, normed, own
    )
    weights = gate_weights(normed, router_weight, chosen)
    rows_here = jnp.concatenate([own, swapped])
    mine_rows = jnp.concatenate([rows_here] + [exchanged(rows_here, mask) for mask in masks])
    other_rows = exchanged(mine_rows, 1)
    kept, given, moved_keys, moved_values = expert_parts(
        mine_rows, other_rows, w_gate, w_up, w_down, arrived_keys, arrived_values
    )
    summed = (kept + exchanged(given, 1).astype(F32)).astype(BF16)
    sent = 2 * CAP
    back = summed[:sent].astype(F32)
    for i, mask in enumerate(masks):
        at = (i + 1) * sent
        back = back + exchanged(summed[at:at + sent], mask).astype(F32)
    own_sums = back[:CAP]
    away_sums = exchanged(back[CAP:].astype(BF16), swap)
    mixed = finished(plan, mine, weights, state, own_sums, away_sums)
    return (mixed, moved_keys, moved_values)


def solution(mesh):
    placed = (
        P(("groups", "attn"), None),
        P(("groups", "attn"), None),
        P(("groups", "attn"), None),
        P(("groups", "attn"), None),
        P(("groups", "attn"), None, None),
        P(("groups", "attn"), None, None),
        P(("groups", "attn"), None),
        P(("groups", "attn")),
        P(("groups", "attn")),
        P(("groups", "attn"), None),
        P(),
        P(None, "attn"),
        P(None, "attn"),
        P("attn", None),
    )
    return jax.shard_map(
        body,
        mesh=mesh,
        in_specs=placed,
        out_specs=(
            P(("groups", "attn"), None),
            P(("groups", "attn"), None, None),
            P(("groups", "attn"), None, None),
        ),
        check_vma=False,
    )
```

time: 85.9 us -> 58.9 us (0.69)
  local copies, waits for them, and re-layouts: 11.1 us -> 0.18 us
  starting transfers between devices: 26.9 us -> 16.2 us
  Pallas kernels: 24.6 us -> 14 us
  waiting for transfers between devices: 21.5 us -> 27.2 us
    unnamed x47 -> x13, local copies, waits for them, and re-layouts: 11.1 us -> 0.08 us
    pallas_call x2 -> x3, Pallas kernels: 20.7 us -> 10.1 us  [the longest x1 4.09 us: staged(): pl.pallas_call(stage_kernel, out_shape=(jax.ShapeDtypeStruct((pages + 5,...]
    ppermute x16 -> x10, starting transfers between devices: 26 us -> 15.6 us  [exchanged(): return lax.ppermute(array, 'attn', [(i, i ^ mask) for i in range(length)])]
    ppermute x16 -> x10, waiting for transfers between devices: 21.5 us -> 27.2 us  [exchanged(): return lax.ppermute(array, 'attn', [(i, i ^ mask) for i in range(length)])]
  transfers between devices with their start and end apart: 18 -> 12, of which waited for: 9 -> 6; matrix products, arithmetic and copies ran while one was open for 1% -> 0% of each run, Pallas kernels for 3% -> 6%
where the time goes in v2:
time: 58.9 us; the launch traced here: 58.8 us
  waiting for transfers between devices  27.2 us (46%)
  starting transfers between devices  16.2 us (28%)
  Pallas kernels  14 us (24%)
  between operations  0.81 us (1%)
    ppermute x10, waiting for transfers between devices, exchanged(): return lax.ppermute(array, 'attn', [(i, i ^ mask) for i in range(length)])  27.2 us
    ppermute x10, starting transfers between devices, exchanged(): return lax.ppermute(array, 'attn', [(i, i ^ mask) for i in range(length)])  15.6 us
    pallas_call x1, Pallas kernels, staged(): pl.pallas_call(stage_kernel, out_shape=(jax.ShapeDtypeStruct((pages + 5,...  4.09 us
    pallas_call x1, Pallas kernels, attended_rest(): pl.pallas_call(rest_kernel, out_shape=attend_shapes(rows, heads)[:3], in_...  3.76 us
    pallas_call x1, Pallas kernels, expert_parts(): pl.pallas_call(expert_kernel, grid=(total // block,), out_shape=(jax.Shap...  2.38 us
    pallas_call x1, Pallas kernels, attended_away(): pl.pallas_call(away_kernel, out_shape=attend_shapes(rows, heads), in_spec...  2.27 us
    pallas_call x1, Pallas kernels, finished(): pl.pallas_call(finish_kernel, out_shape=jax.ShapeDtypeStruct((rows, heads...  1.53 us
  transfers between devices with their start and end apart: 12, of which 6 were waited for; matrix products, arithmetic and copies ran while one was open for 0% of the time, Pallas kernels for 6%

profile of v2, /device:TPU:0, one launch (start us, length us, event | category | flops | bytes accessed | tf_op | source)
XLA Modules:
  0.0 58.8 jit_solution(1631534876827404399)
XLA Ops:
  0.6 0.0 copy-start
  0.7 4.1 %shard_map.157 = (s32[13,12]{1,0:T(8,128)S(1)}, bf16[96,16,1024]{2,1,0:T(8,128)(2,1)S(1)}, bf16[96,16,1024]{2,1,0:T(8,128)(2,1)S(1)}, f32[576,128]{1,0:T(8,128)S...) custom-call(s32[8,12]{1,0:T(8,128)} %bitcast.15, s32[12]{0:T(128)} %lengths_at.1, ...), custom_call_target="tpu_custom_call" | custom-call | bytes 8388608 | tf_op jit(solution)/shard_map/pallas_call | solution.py:133
  4.8 2.3 %shard_map.158 = (f32[12,48,128]{2,1,0:T(8,128)S(1)}, bf16[12,48,128]{2,1,0:T(8,128)(2,1)S(1)}, bf16[5,48,128]{2,1,0:T(8,128)(2,1)S(1)}, bf16[5,48,128]{2,1,0:T(8,128)(2,1)S(1)}) custom-call(s32[13,12]{1,0:T(8,128)S(1)} %get-tuple-element.21.plan, bf16[96,16,1024]{2,1,0:T(8,128)(2,1)S(1)} %get-tuple-element.22.key_pool, ...), custom_call_target="tpu_custom_call" | custom-call | flops 134217728 | bytes 8388608 | tf_op jit(solution)/shard_map/pallas_call | solution.py:286
  7.0 3.3 %collective-permute-start = (bf16[5,48,128]{2,1,0:T(8,128)(2,1)S(1)}, bf16[5,48,128]{2,1,0:T(8,128)(2,1)S(1)}, u32[]{:S(2)}, u32[]{:S(2)}) collective-permute-start(bf16[5,48,128]{2,1,0:T(8,128)(2,1)S(1)} %get-tuple-element.32), channel_id=1, source_target_pairs={{0,8},{1,9},{2,10},{3,11},{4,12},{5,13},{6,14},{7,15},{8,0},{9,1},... | collective-permute-start | bytes 184328 | tf_op jit(solution)/shard_map/ppermute | solution.py:28
  10.4 3.8 %shard_map.159 = (f32[12,48,128]{2,1,0:T(8,128)S(1)}, bf16[12,48,128]{2,1,0:T(8,128)(2,1)S(1)}, bf16[5,48,128]{2,1,0:T(8,128)(2,1)S(1)}) custom-call(s32[13,12]{1,0:T(8,128)S(1)} %get-tuple-element.21.plan, bf16[96,16,1024]{2,1,0:T(8,128)(2,1)S(1)} %get-tuple-element.22.key_pool, bf16[96,16,1024]{2,1,0:T(8,128)(2,1)S(1)} %get-tuple-element.23.value_pool, ...), custom_call_target="tpu_custom_call" | custom-call | flops 268435456 | bytes 25165824 | tf_op jit(solution)/shard_map/pallas_call | solution.py:300
  14.2 0.0 collective-permute-done
  14.2 2.7 %collective-permute-start.1 = (bf16[10,48,128]{2,1,0:T(8,128)(2,1)S(1)}, bf16[10,48,128]{2,1,0:T(8,128)(2,1)S(1)}, u32[]{:S(2)}, u32[]{:S(2)}) collective-permute-start(bf16[10,48,128]{2,1,0:T(8,128)(2,1)S(1)} %get-tuple-element.44), channel_id=1, source_target_pairs={{0,2},{1,3},{2,0},{3,1},{4,6},{5,7},{6,4},{7,5},{8,10},{9,11},{10,... | collective-permute-start | bytes 368648 | tf_op jit(solution)/shard_map/ppermute | solution.py:28
  16.9 1.2 %collective-permute-start.2 = (bf16[10,48,128]{2,1,0:T(8,128)(2,1)S(1)}, bf16[10,48,128]{2,1,0:T(8,128)(2,1)S(1)}, u32[]{:S(2)}, u32[]{:S(2)}) collective-permute-start(bf16[10,48,128]{2,1,0:T(8,128)(2,1)S(1)} %get-tuple-element.44), channel_id=1, source_target_pairs={{0,4},{1,5},{2,6},{3,7},{4,0},{5,1},{6,2},{7,3},{8,12},{9,13},{10,... | collective-permute-start | bytes 368648 | tf_op jit(solution)/shard_map/ppermute | solution.py:28
  18.1 0.0 collective-permute-start.5
  18.1 0.6 %collective-permute-start.6 = (bf16[2,128,1024]{2,1,0:T(8,128)(2,1)S(1)}, bf16[2,128,1024]{2,1,0:T(8,128)(2,1)S(1)}, u32[]{:S(2)}, u32[]{:S(2)}) collective-permute-start(bf16[2,128,1024]{2,1,0:T(8,128)(2,1)S(1)} %get-tuple-element.34), channel_id=1, source_target_pairs={{0,1},{1,2},{2,3},{3,4},{4,5},{5,6},{6,7},{7,8},{8,9},{9,10},{10,1... | collective-permute-start | bytes 1572872 | tf_op jit(solution)/shard_map/ppermute | solution.py:458
  18.8 3.0 %collective-permute-start.3 = (bf16[10,48,128]{2,1,0:T(8,128)(2,1)S(1)}, bf16[10,48,128]{2,1,0:T(8,128)(2,1)S(1)}, u32[]{:S(2)}, u32[]{:S(2)}) collective-permute-start(bf16[10,48,128]{2,1,0:T(8,128)(2,1)S(1)} %get-tuple-element.44), channel_id=1, source_target_pairs={{0,6},{1,7},{2,4},{3,5},{4,2},{5,3},{6,0},{7,1},{8,14},{9,15},{10,... | collective-permute-start | bytes 368648 | tf_op jit(solution)/shard_map/ppermute | solution.py:28
  21.8 0.0 collective-permute-done.1
  21.8 0.0 collective-permute-done.2
  21.8 14.7 %collective-permute-done.3 = bf16[10,48,128]{2,1,0:T(8,128)(2,1)S(1)} collective-permute-done((bf16[10,48,128]{2,1,0:T(8,128)(2,1)S(1)}, bf16[10,48,128]{2,1,0:T(8,128)(2,1)S(1)}, u32[]{:S(2)}, u32[]{:S(2)}) %collective-permute-start.3) | collective-permute-done | bytes 122912 | tf_op jit(solution)/shard_map/ppermute | solution.py:28
  36.5 0.0 copy-start.4
  36.5 0.1 collective-permute-start.4
  36.6 0.0 collective-permute-done.6.arrived_values
  36.6 1.8 %collective-permute-done.4.given_rows = bf16[40,48,128]{2,1,0:T(8,128)(2,1)S(1)} collective-permute-done((bf16[40,48,128]{2,1,0:T(8,128)(2,1)S(1)}, bf16[40,48,128]{2,1,0:T(8,128)(2,1)S(1)}, u32[]{:S(2)}, u32[]{:S(2)}) %collective-permute-start.4) | collective-permute-done | bytes 491552 | tf_op jit(solution)/shard_map/ppermute | solution.py:28
  38.5 2.4 %shard_map.160 = (f32[40,48,128]{2,1,0:T(8,128)S(1)}, bf16[40,48,128]{2,1,0:T(8,128)(2,1)S(1)}, bf16[2,128,1024]{2,1,0:T(8,128)(2,1)}, bf16[2,128,1024]{2,1,0:T(8,128)(2,1)}) custom-call(bf16[40,48,128]{2,1,0:T(8,128)(2,1)S(1)} %constant_dynamic-update-slice_fusion.2.kept_rows, bf16[40,48,128]{2,1,0:T(8,128)(2,1)S(1)} %collective-permute-done.4.given_rows, ...), custom_call_target="tpu_custom_call" | custom-call | flops 400000000 | bytes 8388608 | tf_op jit(solution)/shard_map/pallas_call | solution.py:361
  40.9 0.2 collective-permute-start.7
  41.1 0.2 select_reduce_fusion.1
  41.3 1.5 %collective-permute-done.7 = bf16[40,48,128]{2,1,0:T(8,128)(2,1)S(1)} collective-permute-done((bf16[40,48,128]{2,1,0:T(8,128)(2,1)S(1)}, bf16[40,48,128]{2,1,0:T(8,128)(2,1)S(1)}, u32[]{:S(2)}, u32[]{:S(2)}) %collective-permute-start.7) | collective-permute-done | bytes 491552 | tf_op jit(solution)/shard_map/ppermute | solution.py:28
  42.8 0.1 add_convert_fusion
  42.9 0.1 collective-permute-start.10
  43.0 1.5 %collective-permute-start.8 = (bf16[10,48,128]{2,1,0:T(8,128)(2,1)S(1)}, bf16[10,48,128]{2,1,0:T(8,128)(2,1)S(1)}, u32[]{:S(2)}, u32[]{:S(2)}) collective-permute-start(bf16[10,48,128]{2,1,0:T(8,128)(2,1)S(1)} %get-tuple-element.41), channel_id=1, source_target_pairs={{0,2},{1,3},{2,0},{3,1},{4,6},{5,7},{6,4},{7,5},{8,10},{9,11},{10,... | collective-permute-start | bytes 368648 | tf_op jit(solution)/shard_map/ppermute | solution.py:28
  44.5 2.0 %collective-permute-start.9 = (bf16[10,48,128]{2,1,0:T(8,128)(2,1)S(1)}, bf16[10,48,128]{2,1,0:T(8,128)(2,1)S(1)}, u32[]{:S(2)}, u32[]{:S(2)}) collective-permute-start(bf16[10,48,128]{2,1,0:T(8,128)(2,1)S(1)} %get-tuple-element.43), channel_id=1, source_target_pairs={{0,4},{1,5},{2,6},{3,7},{4,0},{5,1},{6,2},{7,3},{8,12},{9,13},{10,... | collective-permute-start | bytes 368648 | tf_op jit(solution)/shard_map/ppermute | solution.py:28
  46.5 3.6 %collective-permute-done.10 = bf16[10,48,128]{2,1,0:T(8,128)(2,1)S(1)} collective-permute-done((bf16[10,48,128]{2,1,0:T(8,128)(2,1)S(1)}, bf16[10,48,128]{2,1,0:T(8,128)(2,1)S(1)}, u32[]{:S(2)}, u32[]{:S(2)}) %collective-permute-start.10) | collective-permute-done | bytes 122912 | tf_op jit(solution)/shard_map/ppermute | solution.py:28
  50.1 1.0 %collective-permute-done.8 = bf16[10,48,128]{2,1,0:T(8,128)(2,1)S(1)} collective-permute-done((bf16[10,48,128]{2,1,0:T(8,128)(2,1)S(1)}, bf16[10,48,128]{2,1,0:T(8,128)(2,1)S(1)}, u32[]{:S(2)}, u32[]{:S(2)}) %collective-permute-start.8) | collective-permute-done | bytes 122912 | tf_op jit(solution)/shard_map/ppermute | solution.py:28
  51.1 0.1 convert_add_fusion
  51.2 1.5 %collective-permute-start.11 = (bf16[5,48,128]{2,1,0:T(8,128)(2,1)S(1)}, bf16[5,48,128]{2,1,0:T(8,128)(2,1)S(1)}, u32[]{:S(2)}, u32[]{:S(2)}) collective-permute-start(bf16[5,48,128]{2,1,0:T(8,128)(2,1)S(1)} %slice.43), channel_id=1, source_target_pairs={{0,8},{1,9},{2,10},{3,11},{4,12},{5,13},{6,14},{7,15},{8,0},{9,1},... | collective-permute-start | bytes 184328 | tf_op jit(solution)/shard_map/ppermute | solution.py:28
  52.7 4.5 %collective-permute-done.11.away = bf16[5,48,128]{2,1,0:T(8,128)(2,1)S(1)} collective-permute-done((bf16[5,48,128]{2,1,0:T(8,128)(2,1)S(1)}, bf16[5,48,128]{2,1,0:T(8,128)(2,1)S(1)}, u32[]{:S(2)}, u32[]{:S(2)}) %collective-permute-start.11) | collective-permute-done | bytes 61472 | tf_op jit(solution)/shard_map/ppermute | solution.py:28
  57.2 1.5 %shard_map.161 = bf16[12,6144]{1,0:T(8,128)(2,1)} custom-call(s32[13,12]{1,0:T(8,128)S(1)} %get-tuple-element.21.plan, s32[1]{0:T(128)} %bitcast.2.mine, f32[2,12]{1,0:T(2,128)S(1)} %fusion.2.weights, f32[12,48,128]{2,1,0:T(8,128)S(1)} %get-tuple-element.30.state, f32[5,48,128]{2,1,0:T(8,128)S(1)} %slice.37.own, ...), custom_call_target="tpu_custom_call" | custom-call | tf_op jit(solution)/shard_map/pallas_call | solution.py:404
  (21 shorter events, 0.2 us)
Async XLA Ops:
  0.6 40.4 %copy-start = (bf16[6144,8]{0,1:T(8,128)(2,1)S(1)}, bf16[6144,8]{0,1:T(8,128)(2,1)}, u32[]{:S(2)}) copy-start(bf16[6144,8]{0,1:T(8,128)(2,1)} %param.24) | copy-start | bytes 294916
  7.0 7.1 %collective-permute-start = (bf16[5,48,128]{2,1,0:T(8,128)(2,1)S(1)}, bf16[5,48,128]{2,1,0:T(8,128)(2,1)S(1)}, u32[]{:S(2)}, u32[]{:S(2)}) collective-permute-start(bf16[5,48,128]{2,1,0:T(8,128)(2,1)S(1)} %get-tuple-element.32), channel_id=1, source_target_pairs={{0,8},{1,9},{2,10},{3,11},{4,12},{5,13},{6,14},{7,15},{8,0},{9,1},... | collective-permute-start | bytes 184328 | tf_op jit(solution)/shard_map/ppermute | solution.py:28
  10.4 28.1 %copy-start.1 = (bf16[6144,128]{1,0:T(8,128)(2,1)S(1)}, bf16[6144,128]{1,0:T(8,128)(2,1)}, u32[]{:S(2)}) copy-start(bf16[6144,128]{1,0:T(8,128)(2,1)} %w_gate.1) | copy-start | bytes 4718596
  10.4 28.1 %copy-start.2 = (bf16[6144,128]{1,0:T(8,128)(2,1)S(1)}, bf16[6144,128]{1,0:T(8,128)(2,1)}, u32[]{:S(2)}) copy-start(bf16[6144,128]{1,0:T(8,128)(2,1)} %w_up.1) | copy-start | bytes 4718596
  10.4 28.1 %copy-start.3 = (bf16[128,6144]{1,0:T(8,128)(2,1)S(1)}, bf16[128,6144]{1,0:T(8,128)(2,1)}, u32[]{:S(2)}) copy-start(bf16[128,6144]{1,0:T(8,128)(2,1)} %w_down.1) | copy-start | bytes 4718596
  14.2 7.6 %collective-permute-start.1 = (bf16[10,48,128]{2,1,0:T(8,128)(2,1)S(1)}, bf16[10,48,128]{2,1,0:T(8,128)(2,1)S(1)}, u32[]{:S(2)}, u32[]{:S(2)}) collective-permute-start(bf16[10,48,128]{2,1,0:T(8,128)(2,1)S(1)} %get-tuple-element.44), channel_id=1, source_target_pairs={{0,2},{1,3},{2,0},{3,1},{4,6},{5,7},{6,4},{7,5},{8,10},{9,11},{10,... | collective-permute-start | bytes 368648 | tf_op jit(solution)/shard_map/ppermute | solution.py:28
  16.9 4.9 %collective-permute-start.2 = (bf16[10,48,128]{2,1,0:T(8,128)(2,1)S(1)}, bf16[10,48,128]{2,1,0:T(8,128)(2,1)S(1)}, u32[]{:S(2)}, u32[]{:S(2)}) collective-permute-start(bf16[10,48,128]{2,1,0:T(8,128)(2,1)S(1)} %get-tuple-element.44), channel_id=1, source_target_pairs={{0,4},{1,5},{2,6},{3,7},{4,0},{5,1},{6,2},{7,3},{8,12},{9,13},{10,... | collective-permute-start | bytes 368648 | tf_op jit(solution)/shard_map/ppermute | solution.py:28
  18.1 18.5 %collective-permute-start.5 = (bf16[2,128,1024]{2,1,0:T(8,128)(2,1)S(1)}, bf16[2,128,1024]{2,1,0:T(8,128)(2,1)S(1)}, u32[]{:S(2)}, u32[]{:S(2)}) collective-permute-start(bf16[2,128,1024]{2,1,0:T(8,128)(2,1)S(1)} %get-tuple-element.33), channel_id=1, source_target_pairs={{0,1},{1,2},{2,3},{3,4},{4,5},{5,6},{6,7},{7,8},{8,9},{9,10},{10,1... | collective-permute-start | bytes 1572872 | tf_op jit(solution)/shard_map/ppermute | solution.py:457
  18.1 18.5 %collective-permute-start.6 = (bf16[2,128,1024]{2,1,0:T(8,128)(2,1)S(1)}, bf16[2,128,1024]{2,1,0:T(8,128)(2,1)S(1)}, u32[]{:S(2)}, u32[]{:S(2)}) collective-permute-start(bf16[2,128,1024]{2,1,0:T(8,128)(2,1)S(1)} %get-tuple-element.34), channel_id=1, source_target_pairs={{0,1},{1,2},{2,3},{3,4},{4,5},{5,6},{6,7},{7,8},{8,9},{9,10},{10,1... | collective-permute-start | bytes 1572872 | tf_op jit(solution)/shard_map/ppermute | solution.py:458
  18.8 17.7 %collective-permute-start.3 = (bf16[10,48,128]{2,1,0:T(8,128)(2,1)S(1)}, bf16[10,48,128]{2,1,0:T(8,128)(2,1)S(1)}, u32[]{:S(2)}, u32[]{:S(2)}) collective-permute-start(bf16[10,48,128]{2,1,0:T(8,128)(2,1)S(1)} %get-tuple-element.44), channel_id=1, source_target_pairs={{0,6},{1,7},{2,4},{3,5},{4,2},{5,3},{6,0},{7,1},{8,14},{9,15},{10,... | collective-permute-start | bytes 368648 | tf_op jit(solution)/shard_map/ppermute | solution.py:28
  36.5 4.5 %copy-start.4 = (s32[12,2]{0,1:T(2,128)S(1)}, s32[12,2]{0,1:T(2,128)}, u32[]{:S(2)}) copy-start(s32[12,2]{0,1:T(2,128)} %param.23) | copy-start | bytes 292
  36.5 1.9 %collective-permute-start.4 = (bf16[40,48,128]{2,1,0:T(8,128)(2,1)S(1)}, bf16[40,48,128]{2,1,0:T(8,128)(2,1)S(1)}, u32[]{:S(2)}, u32[]{:S(2)}) collective-permute-start(bf16[40,48,128]{2,1,0:T(8,128)(2,1)S(1)} %constant_dynamic-update-slice_fusion.2.kept_rows), channel_id=1, source_target_pairs={{0,1},{1,0},{2,3},{3,2},{4,5},{5,4},{6,7},{7,6},{8,9},{9,8},{10,11... | collective-permute-start | bytes 1474568 | tf_op jit(solution)/shard_map/ppermute | solution.py:28
  40.9 1.9 %collective-permute-start.7 = (bf16[40,48,128]{2,1,0:T(8,128)(2,1)S(1)}, bf16[40,48,128]{2,1,0:T(8,128)(2,1)S(1)}, u32[]{:S(2)}, u32[]{:S(2)}) collective-permute-start(bf16[40,48,128]{2,1,0:T(8,128)(2,1)S(1)} %get-tuple-element.36), channel_id=1, source_target_pairs={{0,1},{1,0},{2,3},{3,2},{4,5},{5,4},{6,7},{7,6},{8,9},{9,8},{10,11... | collective-permute-start | bytes 1474568 | tf_op jit(solution)/shard_map/ppermute | solution.py:28
  42.9 7.2 %collective-permute-start.10 = (bf16[10,48,128]{2,1,0:T(8,128)(2,1)S(1)}, bf16[10,48,128]{2,1,0:T(8,128)(2,1)S(1)}, u32[]{:S(2)}, u32[]{:S(2)}) collective-permute-start(bf16[10,48,128]{2,1,0:T(8,128)(2,1)S(1)} %get-tuple-element.42), channel_id=1, source_target_pairs={{0,6},{1,7},{2,4},{3,5},{4,2},{5,3},{6,0},{7,1},{8,14},{9,15},{10,... | collective-permute-start | bytes 368648 | tf_op jit(solution)/shard_map/ppermute | solution.py:28
  43.0 8.1 %collective-permute-start.8 = (bf16[10,48,128]{2,1,0:T(8,128)(2,1)S(1)}, bf16[10,48,128]{2,1,0:T(8,128)(2,1)S(1)}, u32[]{:S(2)}, u32[]{:S(2)}) collective-permute-start(bf16[10,48,128]{2,1,0:T(8,128)(2,1)S(1)} %get-tuple-element.41), channel_id=1, source_target_pairs={{0,2},{1,3},{2,0},{3,1},{4,6},{5,7},{6,4},{7,5},{8,10},{9,11},{10,... | collective-permute-start | bytes 368648 | tf_op jit(solution)/shard_map/ppermute | solution.py:28
  44.5 6.6 %collective-permute-start.9 = (bf16[10,48,128]{2,1,0:T(8,128)(2,1)S(1)}, bf16[10,48,128]{2,1,0:T(8,128)(2,1)S(1)}, u32[]{:S(2)}, u32[]{:S(2)}) collective-permute-start(bf16[10,48,128]{2,1,0:T(8,128)(2,1)S(1)} %get-tuple-element.43), channel_id=1, source_target_pairs={{0,4},{1,5},{2,6},{3,7},{4,0},{5,1},{6,2},{7,3},{8,12},{9,13},{10,... | collective-permute-start | bytes 368648 | tf_op jit(solution)/shard_map/ppermute | solution.py:28
  51.2 6.1 %collective-permute-start.11 = (bf16[5,48,128]{2,1,0:T(8,128)(2,1)S(1)}, bf16[5,48,128]{2,1,0:T(8,128)(2,1)S(1)}, u32[]{:S(2)}, u32[]{:S(2)}) collective-permute-start(bf16[5,48,128]{2,1,0:T(8,128)(2,1)S(1)} %slice.43), channel_id=1, source_target_pairs={{0,8},{1,9},{2,10},{3,11},{4,12},{5,13},{6,14},{7,15},{8,0},{9,1},... | collective-permute-start | bytes 184328 | tf_op jit(solution)/shard_map/ppermute | solution.py:28

commit v3 on v2

--- a/solution.py
+++ b/solution.py
@@ -1,3 +1,4 @@
+import functools
 import math
 
 import jax
@@ -30,12 +31,13 @@
 
 def stage_kernel(table_at, lengths_at, migrate_at, chosen_at, mine, queries_at, residual_at,
                  new_keys_at, new_values_at, key_pool_at, value_pool_at,
-                 plan, key_pool, value_pool, heads_q, heads_r, moved_keys, moved_values,
-                 table, lengths, migrate, chosen, queries, residual, new_keys, new_values,
-                 fresh, small_sems, row_sems, pool_sems):
+                 plan, key_pool, value_pool, heads_q, heads_r, *rest):
+    moved, scratch = rest[:len(GROUPS)], rest[len(GROUPS):]
+    (table, lengths, migrate, chosen, queries, residual, new_keys, new_values,
+     fresh, small_sems, row_sems, pool_sems) = scratch
     pages, rows = table.shape
     page = key_pool.shape[1]
-    moves = moved_keys.shape[0]
+    moves = migrate.shape[0]
     heads = heads_q.shape[0] // rows
     small = [
         pltpu.make_async_copy(source, target, small_sems.at[i])
@@ -87,12 +89,21 @@
         plan[pages + 2, r] = away_slots[r]
         taken_own = taken_own + own
         taken_away = taken_away + away
-    behind = taken_away
+    only_own = [
+        jnp.where(own_slot >= 0, 1, 0) * jnp.where(away_slot >= 0, 0, 1)
+        for own_slot, away_slot in zip(own_slots, away_slots)
+    ]
+    middle = taken_away
+    behind = taken_away + sum(only_own)
+    for bound, count in enumerate((taken_away, behind)):
+        plan[pages + 4, bound] = (count + 1) // 2
     for r in range(rows):
         is_away = away_slots[r] >= 0
-        plan[pages + 3, jnp.where(is_away, away_slots[r], behind)] = jnp.int32(r)
-        behind = behind + jnp.where(is_away, 0, 1)
-    plan[pages + 4, 0] = taken_away
+        is_own = only_own[r] == 1
+        place = jnp.where(is_away, away_slots[r], jnp.where(is_own, middle, behind))
+        plan[pages + 3, place] = jnp.int32(r)
+        middle = middle + only_own[r]
+        behind = behind + jnp.where(is_away | is_own, 0, 1)
     for copy, side in zip(wide[2:], (0, 1)):
         copy.wait()
         fresh[side] = (new_keys, new_values)[side][...].astype(F32)
@@ -113,12 +124,17 @@
         for p in range(pages):
             number = table[p, request]
             kept = inside + p * page <= length
-            for buffer, out in ((key_pool, moved_keys), (value_pool, moved_values)):
+            for side, buffer in enumerate((key_pool, value_pool)):
+                group, place = PLACES[side * moves + m]
                 block = jnp.where(kept, buffer[number].astype(F32), 0.0)
-                out[m, p * page:(p + 1) * page, :] = block.astype(BF16)
+                moved[group][place, p * page:(p + 1) * page, :] = block.astype(BF16)
 
 
 POOL_CUTS = 3
+GROUPS = ((0, 1), (2, 3))
+PLACES = [(g, group.index(i)) for i in range(sum(map(len, GROUPS)))
+          for g, group in enumerate(GROUPS) if i in group]
+COST = 1 << 20
 
 
 def staged(page_table, lengths, migrate, chosen, mine, queries, residual, new_keys, new_values,
@@ -128,7 +144,10 @@
     kv_width = new_keys.shape[1]
     moves = migrate.shape[0]
     pages = page_table.shape[1]
-    moved = jax.ShapeDtypeStruct((moves, pages * key_pool.shape[1], kv_width), BF16)
+    moved = tuple(
+        jax.ShapeDtypeStruct((len(group), pages * key_pool.shape[1], kv_width), BF16)
+        for group in GROUPS
+    )
     split = jax.ShapeDtypeStruct((rows * heads, HEAD_DIM), F32)
     return pl.pallas_call(
         stage_kernel,
@@ -136,10 +155,10 @@
             jax.ShapeDtypeStruct((pages + 5, rows), jnp.int32),
             jax.ShapeDtypeStruct(key_pool.shape, BF16),
             jax.ShapeDtypeStruct(value_pool.shape, BF16),
-            split, split, moved, moved,
-        ),
+            split, split,
+        ) + moved,
         in_specs=[HBM] * 4 + [SMEM] + [HBM] * 6,
-        out_specs=(SMEM,) + (VMEM,) * 6,
+        out_specs=(SMEM,) + (VMEM,) * (4 + len(moved)),
         scratch_shapes=[
             pltpu.SMEM((pages, rows), jnp.int32),
             pltpu.SMEM(lengths.shape, jnp.int32),
@@ -243,13 +262,12 @@
 
         return carry
 
-    lax.fori_loop(0, (plan[pages + 4, 0] + 1) // 2, step, 0)
-
-
-def rest_kernel(plan, key_pool, value_pool, heads_q, heads_r, state_in, normed_in, own_in,
-                state_out, normed_out, own_out):
+    lax.fori_loop(0, plan[pages + 4, 0], step, 0)
+
+
+def own_kernel(plan, key_pool, value_pool, heads_q, heads_r, state_in, normed_in, own_in,
+               state_out, normed_out, own_out):
     pages = plan.shape[0] - 5
-    rows = state_out.shape[0]
     state_out[...] = state_in[...]
     normed_out[...] = normed_in[...]
     own_out[...] = own_in[...]
@@ -267,7 +285,20 @@
 
         return carry
 
-    lax.fori_loop((plan[pages + 4, 0] + 1) // 2, rows // 2, step, 0)
+    lax.fori_loop(plan[pages + 4, 0], plan[pages + 4, 1], step, 0)
+
+
+def rest_kernel(plan, key_pool, value_pool, heads_q, heads_r, state_in, normed_in, *rest):
+    state_out, normed_out = rest[-2:]
+    pages = plan.shape[0] - 5
+    state_out[...] = state_in[...]
+    normed_out[...] = normed_in[...]
+
+    def step(pair, carry):
+        attend_pair(plan, pair, key_pool, value_pool, heads_q, heads_r, state_out, normed_out)
+        return carry
+
+    lax.fori_loop(plan[pages + 4, 1], state_out.shape[0] // 2, step, 0)
 
 
 def attend_shapes(rows, heads):
@@ -280,54 +311,25 @@
     )
 
 
-def attended_away(plan, key_pool, value_pool, heads_q, heads_r):
+def attended(kernel, outs, cost, plan, key_pool, value_pool, heads_q, heads_r, *before):
     rows = plan.shape[1]
     heads = heads_q.shape[0] // rows
     return pl.pallas_call(
-        away_kernel,
-        out_shape=attend_shapes(rows, heads),
-        in_specs=[SMEM] + [VMEM] * 4,
-        out_specs=(VMEM,) * 4,
+        kernel,
+        out_shape=attend_shapes(rows, heads)[:outs],
+        in_specs=[SMEM] + [VMEM] * (4 + len(before)),
+        out_specs=(VMEM,) * outs,
         compiler_params=pltpu.CompilerParams(vmem_limit_bytes=8 << 20),
-        cost_estimate=pl.CostEstimate(
-            flops=1 << 27, bytes_accessed=8 << 20, transcendentals=1 << 15
-        ),
-    )(plan, key_pool, value_pool, heads_q, heads_r)
-
-
-def attended_rest(plan, key_pool, value_pool, heads_q, heads_r, state, normed, own):
-    rows, heads, _ = state.shape
-    return pl.pallas_call(
-        rest_kernel,
-        out_shape=attend_shapes(rows, heads)[:3],
-        in_specs=[SMEM] + [VMEM] * 7,
-        out_specs=(VMEM,) * 3,
-        compiler_params=pltpu.CompilerParams(vmem_limit_bytes=8 << 20),
-        cost_estimate=pl.CostEstimate(
-            flops=1 << 28, bytes_accessed=24 << 20, transcendentals=1 << 16
-        ),
-    )(plan, key_pool, value_pool, heads_q, heads_r, state, normed, own)
-
-
-def expert_kernel(kept_rows, given_rows, w_gate, w_up, w_down, arrived_keys, arrived_values,
-                  kept, given, moved_keys, moved_values, split, flat, back, sems):
-    copies = [
-        pltpu.make_async_copy(arrived_keys, moved_keys, sems.at[0]),
-        pltpu.make_async_copy(arrived_values, moved_values, sems.at[1]),
-    ]
-
-    @pl.when(pl.program_id(0) == 0)
-    def _():
-        for copy in copies:
-            copy.start()
-
-    block, heads, _ = kept_rows.shape
-    half = block * heads
-    split[:half] = kept_rows[...].astype(F32).reshape(half, HEAD_DIM)
-    split[half:] = given_rows[...].astype(F32).reshape(half, HEAD_DIM)
+        cost_estimate=pl.CostEstimate(flops=cost, bytes_accessed=cost >> 4, transcendentals=0),
+    )(plan, key_pool, value_pool, heads_q, heads_r, *before)
+
+
+def expert_rows(rows, w_gate, w_up, w_down, split, flat, back):
+    block, heads, _ = rows.shape
+    split[...] = rows[...].astype(F32).reshape(block * heads, HEAD_DIM)
     for h in range(heads):
         cols = slice(h * HEAD_DIM, (h + 1) * HEAD_DIM)
-        flat[:, cols] = split[pl.ds(h, 2 * block, stride=heads), :].astype(BF16)
+        flat[:, cols] = split[pl.ds(h, block, stride=heads), :].astype(BF16)
     gate = jnp.dot(flat[...], w_gate[...], preferred_element_type=F32)
     up = jnp.dot(flat[...], w_up[...], preferred_element_type=F32)
     hidden = (gate / (1.0 + jnp.exp(-gate)) * up).astype(BF16)
@@ -336,24 +338,23 @@
         cols = slice(first * HEAD_DIM, (first + wide) * HEAD_DIM)
         part = jnp.dot(hidden, w_down[:, cols], preferred_element_type=F32)
         for h in range(wide):
-            back[pl.ds(first + h, 2 * block, stride=heads), :] = part[
+            back[pl.ds(first + h, block, stride=heads), :] = part[
                 :, h * HEAD_DIM:(h + 1) * HEAD_DIM
             ]
-    kept[...] = back[:half].reshape(block, heads, HEAD_DIM)
-    given[...] = back[half:].reshape(block, heads, HEAD_DIM).astype(BF16)
-
-    @pl.when(pl.program_id(0) == pl.num_programs(0) - 1)
-    def _():
-        for copy in copies:
-            copy.wait()
-
-
-def expert_parts(kept_rows, given_rows, w_gate, w_up, w_down, arrived_keys, arrived_values):
-    total, heads, _ = kept_rows.shape
+
+
+def expert_kernel(rows, w_gate, w_up, w_down, *rest):
+    sums, split, flat, back = rest[-4:]
+    expert_rows(rows, w_gate, w_up, w_down, split, flat, back)
+    sums[...] = back[...].reshape(sums.shape).astype(sums.dtype)
+
+
+def expert_parts(rows, w_gate, w_up, w_down, dtype, *after):
+    total, heads, _ = rows.shape
     block = 8 * CAP
     if total % block:
         block = CAP
-    rows = pl.BlockSpec((block, heads, HEAD_DIM), lambda i: (i, 0, 0))
+    spec = pl.BlockSpec((block, heads, HEAD_DIM), lambda i: (i, 0, 0))
 
     def fixed(array):
         return pl.BlockSpec(array.shape, lambda i: (0, 0))
@@ -361,54 +362,138 @@
     return pl.pallas_call(
         expert_kernel,
         grid=(total // block,),
-        out_shape=(
-            jax.ShapeDtypeStruct(kept_rows.shape, F32),
-            jax.ShapeDtypeStruct(kept_rows.shape, BF16),
-            jax.ShapeDtypeStruct(arrived_keys.shape, BF16),
-            jax.ShapeDtypeStruct(arrived_values.shape, BF16),
+        out_shape=jax.ShapeDtypeStruct(rows.shape, dtype),
+        in_specs=[spec, fixed(w_gate), fixed(w_up), fixed(w_down)] + [ANY] * len(after),
+        out_specs=spec,
+        scratch_shapes=[
+            pltpu.VMEM((block * heads, HEAD_DIM), F32),
+            pltpu.VMEM((block, heads * HEAD_DIM), BF16),
+            pltpu.VMEM((block * heads, HEAD_DIM), F32),
+        ],
+        compiler_params=pltpu.CompilerParams(vmem_limit_bytes=24 << 20),
+        cost_estimate=pl.CostEstimate(
+            flops=200_000_000, bytes_accessed=4 << 20, transcendentals=5120
         ),
-        in_specs=[rows, rows, fixed(w_gate), fixed(w_up), fixed(w_down), ANY, ANY],
-        out_specs=(rows, rows, HBM, HBM),
-        scratch_shapes=[
-            pltpu.VMEM((2 * block * heads, HEAD_DIM), F32),
-            pltpu.VMEM((2 * block, heads * HEAD_DIM), BF16),
-            pltpu.VMEM((2 * block * heads, HEAD_DIM), F32),
-            pltpu.SemaphoreType.DMA((2,)),
-        ],
-        compiler_params=pltpu.CompilerParams(vmem_limit_bytes=32 << 20),
-        cost_estimate=pl.CostEstimate(
-            flops=400_000_000, bytes_accessed=8 << 20, transcendentals=10240
-        ),
-    )(kept_rows, given_rows, w_gate, w_up, w_down, arrived_keys, arrived_values)
-
-
-def finish_kernel(plan, mine, weights, state, own, away, mixed, rows_split):
+    )(rows, w_gate, w_up, w_down, *after)
+
+
+def join_kernel(own, away, *rest):
+    both = rest[-1]
+    both[:CAP] = own[...]
+    both[CAP:] = away[...]
+
+
+def joined(own, away, *after):
+    return pl.pallas_call(
+        join_kernel,
+        out_shape=jax.ShapeDtypeStruct((2 * CAP,) + own.shape[1:], BF16),
+        in_specs=[VMEM, VMEM] + [ANY] * len(after),
+        out_specs=VMEM,
+        compiler_params=pltpu.CompilerParams(vmem_limit_bytes=4 << 20),
+    )(own, away, *after)
+
+
+def hold_kernel(array, after, copy):
+    copy[...] = array[...]
+
+
+def held_back(array, after):
+    return pl.pallas_call(
+        hold_kernel,
+        out_shape=jax.ShapeDtypeStruct(array.shape, array.dtype),
+        in_specs=[VMEM, ANY],
+        out_specs=VMEM,
+        compiler_params=pltpu.CompilerParams(vmem_limit_bytes=4 << 20),
+    )(array, after)
+
+
+def gather_kernel(count, *refs):
+    blocks, rows = refs[:count], refs[-1]
+    size = blocks[0].shape[0]
+    for i, block in enumerate(blocks):
+        rows[i * size:(i + 1) * size] = block[...]
+
+
+def gathered(blocks, *after):
+    size, heads, depth = blocks[0].shape
+    return pl.pallas_call(
+        functools.partial(gather_kernel, len(blocks)),
+        out_shape=jax.ShapeDtypeStruct((size * len(blocks), heads, depth), BF16),
+        in_specs=[VMEM] * len(blocks) + [ANY] * len(after),
+        out_specs=VMEM,
+        compiler_params=pltpu.CompilerParams(vmem_limit_bytes=24 << 20),
+    )(*blocks, *after)
+
+
+def pair_sum_kernel(count, kept, received, *rest):
+    parts = rest[-2 * count:]
+    for i in range(count):
+        for side in range(2):
+            at = slice((2 * i + side) * CAP, (2 * i + side + 1) * CAP)
+            parts[side * count + i][...] = (kept[at] + received[at].astype(F32)).astype(BF16)
+
+
+def pair_sums(kept, received, *after):
+    count = kept.shape[0] // (2 * CAP)
+    part = jax.ShapeDtypeStruct((CAP,) + kept.shape[1:], BF16)
+    parts = pl.pallas_call(
+        functools.partial(pair_sum_kernel, count),
+        out_shape=(part,) * (2 * count),
+        in_specs=[VMEM, VMEM] + [ANY] * len(after),
+        out_specs=(VMEM,) * (2 * count),
+        compiler_params=pltpu.CompilerParams(vmem_limit_bytes=24 << 20),
+    )(kept, received, *after)
+    return parts[:count], parts[count:]
+
+
+def finish_kernel(count, plan, mine, weights, state, away, *rest):
+    owns, rest = rest[:count], rest[count:]
+    arrived, (mixed, moved_keys, moved_values, rows_split, sems) = rest[:-5], rest[-5:]
+    moves = moved_keys.shape[0]
+    targets = [moved.at[m] for moved in (moved_keys, moved_values) for m in range(moves)]
+    copies = [
+        pltpu.make_async_copy(arrived[group].at[place], target, sems.at[i])
+        for i, ((group, place), target) in enumerate(zip(PLACES, targets))
+    ]
+    for copy in copies:
+        copy.start()
     rows, heads, _ = state.shape
     pages = plan.shape[0] - 5
     expert = mine[0]
     for r in range(rows):
         total = state[r]
-        for row, sums, number in ((pages + 1, own, expert), (pages + 2, away, 1 - expert)):
+        for row, sums, number in ((pages + 1, owns, expert), (pages + 2, (away,), 1 - expert)):
             slot = plan[row, r]
             factor = jnp.where(slot >= 0, weights[number, r], 0.0)
-            total = total + factor * sums[jnp.clip(slot, 0, CAP - 1)].astype(F32)
+            at = jnp.clip(slot, 0, CAP - 1)
+            total = total + factor * sum(part[at].astype(F32) for part in sums)
         rows_split[r * heads:(r + 1) * heads, :] = total
     for h in range(heads):
         mixed[:, h * HEAD_DIM:(h + 1) * HEAD_DIM] = rows_split[
             pl.ds(h, rows, stride=heads), :
         ].astype(BF16)
-
-
-def finished(plan, mine, weights, state, own, away):
+    for copy in copies:
+        copy.wait()
+
+
+def finished(plan, mine, weights, state, away, owns, arrived):
     rows, heads, _ = state.shape
-    return pl.pallas_call(
-        finish_kernel,
-        out_shape=jax.ShapeDtypeStruct((rows, heads * HEAD_DIM), BF16),
-        in_specs=[SMEM] * 3 + [VMEM] * 3,
-        out_specs=VMEM,
-        scratch_shapes=[pltpu.VMEM((rows * heads, HEAD_DIM), F32)],
+    moved = jax.ShapeDtypeStruct((len(PLACES) // 2,) + arrived[0].shape[1:], BF16)
+    return pl.pallas_call(
+        functools.partial(finish_kernel, len(owns)),
+        out_shape=(
+            jax.ShapeDtypeStruct((rows, heads * HEAD_DIM), BF16),
+            moved,
+            moved,
+        ),
+        in_specs=[SMEM] * 3 + [VMEM] * (2 + len(owns)) + [ANY] * len(arrived),
+        out_specs=(VMEM, HBM, HBM),
+        scratch_shapes=[
+            pltpu.VMEM((rows * heads, HEAD_DIM), F32),
+            pltpu.SemaphoreType.DMA((len(PLACES),)),
+        ],
         compiler_params=pltpu.CompilerParams(vmem_limit_bytes=8 << 20),
-    )(plan, mine, weights, state, own, away)
+    )(plan, mine, weights, state, away, *owns, *arrived)
 
 
 def gate_weights(normed, router_weight, chosen):
@@ -450,33 +535,35 @@
     masks = list(range(2, swap, 2))
     mine = (lax.axis_index("attn") // (length // EXP_ON)).astype(jnp.int32).reshape(1)
     along = [(i, (i + 1) % length) for i in range(length)]
-    plan, keys, values, heads_q, heads_r, leave_keys, leave_values = staged(
+    plan, keys, values, heads_q, heads_r, *leave = staged(
         page_table, lengths, migrate, chosen, mine, queries, residual, new_keys, new_values,
         key_pool, value_pool,
     )
-    arrived_keys = lax.ppermute(leave_keys, "attn", along)
-    arrived_values = lax.ppermute(leave_values, "attn", along)
-    state, normed, own, away = attended_away(plan, keys, values, heads_q, heads_r)
+    arrived = [None] * len(leave)
+    arrived[0] = lax.ppermute(leave[0], "attn", along)
+    arrived[1] = lax.ppermute(leave[1], "attn", along)
+    held = (plan, keys, values, heads_q, heads_r)
+    state, normed, own, away = attended(away_kernel, 4, COST, *held)
     swapped = exchanged(away, swap)
-    state, normed, own = attended_rest(
-        plan, keys, values, heads_q, heads_r, state, normed, own
-    )
+    state, normed, own = attended(own_kernel, 3, COST, *held, state, normed, own)
+    rows_here = joined(own, swapped, arrived[0])
+    blocks = [rows_here] + [exchanged(rows_here, mask) for mask in masks]
+    state, normed = attended(rest_kernel, 2, COST, *held, state, normed, rows_here)
+    mine_rows = gathered(blocks, state)
     weights = gate_weights(normed, router_weight, chosen)
-    rows_here = jnp.concatenate([own, swapped])
-    mine_rows = jnp.concatenate([rows_here] + [exchanged(rows_here, mask) for mask in masks])
     other_rows = exchanged(mine_rows, 1)
-    kept, given, moved_keys, moved_values = expert_parts(
-        mine_rows, other_rows, w_gate, w_up, w_down, arrived_keys, arrived_values
-    )
-    summed = (kept + exchanged(given, 1).astype(F32)).astype(BF16)
-    sent = 2 * CAP
-    back = summed[:sent].astype(F32)
-    for i, mask in enumerate(masks):
-        at = (i + 1) * sent
-        back = back + exchanged(summed[at:at + sent], mask).astype(F32)
-    own_sums = back[:CAP]
-    away_sums = exchanged(back[CAP:].astype(BF16), swap)
-    mixed = finished(plan, mine, weights, state, own_sums, away_sums)
+    kept = expert_parts(mine_rows, w_gate, w_up, w_down, F32)
+    given = expert_parts(other_rows, w_gate, w_up, w_down, BF16, kept, arrived[1])
+    own_parts, away_parts = pair_sums(kept, exchanged(given, 1))
+    back = away_parts[0].astype(F32)
+    for part, mask in zip(away_parts[1:], masks):
+        back = back + exchanged(part, mask).astype(F32)
+    own_sums = [own_parts[0]]
+    own_sums += [exchanged(part, mask) for part, mask in zip(own_parts[1:], masks)]
+    away_sums = exchanged(back.astype(BF16), swap)
+    mixed, moved_keys, moved_values = finished(
+        plan, mine, weights, state, away_sums, own_sums, arrived
+    )
     return (mixed, moved_keys, moved_values)
 
 

time: 58.9 us -> 51.8 us (0.88)
  waiting for transfers between devices: 27.2 us -> 15.7 us
  starting transfers between devices: 16.2 us -> 18.8 us
  Pallas kernels: 14 us -> 16.1 us
    ppermute x10 -> x13, waiting for transfers between devices: 27.2 us -> 7.06 us  [exchanged(): return lax.ppermute(array, 'attn', [(i, i ^ mask) for i in range(length)])]
    ppermute x2, waiting for transfers between devices: 0.01 us -> 8.61 us  [the longest x1 4.42 us: body(): arrived[0] = lax.ppermute(leave[0], 'attn', along)]
    ppermute x10 -> x13, starting transfers between devices: 15.6 us -> 18.3 us  [exchanged(): return lax.ppermute(array, 'attn', [(i, i ^ mask) for i in range(length)])]
    pallas_call x4 -> x9, Pallas kernels: 9.94 us -> 12 us  [the longest x3 6.64 us: attended(): pl.pallas_call(kernel, out_shape=attend_shapes(rows, heads)[:outs], in_sp...]
  transfers between devices with their start and end apart: 12 -> 15, of which waited for: 6 -> 7; matrix products, arithmetic and copies ran while one was open for 0% -> 0% of each run, Pallas kernels for 6% -> 16%
where the time goes in v3:
time: 51.8 us; the launch traced here: 51.7 us
  starting transfers between devices  18.8 us (36%)
  Pallas kernels  16.1 us (31%)
  waiting for transfers between devices  15.7 us (30%)
  between operations  0.84 us (2%)
    ppermute x13, starting transfers between devices, exchanged(): return lax.ppermute(array, 'attn', [(i, i ^ mask) for i in range(length)])  18.3 us
    ppermute x13, waiting for transfers between devices, exchanged(): return lax.ppermute(array, 'attn', [(i, i ^ mask) for i in range(length)])  7.06 us
    pallas_call x3, Pallas kernels, attended(): pl.pallas_call(kernel, out_shape=attend_shapes(rows, heads)[:outs], in_sp...  6.64 us
    ppermute x1, waiting for transfers between devices, body(): arrived[0] = lax.ppermute(leave[0], 'attn', along)  4.42 us
    ppermute x1, waiting for transfers between devices, body(): arrived[1] = lax.ppermute(leave[1], 'attn', along)  4.19 us
    pallas_call x1, Pallas kernels, staged(): pl.pallas_call(stage_kernel, out_shape=(jax.ShapeDtypeStruct((pages + 5,...  4.09 us
    pallas_call x2, Pallas kernels, expert_parts(): pl.pallas_call(expert_kernel, grid=(total // block,), out_shape=jax.Shape...  2.87 us
    pallas_call x1, Pallas kernels, finished(): pl.pallas_call(functools.partial(finish_kernel, len(owns)), out_shape=(ja...  2.35 us
  transfers between devices with their start and end apart: 15, of which 7 were waited for; matrix products, arithmetic and copies ran while one was open for 0% of the time, Pallas kernels for 16%

profile of v3, /device:TPU:0, one launch (start us, length us, event | category | flops | bytes accessed | tf_op | source)
XLA Modules:
  0.0 51.7 jit_solution(5387273498193583389)
XLA Ops:
  0.6 0.0 copy-start
  0.7 4.1 %shard_map.157 = (s32[13,12]{1,0:T(8,128)S(1)}, bf16[96,16,1024]{2,1,0:T(8,128)(2,1)S(1)}, bf16[96,16,1024]{2,1,0:T(8,128)(2,1)S(1)}, f32[576,128]{1,0:T(8,128)S...) custom-call(s32[8,12]{1,0:T(8,128)} %bitcast.15, s32[12]{0:T(128)} %lengths_at.1, ...), custom_call_target="tpu_custom_call" | custom-call | bytes 8388608 | tf_op jit(solution)/shard_map/pallas_call | solution.py:152
  4.8 0.5 collective-permute-start.1
  5.3 1.5 %shard_map.158 = (f32[12,48,128]{2,1,0:T(8,128)S(1)}, bf16[12,48,128]{2,1,0:T(8,128)(2,1)S(1)}, bf16[5,48,128]{2,1,0:T(8,128)(2,1)S(1)}, bf16[5,48,128]{2,1,0:T(8,128)(2,1)S(1)}) custom-call(s32[13,12]{1,0:T(8,128)S(1)} %get-tuple-element.27.plan, bf16[96,16,1024]{2,1,0:T(8,128)(2,1)S(1)} %get-tuple-element.28.key_pool, ...), custom_call_target="tpu_custom_call" | custom-call | flops 1048576 | bytes 65536 | tf_op jit(solution)/shard_map/pallas_call | solution.py:317
  6.7 4.5 %collective-permute-start = (bf16[5,48,128]{2,1,0:T(8,128)(2,1)S(1)}, bf16[5,48,128]{2,1,0:T(8,128)(2,1)S(1)}, u32[]{:S(2)}, u32[]{:S(2)}) collective-permute-start(bf16[5,48,128]{2,1,0:T(8,128)(2,1)S(1)} %get-tuple-element.38), channel_id=1, source_target_pairs={{0,8},{1,9},{2,10},{3,11},{4,12},{5,13},{6,14},{7,15},{8,0},{9,1},... | collective-permute-start | bytes 184328 | tf_op jit(solution)/shard_map/ppermute | solution.py:29
  11.2 1.5 %shard_map.159 = (f32[12,48,128]{2,1,0:T(8,128)S(1)}, bf16[12,48,128]{2,1,0:T(8,128)(2,1)S(1)}, bf16[5,48,128]{2,1,0:T(8,128)(2,1)S(1)}) custom-call(s32[13,12]{1,0:T(8,128)S(1)} %get-tuple-element.27.plan, bf16[96,16,1024]{2,1,0:T(8,128)(2,1)S(1)} %get-tuple-element.28.key_pool, bf16[96,16,1024]{2,1,0:T(8,128)(2,1)S(1)} %get-tuple-element.29.value_pool, ...), custom_call_target="tpu_custom_call" | custom-call | flops 1048576 | bytes 65536 | tf_op jit(solution)/shard_map/pallas_call | solution.py:317
  12.7 0.8 %collective-permute-done.away = bf16[5,48,128]{2,1,0:T(8,128)(2,1)S(1)} collective-permute-done((bf16[5,48,128]{2,1,0:T(8,128)(2,1)S(1)}, bf16[5,48,128]{2,1,0:T(8,128)(2,1)S(1)}, u32[]{:S(2)}, u32[]{:S(2)}) %collective-permute-start) | collective-permute-done | bytes 61472 | tf_op jit(solution)/shard_map/ppermute | solution.py:29
  13.5 4.4 %collective-permute-done.1.rest_0_.rest_4_ = bf16[2,128,1024]{2,1,0:T(8,128)(2,1)S(1)} collective-permute-done((bf16[2,128,1024]{2,1,0:T(8,128)(2,1)S(1)}, bf16[2,128,1024]{2,1,0:T(8,128)(2,1)S(1)}, u32[]{:S(2)}, u32[]{:S(2)}) %collective-permute-start.1) | collective-permute-done | bytes 524320 | tf_op jit(solution)/shard_map/ppermute | solution.py:543
  17.9 0.3 collective-permute-start.4
  18.2 3.6 %collective-permute-start.3 = (bf16[10,48,128]{2,1,0:T(8,128)(2,1)S(1)}, bf16[10,48,128]{2,1,0:T(8,128)(2,1)S(1)}, u32[]{:S(2)}, u32[]{:S(2)}) collective-permute-start(bf16[10,48,128]{2,1,0:T(8,128)(2,1)S(1)} %shard_map.160.rest_0_.refs_0_), channel_id=1, source_target_pairs={{0,4},{1,5},{2,6},{3,7},{4,0},{5,1},{6,2},{7,3},{8,12},{9,13},{10,... | collective-permute-start | bytes 368648 | tf_op jit(solution)/shard_map/ppermute | solution.py:29
  21.8 0.0 copy-start.2
  21.8 0.0 copy-start.3
  21.8 3.7 %shard_map.161 = (f32[12,48,128]{2,1,0:T(8,128)S(1)}, bf16[12,48,128]{2,1,0:T(8,128)(2,1)S(1)}) custom-call(s32[13,12]{1,0:T(8,128)S(1)} %get-tuple-element.27.plan, bf16[96,16,1024]{2,1,0:T(8,128)(2,1)S(1)} %get-tuple-element.28.key_pool, bf16[96,16,1024]{2,1,0:T(8,128)(2,1)S(1)} %get-tuple-element.29.value_pool, f32[576,128]{1,0:T(8,128)S(1)} %get-tuple-element.30.heads_q, ...), custom_call_target="tpu_custom_call" | custom-call | flops 1048576 | bytes 65536 | tf_op jit(solution)/shard_map/pallas_call | solution.py:317
  25.5 0.0 collective-permute-done.4.refs_3_
  25.5 2.2 %collective-permute-done.3.refs_2_ = bf16[10,48,128]{2,1,0:T(8,128)(2,1)S(1)} collective-permute-done((bf16[10,48,128]{2,1,0:T(8,128)(2,1)S(1)}, bf16[10,48,128]{2,1,0:T(8,128)(2,1)S(1)}, u32[]{:S(2)}, u32[]{:S(2)}) %collective-permute-start.3) | collective-permute-done | bytes 122912 | tf_op jit(solution)/shard_map/ppermute | solution.py:29
  27.8 0.1 collective-permute-start.5
  27.9 1.4 %shard_map.163.rest_0_.kept = f32[40,48,128]{2,1,0:T(8,128)S(1)} custom-call(bf16[40,48,128]{2,1,0:T(8,128)(2,1)S(1)} %shard_map.162.rows, bf16[6144,128]{1,0:T(8,128)(2,1)S(1)} %copy-done.1, bf16[6144,128]{1,0:T(8,128)(2,1)S(1)} %copy-done.2, bf16[128,6144]{1,0:T(8,128)(2,1)S(1)} %copy-done.3), custom_call_target="tpu_custom_call" | custom-call | flops 200000000 | bytes 4194304 | tf_op jit(solution)/shard_map/pallas_call | solution.py:362
  29.3 0.0 copy-start.4
  29.3 4.2 %collective-permute-done.6.rest_1_.rest_5_ = bf16[2,128,1024]{2,1,0:T(8,128)(2,1)S(1)} collective-permute-done((bf16[2,128,1024]{2,1,0:T(8,128)(2,1)S(1)}, bf16[2,128,1024]{2,1,0:T(8,128)(2,1)S(1)}, u32[]{:S(2)}, u32[]{:S(2)}) %collective-permute-start.6) | collective-permute-done | bytes 524320 | tf_op jit(solution)/shard_map/ppermute | solution.py:544
  33.5 1.4 %shard_map.164 = bf16[40,48,128]{2,1,0:T(8,128)(2,1)S(1)} custom-call(bf16[40,48,128]{2,1,0:T(8,128)(2,1)S(1)} %collective-permute-done.5.rows, bf16[6144,128]{1,0:T(8,128)(2,1)S(1)} %copy-done.1, bf16[6144,128]{1,0:T(8,128)(2,1)S(1)} %copy-done.2, bf16[128,6144]{1,0:T(8,128)(2,1)S(1)} %copy-done.3, f32[40,48,128]{2,1,0:T(8,128)S(1)} %shard_map.163.rest_0_.kept, ...), custom_call_target="tpu_custom_call" | custom-call | flops 200000000 | bytes 4194304 | tf_op jit(solution)/shard_map/pallas_call | solution.py:362
  35.0 0.1 collective-permute-start.7
  35.1 0.2 select_reduce_fusion.1
  35.3 1.6 %collective-permute-done.7.received = bf16[40,48,128]{2,1,0:T(8,128)(2,1)S(1)} collective-permute-done((bf16[40,48,128]{2,1,0:T(8,128)(2,1)S(1)}, bf16[40,48,128]{2,1,0:T(8,128)(2,1)S(1)}, u32[]{:S(2)}, u32[]{:S(2)}) %collective-permute-start.7) | collective-permute-done | bytes 491552 | tf_op jit(solution)/shard_map/ppermute | solution.py:29
  36.9 0.1 shard_map.165
  37.0 1.3 %collective-permute-start.8 = (bf16[5,48,128]{2,1,0:T(8,128)(2,1)S(1)}, bf16[5,48,128]{2,1,0:T(8,128)(2,1)S(1)}, u32[]{:S(2)}, u32[]{:S(2)}) collective-permute-start(bf16[5,48,128]{2,1,0:T(8,128)(2,1)S(1)} %get-tuple-element.44), channel_id=1, source_target_pairs={{0,2},{1,3},{2,0},{3,1},{4,6},{5,7},{6,4},{7,5},{8,10},{9,11},{10,... | collective-permute-start | bytes 184328 | tf_op jit(solution)/shard_map/ppermute | solution.py:29
  38.3 2.2 %collective-permute-start.10 = (bf16[5,48,128]{2,1,0:T(8,128)(2,1)S(1)}, bf16[5,48,128]{2,1,0:T(8,128)(2,1)S(1)}, u32[]{:S(2)}, u32[]{:S(2)}) collective-permute-start(bf16[5,48,128]{2,1,0:T(8,128)(2,1)S(1)} %get-tuple-element.46), channel_id=1, source_target_pairs={{0,6},{1,7},{2,4},{3,5},{4,2},{5,3},{6,0},{7,1},{8,14},{9,15},{10,... | collective-permute-start | bytes 184328 | tf_op jit(solution)/shard_map/ppermute | solution.py:29
  40.6 1.3 %collective-permute-start.12 = (bf16[5,48,128]{2,1,0:T(8,128)(2,1)S(1)}, bf16[5,48,128]{2,1,0:T(8,128)(2,1)S(1)}, u32[]{:S(2)}, u32[]{:S(2)}) collective-permute-start(bf16[5,48,128]{2,1,0:T(8,128)(2,1)S(1)} %get-tuple-element.48), channel_id=1, source_target_pairs={{0,2},{1,3},{2,0},{3,1},{4,6},{5,7},{6,4},{7,5},{8,10},{9,11},{10,... | collective-permute-start | bytes 184328 | tf_op jit(solution)/shard_map/ppermute | solution.py:29
  41.9 2.2 %collective-permute-start.14 = (bf16[5,48,128]{2,1,0:T(8,128)(2,1)S(1)}, bf16[5,48,128]{2,1,0:T(8,128)(2,1)S(1)}, u32[]{:S(2)}, u32[]{:S(2)}) collective-permute-start(bf16[5,48,128]{2,1,0:T(8,128)(2,1)S(1)} %get-tuple-element.50), channel_id=1, source_target_pairs={{0,6},{1,7},{2,4},{3,5},{4,2},{5,3},{6,0},{7,1},{8,14},{9,15},{10,... | collective-permute-start | bytes 184328 | tf_op jit(solution)/shard_map/ppermute | solution.py:29
  44.2 2.7 %collective-permute-start.11 = (bf16[5,48,128]{2,1,0:T(8,128)(2,1)S(1)}, bf16[5,48,128]{2,1,0:T(8,128)(2,1)S(1)}, u32[]{:S(2)}, u32[]{:S(2)}) collective-permute-start(bf16[5,48,128]{2,1,0:T(8,128)(2,1)S(1)} %add_convert_fusion), channel_id=1, source_target_pairs={{0,8},{1,9},{2,10},{3,11},{4,12},{5,13},{6,14},{7,15},{8,0},{9,1},... | collective-permute-start | bytes 184328 | tf_op jit(solution)/shard_map/ppermute | solution.py:29
  46.9 0.6 %collective-permute-done.14.rest_3_ = bf16[5,48,128]{2,1,0:T(8,128)(2,1)S(1)} collective-permute-done((bf16[5,48,128]{2,1,0:T(8,128)(2,1)S(1)}, bf16[5,48,128]{2,1,0:T(8,128)(2,1)S(1)}, u32[]{:S(2)}, u32[]{:S(2)}) %collective-permute-start.14) | collective-permute-done | bytes 61472 | tf_op jit(solution)/shard_map/ppermute | solution.py:29
  47.5 1.8 %collective-permute-done.11.away = bf16[5,48,128]{2,1,0:T(8,128)(2,1)S(1)} collective-permute-done((bf16[5,48,128]{2,1,0:T(8,128)(2,1)S(1)}, bf16[5,48,128]{2,1,0:T(8,128)(2,1)S(1)}, u32[]{:S(2)}, u32[]{:S(2)}) %collective-permute-start.11) | collective-permute-done | bytes 61472 | tf_op jit(solution)/shard_map/ppermute | solution.py:29
  49.3 2.3 %shard_map.166 = (bf16[12,6144]{1,0:T(8,128)(2,1)}, bf16[2,128,1024]{2,1,0:T(8,128)(2,1)}, bf16[2,128,1024]{2,1,0:T(8,128)(2,1)}) custom-call(s32[13,12]{1,0:T(8,128)S(1)} %get-tuple-element.27.plan, s32[1]{0:T(128)} %bitcast.2.mine, f32[2,12]{1,0:T(2,128)S(1)} %fusion.2.weights, f32[12,48,128]{2,1,0:T(8,128)S(1)} %get-tuple-element.41.refs_4_.state, ...), custom_call_target="tpu_custom_call" | custom-call | tf_op jit(solution)/shard_map/pallas_call | solution.py:482
  (23 shorter events, 0.1 us)
Async XLA Ops:
  0.6 34.4 %copy-start = (bf16[6144,8]{0,1:T(8,128)(2,1)S(1)}, bf16[6144,8]{0,1:T(8,128)(2,1)}, u32[]{:S(2)}) copy-start(bf16[6144,8]{0,1:T(8,128)(2,1)} %param.24) | copy-start | bytes 294916
  4.8 13.1 %collective-permute-start.1 = (bf16[2,128,1024]{2,1,0:T(8,128)(2,1)S(1)}, bf16[2,128,1024]{2,1,0:T(8,128)(2,1)S(1)}, u32[]{:S(2)}, u32[]{:S(2)}) collective-permute-start(bf16[2,128,1024]{2,1,0:T(8,128)(2,1)S(1)} %get-tuple-element.39), channel_id=1, source_target_pairs={{0,1},{1,2},{2,3},{3,4},{4,5},{5,6},{6,7},{7,8},{8,9},{9,10},{10,1... | collective-permute-start | bytes 1572872 | tf_op jit(solution)/shard_map/ppermute | solution.py:543
  6.7 6.7 %collective-permute-start = (bf16[5,48,128]{2,1,0:T(8,128)(2,1)S(1)}, bf16[5,48,128]{2,1,0:T(8,128)(2,1)S(1)}, u32[]{:S(2)}, u32[]{:S(2)}) collective-permute-start(bf16[5,48,128]{2,1,0:T(8,128)(2,1)S(1)} %get-tuple-element.38), channel_id=1, source_target_pairs={{0,8},{1,9},{2,10},{3,11},{4,12},{5,13},{6,14},{7,15},{8,0},{9,1},... | collective-permute-start | bytes 184328 | tf_op jit(solution)/shard_map/ppermute | solution.py:29
  17.9 7.6 %collective-permute-start.4 = (bf16[10,48,128]{2,1,0:T(8,128)(2,1)S(1)}, bf16[10,48,128]{2,1,0:T(8,128)(2,1)S(1)}, u32[]{:S(2)}, u32[]{:S(2)}) collective-permute-start(bf16[10,48,128]{2,1,0:T(8,128)(2,1)S(1)} %shard_map.160.rest_0_.refs_0_), channel_id=1, source_target_pairs={{0,6},{1,7},{2,4},{3,5},{4,2},{5,3},{6,0},{7,1},{8,14},{9,15},{10,... | collective-permute-start | bytes 368648 | tf_op jit(solution)/shard_map/ppermute | solution.py:29
  18.2 9.5 %collective-permute-start.3 = (bf16[10,48,128]{2,1,0:T(8,128)(2,1)S(1)}, bf16[10,48,128]{2,1,0:T(8,128)(2,1)S(1)}, u32[]{:S(2)}, u32[]{:S(2)}) collective-permute-start(bf16[10,48,128]{2,1,0:T(8,128)(2,1)S(1)} %shard_map.160.rest_0_.refs_0_), channel_id=1, source_target_pairs={{0,4},{1,5},{2,6},{3,7},{4,0},{5,1},{6,2},{7,3},{8,12},{9,13},{10,... | collective-permute-start | bytes 368648 | tf_op jit(solution)/shard_map/ppermute | solution.py:29
  21.8 6.0 %collective-permute-start.2 = (bf16[10,48,128]{2,1,0:T(8,128)(2,1)S(1)}, bf16[10,48,128]{2,1,0:T(8,128)(2,1)S(1)}, u32[]{:S(2)}, u32[]{:S(2)}) collective-permute-start(bf16[10,48,128]{2,1,0:T(8,128)(2,1)S(1)} %shard_map.160.rest_0_.refs_0_), channel_id=1, source_target_pairs={{0,2},{1,3},{2,0},{3,1},{4,6},{5,7},{6,4},{7,5},{8,10},{9,11},{10,... | collective-permute-start | bytes 368648 | tf_op jit(solution)/shard_map/ppermute | solution.py:29
  21.8 11.8 %collective-permute-start.6 = (bf16[2,128,1024]{2,1,0:T(8,128)(2,1)S(1)}, bf16[2,128,1024]{2,1,0:T(8,128)(2,1)S(1)}, u32[]{:S(2)}, u32[]{:S(2)}) collective-permute-start(bf16[2,128,1024]{2,1,0:T(8,128)(2,1)S(1)} %get-tuple-element.42), channel_id=1, source_target_pairs={{0,1},{1,2},{2,3},{3,4},{4,5},{5,6},{6,7},{7,8},{8,9},{9,10},{10,1... | collective-permute-start | bytes 1572872 | tf_op jit(solution)/shard_map/ppermute | solution.py:544
  21.8 6.1 %copy-start.1 = (bf16[6144,128]{1,0:T(8,128)(2,1)S(1)}, bf16[6144,128]{1,0:T(8,128)(2,1)}, u32[]{:S(2)}) copy-start(bf16[6144,128]{1,0:T(8,128)(2,1)} %w_gate.3) | copy-start | bytes 4718596
  21.8 6.1 %copy-start.2 = (bf16[6144,128]{1,0:T(8,128)(2,1)S(1)}, bf16[6144,128]{1,0:T(8,128)(2,1)}, u32[]{:S(2)}) copy-start(bf16[6144,128]{1,0:T(8,128)(2,1)} %w_up.3) | copy-start | bytes 4718596
  21.8 6.1 %copy-start.3 = (bf16[128,6144]{1,0:T(8,128)(2,1)S(1)}, bf16[128,6144]{1,0:T(8,128)(2,1)}, u32[]{:S(2)}) copy-start(bf16[128,6144]{1,0:T(8,128)(2,1)} %w_down.3) | copy-start | bytes 4718596
  27.8 5.8 %collective-permute-start.5 = (bf16[40,48,128]{2,1,0:T(8,128)(2,1)S(1)}, bf16[40,48,128]{2,1,0:T(8,128)(2,1)S(1)}, u32[]{:S(2)}, u32[]{:S(2)}) collective-permute-start(bf16[40,48,128]{2,1,0:T(8,128)(2,1)S(1)} %shard_map.162.rows), channel_id=1, source_target_pairs={{0,1},{1,0},{2,3},{3,2},{4,5},{5,4},{6,7},{7,6},{8,9},{9,8},{10,11... | collective-permute-start | bytes 1474568 | tf_op jit(solution)/shard_map/ppermute | solution.py:29
  29.3 5.7 %copy-start.4 = (s32[12,2]{0,1:T(2,128)S(1)}, s32[12,2]{0,1:T(2,128)}, u32[]{:S(2)}) copy-start(s32[12,2]{0,1:T(2,128)} %param.23) | copy-start | bytes 292
  35.0 1.9 %collective-permute-start.7 = (bf16[40,48,128]{2,1,0:T(8,128)(2,1)S(1)}, bf16[40,48,128]{2,1,0:T(8,128)(2,1)S(1)}, u32[]{:S(2)}, u32[]{:S(2)}) collective-permute-start(bf16[40,48,128]{2,1,0:T(8,128)(2,1)S(1)} %shard_map.164), channel_id=1, source_target_pairs={{0,1},{1,0},{2,3},{3,2},{4,5},{5,4},{6,7},{7,6},{8,9},{9,8},{10,11... | collective-permute-start | bytes 1474568 | tf_op jit(solution)/shard_map/ppermute | solution.py:29
  37.0 4.9 %collective-permute-start.8 = (bf16[5,48,128]{2,1,0:T(8,128)(2,1)S(1)}, bf16[5,48,128]{2,1,0:T(8,128)(2,1)S(1)}, u32[]{:S(2)}, u32[]{:S(2)}) collective-permute-start(bf16[5,48,128]{2,1,0:T(8,128)(2,1)S(1)} %get-tuple-element.44), channel_id=1, source_target_pairs={{0,2},{1,3},{2,0},{3,1},{4,6},{5,7},{6,4},{7,5},{8,10},{9,11},{10,... | collective-permute-start | bytes 184328 | tf_op jit(solution)/shard_map/ppermute | solution.py:29
  38.3 5.8 %collective-permute-start.9 = (bf16[5,48,128]{2,1,0:T(8,128)(2,1)S(1)}, bf16[5,48,128]{2,1,0:T(8,128)(2,1)S(1)}, u32[]{:S(2)}, u32[]{:S(2)}) collective-permute-start(bf16[5,48,128]{2,1,0:T(8,128)(2,1)S(1)} %get-tuple-element.45), channel_id=1, source_target_pairs={{0,4},{1,5},{2,6},{3,7},{4,0},{5,1},{6,2},{7,3},{8,12},{9,13},{10,... | collective-permute-start | bytes 184328 | tf_op jit(solution)/shard_map/ppermute | solution.py:29
  38.3 5.8 %collective-permute-start.10 = (bf16[5,48,128]{2,1,0:T(8,128)(2,1)S(1)}, bf16[5,48,128]{2,1,0:T(8,128)(2,1)S(1)}, u32[]{:S(2)}, u32[]{:S(2)}) collective-permute-start(bf16[5,48,128]{2,1,0:T(8,128)(2,1)S(1)} %get-tuple-element.46), channel_id=1, source_target_pairs={{0,6},{1,7},{2,4},{3,5},{4,2},{5,3},{6,0},{7,1},{8,14},{9,15},{10,... | collective-permute-start | bytes 184328 | tf_op jit(solution)/shard_map/ppermute | solution.py:29
  40.6 6.4 %collective-permute-start.12 = (bf16[5,48,128]{2,1,0:T(8,128)(2,1)S(1)}, bf16[5,48,128]{2,1,0:T(8,128)(2,1)S(1)}, u32[]{:S(2)}, u32[]{:S(2)}) collective-permute-start(bf16[5,48,128]{2,1,0:T(8,128)(2,1)S(1)} %get-tuple-element.48), channel_id=1, source_target_pairs={{0,2},{1,3},{2,0},{3,1},{4,6},{5,7},{6,4},{7,5},{8,10},{9,11},{10,... | collective-permute-start | bytes 184328 | tf_op jit(solution)/shard_map/ppermute | solution.py:29
  41.9 5.0 %collective-permute-start.13 = (bf16[5,48,128]{2,1,0:T(8,128)(2,1)S(1)}, bf16[5,48,128]{2,1,0:T(8,128)(2,1)S(1)}, u32[]{:S(2)}, u32[]{:S(2)}) collective-permute-start(bf16[5,48,128]{2,1,0:T(8,128)(2,1)S(1)} %get-tuple-element.49), channel_id=1, source_target_pairs={{0,4},{1,5},{2,6},{3,7},{4,0},{5,1},{6,2},{7,3},{8,12},{9,13},{10,... | collective-permute-start | bytes 184328 | tf_op jit(solution)/shard_map/ppermute | solution.py:29
  41.9 5.6 %collective-permute-start.14 = (bf16[5,48,128]{2,1,0:T(8,128)(2,1)S(1)}, bf16[5,48,128]{2,1,0:T(8,128)(2,1)S(1)}, u32[]{:S(2)}, u32[]{:S(2)}) collective-permute-start(bf16[5,48,128]{2,1,0:T(8,128)(2,1)S(1)} %get-tuple-element.50), channel_id=1, source_target_pairs={{0,6},{1,7},{2,4},{3,5},{4,2},{5,3},{6,0},{7,1},{8,14},{9,15},{10,... | collective-permute-start | bytes 184328 | tf_op jit(solution)/shard_map/ppermute | solution.py:29
  44.2 5.2 %collective-permute-start.11 = (bf16[5,48,128]{2,1,0:T(8,128)(2,1)S(1)}, bf16[5,48,128]{2,1,0:T(8,128)(2,1)S(1)}, u32[]{:S(2)}, u32[]{:S(2)}) collective-permute-start(bf16[5,48,128]{2,1,0:T(8,128)(2,1)S(1)} %add_convert_fusion), channel_id=1, source_target_pairs={{0,8},{1,9},{2,10},{3,11},{4,12},{5,13},{6,14},{7,15},{8,0},{9,1},... | collective-permute-start | bytes 184328 | tf_op jit(solution)/shard_map/ppermute | solution.py:29

commit v4 on v3

--- a/solution.py
+++ b/solution.py
@@ -131,7 +131,7 @@
 
 
 POOL_CUTS = 3
-GROUPS = ((0, 1), (2, 3))
+GROUPS = ((0,), (1, 2, 3))
 PLACES = [(g, group.index(i)) for i in range(sum(map(len, GROUPS)))
           for g, group in enumerate(GROUPS) if i in group]
 COST = 1 << 20
@@ -324,57 +324,67 @@
     )(plan, key_pool, value_pool, heads_q, heads_r, *before)
 
 
-def expert_rows(rows, w_gate, w_up, w_down, split, flat, back):
-    block, heads, _ = rows.shape
-    split[...] = rows[...].astype(F32).reshape(block * heads, HEAD_DIM)
-    for h in range(heads):
-        cols = slice(h * HEAD_DIM, (h + 1) * HEAD_DIM)
-        flat[:, cols] = split[pl.ds(h, block, stride=heads), :].astype(BF16)
-    gate = jnp.dot(flat[...], w_gate[...], preferred_element_type=F32)
-    up = jnp.dot(flat[...], w_up[...], preferred_element_type=F32)
-    hidden = (gate / (1.0 + jnp.exp(-gate)) * up).astype(BF16)
+def expert_kernel(block, rows, *rest):
+    weights, (sums, split, flat, back) = rest[:6], rest[-4:]
+    total, heads, _ = rows.shape
+    units = weights[0].shape[1]
+    deep = 4 * HEAD_DIM
     wide = 4
-    for first in range(0, heads, wide):
-        cols = slice(first * HEAD_DIM, (first + wide) * HEAD_DIM)
-        part = jnp.dot(hidden, w_down[:, cols], preferred_element_type=F32)
-        for h in range(wide):
-            back[pl.ds(first + h, block, stride=heads), :] = part[
-                :, h * HEAD_DIM:(h + 1) * HEAD_DIM
-            ]
-
-
-def expert_kernel(rows, w_gate, w_up, w_down, *rest):
-    sums, split, flat, back = rest[-4:]
-    expert_rows(rows, w_gate, w_up, w_down, split, flat, back)
-    sums[...] = back[...].reshape(sums.shape).astype(sums.dtype)
-
-
-def expert_parts(rows, w_gate, w_up, w_down, dtype, *after):
+
+    def step(i, carry):
+        here = pl.ds(i * block, block)
+        split[...] = rows[here].astype(F32).reshape(block * heads, HEAD_DIM)
+        for h in range(heads):
+            cols = slice(h * HEAD_DIM, (h + 1) * HEAD_DIM)
+            flat[:, cols] = split[pl.ds(h, block, stride=heads), :].astype(BF16)
+        both = jnp.zeros((block, 4 * units), F32)
+        for first in range(0, heads * HEAD_DIM, deep):
+            at = slice(first, first + deep)
+            both = both + jnp.dot(
+                flat[:, at], jnp.concatenate([w[at] for w in weights[:4]], axis=1),
+                preferred_element_type=F32,
+            )
+        gate, up = both[:, :2 * units], both[:, 2 * units:]
+        hidden = (gate / (1.0 + jnp.exp(-gate)) * up).astype(BF16)
+        for first in range(0, heads, wide):
+            cols = slice(first * HEAD_DIM, (first + wide) * HEAD_DIM)
+            part = jnp.dot(
+                hidden, jnp.concatenate([w[:, cols] for w in weights[4:6]], axis=0),
+                preferred_element_type=F32,
+            )
+            for h in range(wide):
+                back[pl.ds(first + h, block, stride=heads), :] = part[
+                    :, h * HEAD_DIM:(h + 1) * HEAD_DIM
+                ]
+        sums[here] = back[...].reshape(block, heads, HEAD_DIM).astype(BF16)
+        return carry
+
+    if total == block:
+        step(0, 0)
+    else:
+        lax.fori_loop(0, total // block, step, 0)
+
+
+def expert_parts(rows, weights, *after):
     total, heads, _ = rows.shape
     block = 8 * CAP
     if total % block:
         block = CAP
-    spec = pl.BlockSpec((block, heads, HEAD_DIM), lambda i: (i, 0, 0))
-
-    def fixed(array):
-        return pl.BlockSpec(array.shape, lambda i: (0, 0))
-
-    return pl.pallas_call(
-        expert_kernel,
-        grid=(total // block,),
-        out_shape=jax.ShapeDtypeStruct(rows.shape, dtype),
-        in_specs=[spec, fixed(w_gate), fixed(w_up), fixed(w_down)] + [ANY] * len(after),
-        out_specs=spec,
+    return pl.pallas_call(
+        functools.partial(expert_kernel, block),
+        out_shape=jax.ShapeDtypeStruct(rows.shape, BF16),
+        in_specs=[VMEM] * (1 + len(weights)) + [ANY] * len(after),
+        out_specs=VMEM,
         scratch_shapes=[
             pltpu.VMEM((block * heads, HEAD_DIM), F32),
             pltpu.VMEM((block, heads * HEAD_DIM), BF16),
             pltpu.VMEM((block * heads, HEAD_DIM), F32),
         ],
-        compiler_params=pltpu.CompilerParams(vmem_limit_bytes=24 << 20),
+        compiler_params=pltpu.CompilerParams(vmem_limit_bytes=8 << 20),
         cost_estimate=pl.CostEstimate(
-            flops=200_000_000, bytes_accessed=4 << 20, transcendentals=5120
+            flops=400_000_000, bytes_accessed=10 << 20, transcendentals=10240
         ),
-    )(rows, w_gate, w_up, w_down, *after)
+    )(rows, *weights, *after)
 
 
 def join_kernel(own, away, *rest):
@@ -423,27 +433,6 @@
         out_specs=VMEM,
         compiler_params=pltpu.CompilerParams(vmem_limit_bytes=24 << 20),
     )(*blocks, *after)
-
-
-def pair_sum_kernel(count, kept, received, *rest):
-    parts = rest[-2 * count:]
-    for i in range(count):
-        for side in range(2):
-            at = slice((2 * i + side) * CAP, (2 * i + side + 1) * CAP)
-            parts[side * count + i][...] = (kept[at] + received[at].astype(F32)).astype(BF16)
-
-
-def pair_sums(kept, received, *after):
-    count = kept.shape[0] // (2 * CAP)
-    part = jax.ShapeDtypeStruct((CAP,) + kept.shape[1:], BF16)
-    parts = pl.pallas_call(
-        functools.partial(pair_sum_kernel, count),
-        out_shape=(part,) * (2 * count),
-        in_specs=[VMEM, VMEM] + [ANY] * len(after),
-        out_specs=(VMEM,) * (2 * count),
-        compiler_params=pltpu.CompilerParams(vmem_limit_bytes=24 << 20),
-    )(kept, received, *after)
-    return parts[:count], parts[count:]
 
 
 def finish_kernel(count, plan, mine, weights, state, away, *rest):
@@ -547,14 +536,16 @@
     swapped = exchanged(away, swap)
     state, normed, own = attended(own_kernel, 3, COST, *held, state, normed, own)
     rows_here = joined(own, swapped, arrived[0])
+    others = [exchanged(w, 1) for w in (w_gate, w_up, w_down)]
     blocks = [rows_here] + [exchanged(rows_here, mask) for mask in masks]
-    state, normed = attended(rest_kernel, 2, COST, *held, state, normed, rows_here)
+    state, normed = attended(rest_kernel, 2, COST, *held, state, normed, rows_here, *others)
     mine_rows = gathered(blocks, state)
     weights = gate_weights(normed, router_weight, chosen)
-    other_rows = exchanged(mine_rows, 1)
-    kept = expert_parts(mine_rows, w_gate, w_up, w_down, F32)
-    given = expert_parts(other_rows, w_gate, w_up, w_down, BF16, kept, arrived[1])
-    own_parts, away_parts = pair_sums(kept, exchanged(given, 1))
+    sums = expert_parts(
+        mine_rows, [w for pair in zip((w_gate, w_up, w_down), others) for w in pair]
+    )
+    parts = [sums[i * CAP:(i + 1) * CAP] for i in range(2 * len(blocks))]
+    own_parts, away_parts = parts[0::2], parts[1::2]
     back = away_parts[0].astype(F32)
     for part, mask in zip(away_parts[1:], masks):
         back = back + exchanged(part, mask).astype(F32)

time: 51.8 us -> 47.5 us (0.917)
  waiting for transfers between devices: 15.7 us -> 10.2 us
  Pallas kernels: 16.1 us -> 17.5 us
    ppermute x1, waiting for transfers between devices: 4.19 us -> 0.01 us  [body(): arrived[1] = lax.ppermute(leave[1], 'attn', along)]
    ppermute x1, waiting for transfers between devices: 4.42 us -> 1.06 us  [body(): arrived[0] = lax.ppermute(leave[0], 'attn', along)]
    ppermute x13 -> x14, waiting for transfers between devices: 7.06 us -> 9.12 us  [exchanged(): return lax.ppermute(array, 'attn', [(i, i ^ mask) for i in range(length)])]
    pallas_call x3, Pallas kernels: 6.64 us -> 7.56 us  [attended(): pl.pallas_call(kernel, out_shape=attend_shapes(rows, heads)[:outs], in_sp...]
    pallas_call x3 -> x1, Pallas kernels: 2.95 us -> 3.48 us  [expert_parts(): pl.pallas_call(functools.partial(expert_kernel, block), out_shape=jax.Sha...]
    ppermute x13 -> x14, starting transfers between devices: 18.3 us -> 18.3 us  [exchanged(): return lax.ppermute(array, 'attn', [(i, i ^ mask) for i in range(length)])]
  transfers between devices with their start and end apart: 15 -> 16, of which waited for: 7 -> 9; matrix products, arithmetic and copies ran while one was open for 0% -> 1% of each run, Pallas kernels for 16% -> 32%
where the time goes in v4:
time: 47.5 us; the launch traced here: 47.3 us
  starting transfers between devices  18.5 us (39%)
  Pallas kernels  17.5 us (37%)
  waiting for transfers between devices  10.2 us (21%)
  between operations  0.81 us (2%)
    ppermute x14, starting transfers between devices, exchanged(): return lax.ppermute(array, 'attn', [(i, i ^ mask) for i in range(length)])  18.3 us
    ppermute x14, waiting for transfers between devices, exchanged(): return lax.ppermute(array, 'attn', [(i, i ^ mask) for i in range(length)])  9.12 us
    pallas_call x3, Pallas kernels, attended(): pl.pallas_call(kernel, out_shape=attend_shapes(rows, heads)[:outs], in_sp...  7.56 us
    pallas_call x1, Pallas kernels, staged(): pl.pallas_call(stage_kernel, out_shape=(jax.ShapeDtypeStruct((pages + 5,...  4.05 us
    pallas_call x1, Pallas kernels, expert_parts(): pl.pallas_call(functools.partial(expert_kernel, block), out_shape=jax.Sha...  3.48 us
    pallas_call x1, Pallas kernels, finished(): pl.pallas_call(functools.partial(finish_kernel, len(owns)), out_shape=(ja...  2.35 us
    ppermute x1, waiting for transfers between devices, body(): arrived[0] = lax.ppermute(leave[0], 'attn', along)  1.06 us
  transfers between devices with their start and end apart: 16, of which 9 were waited for; matrix products, arithmetic and copies ran while one was open for 1% of the time, Pallas kernels for 32%

profile of v4, /device:TPU:0, one launch (start us, length us, event | category | flops | bytes accessed | tf_op | source)
XLA Modules:
  0.0 47.3 jit_solution(14171638999463221596)
XLA Ops:
  0.6 0.0 copy-start
  0.6 0.5 %collective-permute-start.2 = (bf16[6144,128]{1,0:T(8,128)(2,1)}, bf16[6144,128]{1,0:T(8,128)(2,1)S(1)}, u32[]{:S(2)}, u32[]{:S(2)}) collective-permute-start(bf16[6144,128]{1,0:T(8,128)(2,1)} %rest_0_.1), channel_id=1, source_target_pairs={{0,1},{1,0},{2,3},{3,2},{4,5},{5,4},{6,7},{7,6},{8,9},{9,8},{10,11... | collective-permute-start | bytes 4718600 | tf_op jit(solution)/shard_map/ppermute | solution.py:29
  1.2 0.1 collective-permute-start.3
  1.2 0.4 collective-permute-start.4
  1.7 4.1 %shard_map.157 = (s32[13,12]{1,0:T(8,128)S(1)}, bf16[96,16,1024]{2,1,0:T(8,128)(2,1)S(1)}, bf16[96,16,1024]{2,1,0:T(8,128)(2,1)S(1)}, f32[576,128]{1,0:T(8,128)S...) custom-call(s32[8,12]{1,0:T(8,128)} %bitcast.15, s32[12]{0:T(128)} %lengths_at.1, ...), custom_call_target="tpu_custom_call" | custom-call | bytes 8388608 | tf_op jit(solution)/shard_map/pallas_call | solution.py:152
  5.7 0.1 collective-permute-start.1
  5.9 1.5 %shard_map.158 = (f32[12,48,128]{2,1,0:T(8,128)S(1)}, bf16[12,48,128]{2,1,0:T(8,128)(2,1)S(1)}, bf16[5,48,128]{2,1,0:T(8,128)(2,1)S(1)}, bf16[5,48,128]{2,1,0:T(8,128)(2,1)S(1)}) custom-call(s32[13,12]{1,0:T(8,128)S(1)} %get-tuple-element.19.plan, bf16[96,16,1024]{2,1,0:T(8,128)(2,1)S(1)} %get-tuple-element.20.key_pool, ...), custom_call_target="tpu_custom_call" | custom-call | flops 1048576 | bytes 65536 | tf_op jit(solution)/shard_map/pallas_call | solution.py:317
  7.4 4.9 %collective-permute-start = (bf16[5,48,128]{2,1,0:T(8,128)(2,1)S(1)}, bf16[5,48,128]{2,1,0:T(8,128)(2,1)S(1)}, u32[]{:S(2)}, u32[]{:S(2)}) collective-permute-start(bf16[5,48,128]{2,1,0:T(8,128)(2,1)S(1)} %get-tuple-element.30), channel_id=1, source_target_pairs={{0,8},{1,9},{2,10},{3,11},{4,12},{5,13},{6,14},{7,15},{8,0},{9,1},... | collective-permute-start | bytes 184328 | tf_op jit(solution)/shard_map/ppermute | solution.py:29
  12.2 2.2 %shard_map.159 = (f32[12,48,128]{2,1,0:T(8,128)S(1)}, bf16[12,48,128]{2,1,0:T(8,128)(2,1)S(1)}, bf16[5,48,128]{2,1,0:T(8,128)(2,1)S(1)}) custom-call(s32[13,12]{1,0:T(8,128)S(1)} %get-tuple-element.19.plan, bf16[96,16,1024]{2,1,0:T(8,128)(2,1)S(1)} %get-tuple-element.20.key_pool, bf16[96,16,1024]{2,1,0:T(8,128)(2,1)S(1)} %get-tuple-element.21.value_pool, ...), custom_call_target="tpu_custom_call" | custom-call | flops 1048576 | bytes 65536 | tf_op jit(solution)/shard_map/pallas_call | solution.py:317
  14.5 0.2 collective-permute-done.away
  14.6 1.1 %collective-permute-done.1.rest_0_.rest_4_ = bf16[1,128,1024]{2,1,0:T(8,128)(2,1)S(1)} collective-permute-done((bf16[1,128,1024]{2,1,0:T(8,128)(2,1)S(1)}, bf16[1,128,1024]{2,1,0:T(8,128)(2,1)S(1)}, u32[]{:S(2)}, u32[]{:S(2)}) %collective-permute-start.1) | collective-permute-done | bytes 262176 | tf_op jit(solution)/shard_map/ppermute | solution.py:532
  15.7 3.0 %collective-permute-start.5 = (bf16[10,48,128]{2,1,0:T(8,128)(2,1)S(1)}, bf16[10,48,128]{2,1,0:T(8,128)(2,1)S(1)}, u32[]{:S(2)}, u32[]{:S(2)}) collective-permute-start(bf16[10,48,128]{2,1,0:T(8,128)(2,1)S(1)} %shard_map.160.rest_0_.refs_0_), channel_id=1, source_target_pairs={{0,2},{1,3},{2,0},{3,1},{4,6},{5,7},{6,4},{7,5},{8,10},{9,11},{10,... | collective-permute-start | bytes 368648 | tf_op jit(solution)/shard_map/ppermute | solution.py:29
  18.7 1.5 %collective-permute-start.7 = (bf16[10,48,128]{2,1,0:T(8,128)(2,1)S(1)}, bf16[10,48,128]{2,1,0:T(8,128)(2,1)S(1)}, u32[]{:S(2)}, u32[]{:S(2)}) collective-permute-start(bf16[10,48,128]{2,1,0:T(8,128)(2,1)S(1)} %shard_map.160.rest_0_.refs_0_), channel_id=1, source_target_pairs={{0,6},{1,7},{2,4},{3,5},{4,2},{5,3},{6,0},{7,1},{8,14},{9,15},{10,... | collective-permute-start | bytes 368648 | tf_op jit(solution)/shard_map/ppermute | solution.py:29
  20.3 0.1 collective-permute-start.15
  20.4 3.9 %shard_map.161 = (f32[12,48,128]{2,1,0:T(8,128)S(1)}, bf16[12,48,128]{2,1,0:T(8,128)(2,1)S(1)}) custom-call(s32[13,12]{1,0:T(8,128)S(1)} %get-tuple-element.19.plan, bf16[96,16,1024]{2,1,0:T(8,128)(2,1)S(1)} %get-tuple-element.20.key_pool, bf16[96,16,1024]{2,1,0:T(8,128)(2,1)S(1)} %get-tuple-element.21.value_pool, f32[576,128]{1,0:T(8,128)S(1)} %get-tuple-element.22.heads_q, ...), custom_call_target="tpu_custom_call" | custom-call | flops 1048576 | bytes 65536 | tf_op jit(solution)/shard_map/pallas_call | solution.py:317
  24.3 0.7 %collective-permute-done.6.refs_2_ = bf16[10,48,128]{2,1,0:T(8,128)(2,1)S(1)} collective-permute-done((bf16[10,48,128]{2,1,0:T(8,128)(2,1)S(1)}, bf16[10,48,128]{2,1,0:T(8,128)(2,1)S(1)}, u32[]{:S(2)}, u32[]{:S(2)}) %collective-permute-start.6) | collective-permute-done | bytes 122912 | tf_op jit(solution)/shard_map/ppermute | solution.py:29
  25.0 1.4 %collective-permute-done.7.refs_3_ = bf16[10,48,128]{2,1,0:T(8,128)(2,1)S(1)} collective-permute-done((bf16[10,48,128]{2,1,0:T(8,128)(2,1)S(1)}, bf16[10,48,128]{2,1,0:T(8,128)(2,1)S(1)}, u32[]{:S(2)}, u32[]{:S(2)}) %collective-permute-start.7) | collective-permute-done | bytes 122912 | tf_op jit(solution)/shard_map/ppermute | solution.py:29
  26.4 3.5 %shard_map.163 = bf16[40,48,128]{2,1,0:T(8,128)(2,1)S(1)} custom-call(bf16[40,48,128]{2,1,0:T(8,128)(2,1)S(1)} %shard_map.162.rows, bf16[6144,128]{1,0:T(8,128)(2,1)S(1)} %copy-done.1, bf16[6144,128]{1,0:T(8,128)(2,1)S(1)} %collective-permute-done.2.rest_1_, bf16[6144,128]{1,0:T(8,128)(2,1)S(1)} %copy-done.2, ...), custom_call_target="tpu_custom_call" | custom-call | flops 400000000 | bytes 10485760 | tf_op jit(solution)/shard_map/pallas_call | solution.py:373
  30.0 1.4 %collective-permute-start.10 = (bf16[5,48,128]{2,1,0:T(8,128)(2,1)S(1)}, bf16[5,48,128]{2,1,0:T(8,128)(2,1)S(1)}, u32[]{:S(2)}, u32[]{:S(2)}) collective-permute-start(bf16[5,48,128]{2,1,0:T(8,128)(2,1)S(1)} %get-tuple-element.41), channel_id=1, source_target_pairs={{0,6},{1,7},{2,4},{3,5},{4,2},{5,3},{6,0},{7,1},{8,14},{9,15},{10,... | collective-permute-start | bytes 184328 | tf_op jit(solution)/shard_map/ppermute | solution.py:29
  31.4 1.7 %collective-permute-start.8 = (bf16[5,48,128]{2,1,0:T(8,128)(2,1)S(1)}, bf16[5,48,128]{2,1,0:T(8,128)(2,1)S(1)}, u32[]{:S(2)}, u32[]{:S(2)}) collective-permute-start(bf16[5,48,128]{2,1,0:T(8,128)(2,1)S(1)} %get-tuple-element.43), channel_id=1, source_target_pairs={{0,2},{1,3},{2,0},{3,1},{4,6},{5,7},{6,4},{7,5},{8,10},{9,11},{10,... | collective-permute-start | bytes 184328 | tf_op jit(solution)/shard_map/ppermute | solution.py:29
  33.0 0.5 collective-permute-start.9
  33.5 1.6 %collective-permute-start.12 = (bf16[5,48,128]{2,1,0:T(8,128)(2,1)S(1)}, bf16[5,48,128]{2,1,0:T(8,128)(2,1)S(1)}, u32[]{:S(2)}, u32[]{:S(2)}) collective-permute-start(bf16[5,48,128]{2,1,0:T(8,128)(2,1)S(1)} %get-tuple-element.39), channel_id=1, source_target_pairs={{0,2},{1,3},{2,0},{3,1},{4,6},{5,7},{6,4},{7,5},{8,10},{9,11},{10,... | collective-permute-start | bytes 184328 | tf_op jit(solution)/shard_map/ppermute | solution.py:29
  35.2 0.2 select_reduce_fusion.1
  35.4 1.6 %collective-permute-done.10 = bf16[5,48,128]{2,1,0:T(8,128)(2,1)S(1)} collective-permute-done((bf16[5,48,128]{2,1,0:T(8,128)(2,1)S(1)}, bf16[5,48,128]{2,1,0:T(8,128)(2,1)S(1)}, u32[]{:S(2)}, u32[]{:S(2)}) %collective-permute-start.10) | collective-permute-done | bytes 61472 | tf_op jit(solution)/shard_map/ppermute | solution.py:29
  36.9 0.4 collective-permute-start.13
  37.3 0.9 %collective-permute-done.8 = bf16[5,48,128]{2,1,0:T(8,128)(2,1)S(1)} collective-permute-done((bf16[5,48,128]{2,1,0:T(8,128)(2,1)S(1)}, bf16[5,48,128]{2,1,0:T(8,128)(2,1)S(1)}, u32[]{:S(2)}, u32[]{:S(2)}) %collective-permute-start.8) | collective-permute-done | bytes 61472 | tf_op jit(solution)/shard_map/ppermute | solution.py:29
  38.2 0.7 %collective-permute-start.14 = (bf16[5,48,128]{2,1,0:T(8,128)(2,1)S(1)}, bf16[5,48,128]{2,1,0:T(8,128)(2,1)S(1)}, u32[]{:S(2)}, u32[]{:S(2)}) collective-permute-start(bf16[5,48,128]{2,1,0:T(8,128)(2,1)S(1)} %get-tuple-element.37), channel_id=1, source_target_pairs={{0,6},{1,7},{2,4},{3,5},{4,2},{5,3},{6,0},{7,1},{8,14},{9,15},{10,... | collective-permute-start | bytes 184328 | tf_op jit(solution)/shard_map/ppermute | solution.py:29
  38.9 1.6 %collective-permute-start.11 = (bf16[5,48,128]{2,1,0:T(8,128)(2,1)S(1)}, bf16[5,48,128]{2,1,0:T(8,128)(2,1)S(1)}, u32[]{:S(2)}, u32[]{:S(2)}) collective-permute-start(bf16[5,48,128]{2,1,0:T(8,128)(2,1)S(1)} %add_convert_fusion), channel_id=1, source_target_pairs={{0,8},{1,9},{2,10},{3,11},{4,12},{5,13},{6,14},{7,15},{8,0},{9,1},... | collective-permute-start | bytes 184328 | tf_op jit(solution)/shard_map/ppermute | solution.py:29
  40.6 1.2 %collective-permute-done.13.rest_2_ = bf16[5,48,128]{2,1,0:T(8,128)(2,1)S(1)} collective-permute-done((bf16[5,48,128]{2,1,0:T(8,128)(2,1)S(1)}, bf16[5,48,128]{2,1,0:T(8,128)(2,1)S(1)}, u32[]{:S(2)}, u32[]{:S(2)}) %collective-permute-start.13) | collective-permute-done | bytes 61472 | tf_op jit(solution)/shard_map/ppermute | solution.py:29
  41.8 2.2 %collective-permute-done.14.rest_3_ = bf16[5,48,128]{2,1,0:T(8,128)(2,1)S(1)} collective-permute-done((bf16[5,48,128]{2,1,0:T(8,128)(2,1)S(1)}, bf16[5,48,128]{2,1,0:T(8,128)(2,1)S(1)}, u32[]{:S(2)}, u32[]{:S(2)}) %collective-permute-start.14) | collective-permute-done | bytes 61472 | tf_op jit(solution)/shard_map/ppermute | solution.py:29
  44.0 1.0 %collective-permute-done.11.away = bf16[5,48,128]{2,1,0:T(8,128)(2,1)S(1)} collective-permute-done((bf16[5,48,128]{2,1,0:T(8,128)(2,1)S(1)}, bf16[5,48,128]{2,1,0:T(8,128)(2,1)S(1)}, u32[]{:S(2)}, u32[]{:S(2)}) %collective-permute-start.11) | collective-permute-done | bytes 61472 | tf_op jit(solution)/shard_map/ppermute | solution.py:29
  45.0 2.3 %shard_map.164 = (bf16[12,6144]{1,0:T(8,128)(2,1)}, bf16[2,128,1024]{2,1,0:T(8,128)(2,1)}, bf16[2,128,1024]{2,1,0:T(8,128)(2,1)}) custom-call(s32[13,12]{1,0:T(8,128)S(1)} %get-tuple-element.19.plan, s32[1]{0:T(128)} %bitcast.2.mine, f32[2,12]{1,0:T(2,128)S(1)} %fusion.2.weights, f32[12,48,128]{2,1,0:T(8,128)S(1)} %get-tuple-element.33.refs_4_.state, ...), custom_call_target="tpu_custom_call" | custom-call | tf_op jit(solution)/shard_map/pallas_call | solution.py:471
  (24 shorter events, 0.2 us)
Async XLA Ops:
  0.6 34.5 %copy-start = (bf16[6144,8]{0,1:T(8,128)(2,1)S(1)}, bf16[6144,8]{0,1:T(8,128)(2,1)}, u32[]{:S(2)}) copy-start(bf16[6144,8]{0,1:T(8,128)(2,1)} %param.24) | copy-start | bytes 294916
  0.6 18.1 %collective-permute-start.2 = (bf16[6144,128]{1,0:T(8,128)(2,1)}, bf16[6144,128]{1,0:T(8,128)(2,1)S(1)}, u32[]{:S(2)}, u32[]{:S(2)}) collective-permute-start(bf16[6144,128]{1,0:T(8,128)(2,1)} %rest_0_.1), channel_id=1, source_target_pairs={{0,1},{1,0},{2,3},{3,2},{4,5},{5,4},{6,7},{7,6},{8,9},{9,8},{10,11... | collective-permute-start | bytes 4718600 | tf_op jit(solution)/shard_map/ppermute | solution.py:29
  1.2 19.1 %collective-permute-start.3 = (bf16[6144,128]{1,0:T(8,128)(2,1)}, bf16[6144,128]{1,0:T(8,128)(2,1)S(1)}, u32[]{:S(2)}, u32[]{:S(2)}) collective-permute-start(bf16[6144,128]{1,0:T(8,128)(2,1)} %rest_2_.1), channel_id=1, source_target_pairs={{0,1},{1,0},{2,3},{3,2},{4,5},{5,4},{6,7},{7,6},{8,9},{9,8},{10,11... | collective-permute-start | bytes 4718600 | tf_op jit(solution)/shard_map/ppermute | solution.py:29
  1.2 19.1 %collective-permute-start.4 = (bf16[128,6144]{1,0:T(8,128)(2,1)}, bf16[128,6144]{1,0:T(8,128)(2,1)}, u32[]{:S(2)}, u32[]{:S(2)}) collective-permute-start(bf16[128,6144]{1,0:T(8,128)(2,1)} %rest_4_.1), channel_id=1, source_target_pairs={{0,1},{1,0},{2,3},{3,2},{4,5},{5,4},{6,7},{7,6},{8,9},{9,8},{10,11... | collective-permute-start | bytes 4718600 | tf_op jit(solution)/shard_map/ppermute | solution.py:29
  5.7 10.0 %collective-permute-start.1 = (bf16[1,128,1024]{2,1,0:T(8,128)(2,1)S(1)}, bf16[1,128,1024]{2,1,0:T(8,128)(2,1)S(1)}, u32[]{:S(2)}, u32[]{:S(2)}) collective-permute-start(bf16[1,128,1024]{2,1,0:T(8,128)(2,1)S(1)} %get-tuple-element.31), channel_id=1, source_target_pairs={{0,1},{1,2},{2,3},{3,4},{4,5},{5,6},{6,7},{7,8},{8,9},{9,10},{10,1... | collective-permute-start | bytes 786440 | tf_op jit(solution)/shard_map/ppermute | solution.py:532
  7.4 7.3 %collective-permute-start = (bf16[5,48,128]{2,1,0:T(8,128)(2,1)S(1)}, bf16[5,48,128]{2,1,0:T(8,128)(2,1)S(1)}, u32[]{:S(2)}, u32[]{:S(2)}) collective-permute-start(bf16[5,48,128]{2,1,0:T(8,128)(2,1)S(1)} %get-tuple-element.30), channel_id=1, source_target_pairs={{0,8},{1,9},{2,10},{3,11},{4,12},{5,13},{6,14},{7,15},{8,0},{9,1},... | collective-permute-start | bytes 184328 | tf_op jit(solution)/shard_map/ppermute | solution.py:29
  12.2 8.1 %copy-start.4 = (s32[12,2]{0,1:T(2,128)S(1)}, s32[12,2]{0,1:T(2,128)}, u32[]{:S(2)}) copy-start(s32[12,2]{0,1:T(2,128)} %param.23) | copy-start | bytes 292
  15.7 8.6 %collective-permute-start.5 = (bf16[10,48,128]{2,1,0:T(8,128)(2,1)S(1)}, bf16[10,48,128]{2,1,0:T(8,128)(2,1)S(1)}, u32[]{:S(2)}, u32[]{:S(2)}) collective-permute-start(bf16[10,48,128]{2,1,0:T(8,128)(2,1)S(1)} %shard_map.160.rest_0_.refs_0_), channel_id=1, source_target_pairs={{0,2},{1,3},{2,0},{3,1},{4,6},{5,7},{6,4},{7,5},{8,10},{9,11},{10,... | collective-permute-start | bytes 368648 | tf_op jit(solution)/shard_map/ppermute | solution.py:29
  18.7 6.2 %collective-permute-start.6 = (bf16[10,48,128]{2,1,0:T(8,128)(2,1)S(1)}, bf16[10,48,128]{2,1,0:T(8,128)(2,1)S(1)}, u32[]{:S(2)}, u32[]{:S(2)}) collective-permute-start(bf16[10,48,128]{2,1,0:T(8,128)(2,1)S(1)} %shard_map.160.rest_0_.refs_0_), channel_id=1, source_target_pairs={{0,4},{1,5},{2,6},{3,7},{4,0},{5,1},{6,2},{7,3},{8,12},{9,13},{10,... | collective-permute-start | bytes 368648 | tf_op jit(solution)/shard_map/ppermute | solution.py:29
  18.7 7.6 %collective-permute-start.7 = (bf16[10,48,128]{2,1,0:T(8,128)(2,1)S(1)}, bf16[10,48,128]{2,1,0:T(8,128)(2,1)S(1)}, u32[]{:S(2)}, u32[]{:S(2)}) collective-permute-start(bf16[10,48,128]{2,1,0:T(8,128)(2,1)S(1)} %shard_map.160.rest_0_.refs_0_), channel_id=1, source_target_pairs={{0,6},{1,7},{2,4},{3,5},{4,2},{5,3},{6,0},{7,1},{8,14},{9,15},{10,... | collective-permute-start | bytes 368648 | tf_op jit(solution)/shard_map/ppermute | solution.py:29
  20.3 20.3 %collective-permute-start.15 = (bf16[3,128,1024]{2,1,0:T(8,128)(2,1)S(1)}, bf16[3,128,1024]{2,1,0:T(8,128)(2,1)S(1)}, u32[]{:S(2)}, u32[]{:S(2)}) collective-permute-start(bf16[3,128,1024]{2,1,0:T(8,128)(2,1)S(1)} %get-tuple-element.34), channel_id=1, source_target_pairs={{0,1},{1,2},{2,3},{3,4},{4,5},{5,6},{6,7},{7,8},{8,9},{9,10},{10,1... | collective-permute-start | bytes 2359304 | tf_op jit(solution)/shard_map/ppermute | solution.py:533
  20.4 6.0 %copy-start.1 = (bf16[6144,128]{1,0:T(8,128)(2,1)S(1)}, bf16[6144,128]{1,0:T(8,128)(2,1)}, u32[]{:S(2)}) copy-start(bf16[6144,128]{1,0:T(8,128)(2,1)} %rest_0_.1) | copy-start | bytes 4718596
  20.4 6.0 %copy-start.2 = (bf16[6144,128]{1,0:T(8,128)(2,1)S(1)}, bf16[6144,128]{1,0:T(8,128)(2,1)}, u32[]{:S(2)}) copy-start(bf16[6144,128]{1,0:T(8,128)(2,1)} %rest_2_.1) | copy-start | bytes 4718596
  20.4 6.0 %copy-start.3 = (bf16[128,6144]{1,0:T(8,128)(2,1)S(1)}, bf16[128,6144]{1,0:T(8,128)(2,1)}, u32[]{:S(2)}) copy-start(bf16[128,6144]{1,0:T(8,128)(2,1)} %rest_4_.1) | copy-start | bytes 4718596
  30.0 7.0 %collective-permute-start.10 = (bf16[5,48,128]{2,1,0:T(8,128)(2,1)S(1)}, bf16[5,48,128]{2,1,0:T(8,128)(2,1)S(1)}, u32[]{:S(2)}, u32[]{:S(2)}) collective-permute-start(bf16[5,48,128]{2,1,0:T(8,128)(2,1)S(1)} %get-tuple-element.41), channel_id=1, source_target_pairs={{0,6},{1,7},{2,4},{3,5},{4,2},{5,3},{6,0},{7,1},{8,14},{9,15},{10,... | collective-permute-start | bytes 184328 | tf_op jit(solution)/shard_map/ppermute | solution.py:29
  31.4 6.8 %collective-permute-start.8 = (bf16[5,48,128]{2,1,0:T(8,128)(2,1)S(1)}, bf16[5,48,128]{2,1,0:T(8,128)(2,1)S(1)}, u32[]{:S(2)}, u32[]{:S(2)}) collective-permute-start(bf16[5,48,128]{2,1,0:T(8,128)(2,1)S(1)} %get-tuple-element.43), channel_id=1, source_target_pairs={{0,2},{1,3},{2,0},{3,1},{4,6},{5,7},{6,4},{7,5},{8,10},{9,11},{10,... | collective-permute-start | bytes 184328 | tf_op jit(solution)/shard_map/ppermute | solution.py:29
  33.0 5.8 %collective-permute-start.9 = (bf16[5,48,128]{2,1,0:T(8,128)(2,1)S(1)}, bf16[5,48,128]{2,1,0:T(8,128)(2,1)S(1)}, u32[]{:S(2)}, u32[]{:S(2)}) collective-permute-start(bf16[5,48,128]{2,1,0:T(8,128)(2,1)S(1)} %get-tuple-element.42), channel_id=1, source_target_pairs={{0,4},{1,5},{2,6},{3,7},{4,0},{5,1},{6,2},{7,3},{8,12},{9,13},{10,... | collective-permute-start | bytes 184328 | tf_op jit(solution)/shard_map/ppermute | solution.py:29
  33.5 7.1 %collective-permute-start.12 = (bf16[5,48,128]{2,1,0:T(8,128)(2,1)S(1)}, bf16[5,48,128]{2,1,0:T(8,128)(2,1)S(1)}, u32[]{:S(2)}, u32[]{:S(2)}) collective-permute-start(bf16[5,48,128]{2,1,0:T(8,128)(2,1)S(1)} %get-tuple-element.39), channel_id=1, source_target_pairs={{0,2},{1,3},{2,0},{3,1},{4,6},{5,7},{6,4},{7,5},{8,10},{9,11},{10,... | collective-permute-start | bytes 184328 | tf_op jit(solution)/shard_map/ppermute | solution.py:29
  36.9 4.9 %collective-permute-start.13 = (bf16[5,48,128]{2,1,0:T(8,128)(2,1)S(1)}, bf16[5,48,128]{2,1,0:T(8,128)(2,1)S(1)}, u32[]{:S(2)}, u32[]{:S(2)}) collective-permute-start(bf16[5,48,128]{2,1,0:T(8,128)(2,1)S(1)} %get-tuple-element.38), channel_id=1, source_target_pairs={{0,4},{1,5},{2,6},{3,7},{4,0},{5,1},{6,2},{7,3},{8,12},{9,13},{10,... | collective-permute-start | bytes 184328 | tf_op jit(solution)/shard_map/ppermute | solution.py:29
  38.2 5.8 %collective-permute-start.14 = (bf16[5,48,128]{2,1,0:T(8,128)(2,1)S(1)}, bf16[5,48,128]{2,1,0:T(8,128)(2,1)S(1)}, u32[]{:S(2)}, u32[]{:S(2)}) collective-permute-start(bf16[5,48,128]{2,1,0:T(8,128)(2,1)S(1)} %get-tuple-element.37), channel_id=1, source_target_pairs={{0,6},{1,7},{2,4},{3,5},{4,2},{5,3},{6,0},{7,1},{8,14},{9,15},{10,... | collective-permute-start | bytes 184328 | tf_op jit(solution)/shard_map/ppermute | solution.py:29
  38.9 6.0 %collective-permute-start.11 = (bf16[5,48,128]{2,1,0:T(8,128)(2,1)S(1)}, bf16[5,48,128]{2,1,0:T(8,128)(2,1)S(1)}, u32[]{:S(2)}, u32[]{:S(2)}) collective-permute-start(bf16[5,48,128]{2,1,0:T(8,128)(2,1)S(1)} %add_convert_fusion), channel_id=1, source_target_pairs={{0,8},{1,9},{2,10},{3,11},{4,12},{5,13},{6,14},{7,15},{8,0},{9,1},... | collective-permute-start | bytes 184328 | tf_op jit(solution)/shard_map/ppermute | solution.py:29

commit v5 on v4

--- a/solution.py
+++ b/solution.py
@@ -95,8 +95,7 @@
     ]
     middle = taken_away
     behind = taken_away + sum(only_own)
-    for bound, count in enumerate((taken_away, behind)):
-        plan[pages + 4, bound] = (count + 1) // 2
+    plan[pages + 4, 0] = behind
     for r in range(rows):
         is_away = away_slots[r] >= 0
         is_own = only_own[r] == 1
@@ -179,7 +178,7 @@
       *[in_hbm(a) for a in (queries, residual, new_keys, new_values, key_pool, value_pool)])
 
 
-def attend_pair(plan, pair, key_pool, value_pool, heads_q, heads_r, state_out, normed_out):
+def attend_some(plan, places, key_pool, value_pool, heads_q, heads_r, state_out, normed_out):
     page = key_pool.shape[1]
     kv_heads = key_pool.shape[2] // HEAD_DIM
     rows, heads, _ = state_out.shape
@@ -189,9 +188,9 @@
     head_of = lax.broadcasted_iota(jnp.int32, (heads, HEAD_DIM), 0)
     at_of = lax.broadcasted_iota(jnp.int32, (heads, positions), 1)
     in_group = [(head_of >= g * group) & (head_of < (g + 1) * group) for g in range(kv_heads)]
-    both = [plan[pages + 3, 2 * pair + i] for i in range(2)]
-    starts = [pl.multiple_of(r * heads, 8) for r in both]
-    numbers = [[plan[p, r] for p in range(pages)] for r in both]
+    some = [plan[pages + 3, place] for place in places]
+    starts = [pl.multiple_of(r * heads, 8) for r in some]
+    numbers = [[plan[p, r] for p in range(pages)] for r in some]
     queries = [heads_q[pl.ds(start, heads), :] for start in starts]
     spread = [
         jnp.concatenate(
@@ -206,7 +205,7 @@
         ) * (1.0 / math.sqrt(HEAD_DIM))
         for rows_q, number in zip(spread, numbers)
     ]
-    visible = [at_of <= plan[pages, r] for r in both]
+    visible = [at_of <= plan[pages, r] for r in some]
     scores = [jnp.where(seen, score, -jnp.inf) for seen, score in zip(visible, scores)]
     highest = [jnp.max(score, axis=1, keepdims=True) for score in scores]
     exponent = [
@@ -236,10 +235,10 @@
         (state * lax.rsqrt(square / (heads * HEAD_DIM) + 1e-05)).astype(BF16)
         for state, square in zip(states, squares)
     ]
-    for r, state, rows_n in zip(both, states, normed):
+    for r, state, rows_n in zip(some, states, normed):
         state_out[r] = state
         normed_out[r] = rows_n
-    return both, normed
+    return some, normed
 
 
 def away_kernel(plan, key_pool, value_pool, heads_q, heads_r,
@@ -247,22 +246,16 @@
     pages = plan.shape[0] - 5
     own_out[...] = jnp.zeros_like(own_out)
     away_out[...] = jnp.zeros_like(away_out)
-
-    def step(pair, carry):
-        both, normed = attend_pair(
-            plan, pair, key_pool, value_pool, heads_q, heads_r, state_out, normed_out
-        )
-        for r, rows_n in zip(both, normed):
-            for row, out in ((pages + 1, own_out), (pages + 2, away_out)):
-                slot = plan[row, r]
-
-                @pl.when(slot >= 0)
-                def _():
-                    out[jnp.clip(slot, 0, CAP - 1)] = rows_n
-
-        return carry
-
-    lax.fori_loop(0, plan[pages + 4, 0], step, 0)
+    some, normed = attend_some(
+        plan, range(CAP), key_pool, value_pool, heads_q, heads_r, state_out, normed_out
+    )
+    for r, rows_n in zip(some, normed):
+        for row, out in ((pages + 1, own_out), (pages + 2, away_out)):
+            slot = plan[row, r]
+
+            @pl.when(slot >= 0)
+            def _():
+                out[jnp.clip(slot, 0, CAP - 1)] = rows_n
 
 
 def own_kernel(plan, key_pool, value_pool, heads_q, heads_r, state_in, normed_in, own_in,
@@ -271,34 +264,15 @@
     state_out[...] = state_in[...]
     normed_out[...] = normed_in[...]
     own_out[...] = own_in[...]
-
-    def step(pair, carry):
-        both, normed = attend_pair(
-            plan, pair, key_pool, value_pool, heads_q, heads_r, state_out, normed_out
-        )
-        for r, rows_n in zip(both, normed):
-            slot = plan[pages + 1, r]
-
-            @pl.when(slot >= 0)
-            def _():
-                own_out[jnp.clip(slot, 0, CAP - 1)] = rows_n
-
-        return carry
-
-    lax.fori_loop(plan[pages + 4, 0], plan[pages + 4, 1], step, 0)
-
-
-def rest_kernel(plan, key_pool, value_pool, heads_q, heads_r, state_in, normed_in, *rest):
-    state_out, normed_out = rest[-2:]
-    pages = plan.shape[0] - 5
-    state_out[...] = state_in[...]
-    normed_out[...] = normed_in[...]
-
-    def step(pair, carry):
-        attend_pair(plan, pair, key_pool, value_pool, heads_q, heads_r, state_out, normed_out)
-        return carry
-
-    lax.fori_loop(plan[pages + 4, 1], state_out.shape[0] // 2, step, 0)
+    some, normed = attend_some(
+        plan, range(CAP, state_out.shape[0]), key_pool, value_pool, heads_q, heads_r, state_out, normed_out
+    )
+    for r, rows_n in zip(some, normed):
+        slot = plan[pages + 1, r]
+
+        @pl.when(slot >= 0)
+        def _():
+            own_out[jnp.clip(slot, 0, CAP - 1)] = rows_n
 
 
 def attend_shapes(rows, heads):
@@ -403,18 +377,20 @@
     )(own, away, *after)
 
 
-def hold_kernel(array, after, copy):
-    copy[...] = array[...]
-
-
-def held_back(array, after):
-    return pl.pallas_call(
-        hold_kernel,
-        out_shape=jax.ShapeDtypeStruct(array.shape, array.dtype),
-        in_specs=[VMEM, ANY],
-        out_specs=VMEM,
-        compiler_params=pltpu.CompilerParams(vmem_limit_bytes=4 << 20),
-    )(array, after)
+def hold_kernel(count, *refs):
+    for array, copy in zip(refs[:count], refs[-count:]):
+        copy[...] = array[...]
+
+
+def held_back(arrays, *after):
+    count = len(arrays)
+    return pl.pallas_call(
+        functools.partial(hold_kernel, count),
+        out_shape=tuple(jax.ShapeDtypeStruct(a.shape, a.dtype) for a in arrays),
+        in_specs=[VMEM] * count + [ANY] * len(after),
+        out_specs=(VMEM,) * count,
+        compiler_params=pltpu.CompilerParams(vmem_limit_bytes=24 << 20),
+    )(*arrays, *after)
 
 
 def gather_kernel(count, *refs):
@@ -437,15 +413,7 @@
 
 def finish_kernel(count, plan, mine, weights, state, away, *rest):
     owns, rest = rest[:count], rest[count:]
-    arrived, (mixed, moved_keys, moved_values, rows_split, sems) = rest[:-5], rest[-5:]
-    moves = moved_keys.shape[0]
-    targets = [moved.at[m] for moved in (moved_keys, moved_values) for m in range(moves)]
-    copies = [
-        pltpu.make_async_copy(arrived[group].at[place], target, sems.at[i])
-        for i, ((group, place), target) in enumerate(zip(PLACES, targets))
-    ]
-    for copy in copies:
-        copy.start()
+    mixed, rows_split = rest[-2:]
     rows, heads, _ = state.shape
     pages = plan.shape[0] - 5
     expert = mine[0]
@@ -461,28 +429,44 @@
         mixed[:, h * HEAD_DIM:(h + 1) * HEAD_DIM] = rows_split[
             pl.ds(h, rows, stride=heads), :
         ].astype(BF16)
+
+
+def finished(plan, mine, weights, state, away, owns, *after):
+    rows, heads, _ = state.shape
+    return pl.pallas_call(
+        functools.partial(finish_kernel, len(owns)),
+        out_shape=jax.ShapeDtypeStruct((rows, heads * HEAD_DIM), BF16),
+        in_specs=[SMEM] * 3 + [VMEM] * (2 + len(owns)) + [ANY] * len(after),
+        out_specs=VMEM,
+        scratch_shapes=[pltpu.VMEM((rows * heads, HEAD_DIM), F32)],
+        compiler_params=pltpu.CompilerParams(vmem_limit_bytes=8 << 20),
+    )(plan, mine, weights, state, away, *owns, *after)
+
+
+def deliver_kernel(count, *refs):
+    arrived, (moved_keys, moved_values, sems) = refs[:count], refs[-3:]
+    moves = moved_keys.shape[0]
+    targets = [moved.at[m] for moved in (moved_keys, moved_values) for m in range(moves)]
+    copies = [
+        pltpu.make_async_copy(arrived[group].at[place], target, sems.at[i])
+        for i, ((group, place), target) in enumerate(zip(PLACES, targets))
+    ]
+    for copy in copies:
+        copy.start()
     for copy in copies:
         copy.wait()
 
 
-def finished(plan, mine, weights, state, away, owns, arrived):
-    rows, heads, _ = state.shape
+def delivered(arrived, *after):
     moved = jax.ShapeDtypeStruct((len(PLACES) // 2,) + arrived[0].shape[1:], BF16)
     return pl.pallas_call(
-        functools.partial(finish_kernel, len(owns)),
-        out_shape=(
-            jax.ShapeDtypeStruct((rows, heads * HEAD_DIM), BF16),
-            moved,
-            moved,
-        ),
-        in_specs=[SMEM] * 3 + [VMEM] * (2 + len(owns)) + [ANY] * len(arrived),
-        out_specs=(VMEM, HBM, HBM),
-        scratch_shapes=[
-            pltpu.VMEM((rows * heads, HEAD_DIM), F32),
-            pltpu.SemaphoreType.DMA((len(PLACES),)),
-        ],
-        compiler_params=pltpu.CompilerParams(vmem_limit_bytes=8 << 20),
-    )(plan, mine, weights, state, away, *owns, *arrived)
+        functools.partial(deliver_kernel, len(arrived)),
+        out_shape=(moved, moved),
+        in_specs=[ANY] * (len(arrived) + len(after)),
+        out_specs=(HBM, HBM),
+        scratch_shapes=[pltpu.SemaphoreType.DMA((len(PLACES),))],
+        compiler_params=pltpu.CompilerParams(vmem_limit_bytes=4 << 20),
+    )(*arrived, *after)
 
 
 def gate_weights(normed, router_weight, chosen):
@@ -538,8 +522,8 @@
     rows_here = joined(own, swapped, arrived[0])
     others = [exchanged(w, 1) for w in (w_gate, w_up, w_down)]
     blocks = [rows_here] + [exchanged(rows_here, mask) for mask in masks]
-    state, normed = attended(rest_kernel, 2, COST, *held, state, normed, rows_here, *others)
-    mine_rows = gathered(blocks, state)
+    normed, = held_back([normed], rows_here, *others)
+    mine_rows = gathered(blocks, normed)
     weights = gate_weights(normed, router_weight, chosen)
     sums = expert_parts(
         mine_rows, [w for pair in zip((w_gate, w_up, w_down), others) for w in pair]
@@ -552,9 +536,8 @@
     own_sums = [own_parts[0]]
     own_sums += [exchanged(part, mask) for part, mask in zip(own_parts[1:], masks)]
     away_sums = exchanged(back.astype(BF16), swap)
-    mixed, moved_keys, moved_values = finished(
-        plan, mine, weights, state, away_sums, own_sums, arrived
-    )
+    moved_keys, moved_values = delivered(arrived, back)
+    mixed = finished(plan, mine, weights, state, away_sums, own_sums, in_hbm(moved_keys))
     return (mixed, moved_keys, moved_values)
 
 

time: 47.5 us -> 46.6 us (0.981)
  waiting for transfers between devices: 10.2 us -> 13.8 us
  Pallas kernels: 17.5 us -> 14 us
  starting transfers between devices: 18.5 us -> 17.6 us
    pallas_call x3 -> x2, Pallas kernels: 7.56 us -> 3.83 us  [attended(): pl.pallas_call(kernel, out_shape=attend_shapes(rows, heads)[:outs], in_sp...]
    ppermute x14, waiting for transfers between devices: 9.12 us -> 12.4 us  [exchanged(): return lax.ppermute(array, 'attn', [(i, i ^ mask) for i in range(length)])]
    ppermute x14, starting transfers between devices: 18.3 us -> 17.4 us  [exchanged(): return lax.ppermute(array, 'attn', [(i, i ^ mask) for i in range(length)])]
    pallas_call x1 -> x3, Pallas kernels: 2.35 us -> 2.59 us  [the longest x1 1.58 us: finished(): pl.pallas_call(functools.partial(finish_kernel, len(owns)), out_shape=jax...]
  transfers between devices with their start and end apart: 16 -> 16, of which waited for: 9 -> 10; matrix products, arithmetic and copies ran while one was open for 1% -> 1% of each run, Pallas kernels for 32% -> 27%
where the time goes in v5:
time: 46.6 us; the launch traced here: 46.5 us
  starting transfers between devices  17.6 us (38%)
  Pallas kernels  14 us (30%)
  waiting for transfers between devices  13.8 us (30%)
  between operations  0.81 us (2%)
    ppermute x14, starting transfers between devices, exchanged(): return lax.ppermute(array, 'attn', [(i, i ^ mask) for i in range(length)])  17.4 us
    ppermute x14, waiting for transfers between devices, exchanged(): return lax.ppermute(array, 'attn', [(i, i ^ mask) for i in range(length)])  12.4 us
    pallas_call x1, Pallas kernels, staged(): pl.pallas_call(stage_kernel, out_shape=(jax.ShapeDtypeStruct((pages + 5,...  4.05 us
    pallas_call x2, Pallas kernels, attended(): pl.pallas_call(kernel, out_shape=attend_shapes(rows, heads)[:outs], in_sp...  3.83 us
    pallas_call x1, Pallas kernels, expert_parts(): pl.pallas_call(functools.partial(expert_kernel, block), out_shape=jax.Sha...  3.46 us
    pallas_call x1, Pallas kernels, finished(): pl.pallas_call(functools.partial(finish_kernel, len(owns)), out_shape=jax...  1.58 us
    ppermute x1, waiting for transfers between devices, body(): arrived[0] = lax.ppermute(leave[0], 'attn', along)  1.46 us
    pallas_call x1, Pallas kernels, delivered(): pl.pallas_call(functools.partial(deliver_kernel, len(arrived)), out_shape...  1 us
  transfers between devices with their start and end apart: 16, of which 10 were waited for; matrix products, arithmetic and copies ran while one was open for 1% of the time, Pallas kernels for 27%

profile of v5, /device:TPU:0, one launch (start us, length us, event | category | flops | bytes accessed | tf_op | source)
XLA Modules:
  0.0 46.5 jit_solution(12189469168180590839)
XLA Ops:
  0.6 0.0 copy-start
  0.6 0.5 %collective-permute-start.2 = (bf16[6144,128]{1,0:T(8,128)(2,1)}, bf16[6144,128]{1,0:T(8,128)(2,1)S(1)}, u32[]{:S(2)}, u32[]{:S(2)}) collective-permute-start(bf16[6144,128]{1,0:T(8,128)(2,1)} %rest_0_.1), channel_id=1, source_target_pairs={{0,1},{1,0},{2,3},{3,2},{4,5},{5,4},{6,7},{7,6},{8,9},{9,8},{10,11... | collective-permute-start | bytes 4718600 | tf_op jit(solution)/shard_map/ppermute | solution.py:29
  1.2 0.1 collective-permute-start.3
  1.2 0.4 collective-permute-start.4
  1.7 4.1 %shard_map.157 = (s32[13,12]{1,0:T(8,128)S(1)}, bf16[96,16,1024]{2,1,0:T(8,128)(2,1)S(1)}, bf16[96,16,1024]{2,1,0:T(8,128)(2,1)S(1)}, f32[576,128]{1,0:T(8,128)S...) custom-call(s32[8,12]{1,0:T(8,128)} %bitcast.15, s32[12]{0:T(128)} %lengths_at.1, ...), custom_call_target="tpu_custom_call" | custom-call | bytes 8388608 | tf_op jit(solution)/shard_map/pallas_call | solution.py:151
  5.7 0.1 collective-permute-start.1
  5.9 1.8 %shard_map.158 = (f32[12,48,128]{2,1,0:T(8,128)S(1)}, bf16[12,48,128]{2,1,0:T(8,128)(2,1)S(1)}, bf16[5,48,128]{2,1,0:T(8,128)(2,1)S(1)}, bf16[5,48,128]{2,1,0:T(8,128)(2,1)S(1)}) custom-call(s32[13,12]{1,0:T(8,128)S(1)} %get-tuple-element.19.plan, bf16[96,16,1024]{2,1,0:T(8,128)(2,1)S(1)} %get-tuple-element.20.key_pool, ...), custom_call_target="tpu_custom_call" | custom-call | flops 1048576 | bytes 65536 | tf_op jit(solution)/shard_map/pallas_call | solution.py:291
  7.7 4.1 %collective-permute-start = (bf16[5,48,128]{2,1,0:T(8,128)(2,1)S(1)}, bf16[5,48,128]{2,1,0:T(8,128)(2,1)S(1)}, u32[]{:S(2)}, u32[]{:S(2)}) collective-permute-start(bf16[5,48,128]{2,1,0:T(8,128)(2,1)S(1)} %get-tuple-element.29), channel_id=1, source_target_pairs={{0,8},{1,9},{2,10},{3,11},{4,12},{5,13},{6,14},{7,15},{8,0},{9,1},... | collective-permute-start | bytes 184328 | tf_op jit(solution)/shard_map/ppermute | solution.py:29
  11.8 2.0 %shard_map.159 = (f32[12,48,128]{2,1,0:T(8,128)S(1)}, bf16[12,48,128]{2,1,0:T(8,128)(2,1)S(1)}, bf16[5,48,128]{2,1,0:T(8,128)(2,1)S(1)}) custom-call(s32[13,12]{1,0:T(8,128)S(1)} %get-tuple-element.19.plan, bf16[96,16,1024]{2,1,0:T(8,128)(2,1)S(1)} %get-tuple-element.20.key_pool, bf16[96,16,1024]{2,1,0:T(8,128)(2,1)S(1)} %get-tuple-element.21.value_pool, ...), custom_call_target="tpu_custom_call" | custom-call | flops 1048576 | bytes 65536 | tf_op jit(solution)/shard_map/pallas_call | solution.py:291
  13.8 0.4 collective-permute-done.away
  14.2 1.5 %collective-permute-done.1.rest_0_.refs_0_ = bf16[1,128,1024]{2,1,0:T(8,128)(2,1)S(1)} collective-permute-done((bf16[1,128,1024]{2,1,0:T(8,128)(2,1)S(1)}, bf16[1,128,1024]{2,1,0:T(8,128)(2,1)S(1)}, u32[]{:S(2)}, u32[]{:S(2)}) %collective-permute-start.1) | collective-permute-done | bytes 262176 | tf_op jit(solution)/shard_map/ppermute | solution.py:516
  15.6 3.2 %collective-permute-start.5 = (bf16[10,48,128]{2,1,0:T(8,128)(2,1)S(1)}, bf16[10,48,128]{2,1,0:T(8,128)(2,1)S(1)}, u32[]{:S(2)}, u32[]{:S(2)}) collective-permute-start(bf16[10,48,128]{2,1,0:T(8,128)(2,1)S(1)} %shard_map.160.refs_1_.refs_0_), channel_id=1, source_target_pairs={{0,2},{1,3},{2,0},{3,1},{4,6},{5,7},{6,4},{7,5},{8,10},{9,11},{10,... | collective-permute-start | bytes 368648 | tf_op jit(solution)/shard_map/ppermute | solution.py:29
  18.8 1.5 %collective-permute-start.7 = (bf16[10,48,128]{2,1,0:T(8,128)(2,1)S(1)}, bf16[10,48,128]{2,1,0:T(8,128)(2,1)S(1)}, u32[]{:S(2)}, u32[]{:S(2)}) collective-permute-start(bf16[10,48,128]{2,1,0:T(8,128)(2,1)S(1)} %shard_map.160.refs_1_.refs_0_), channel_id=1, source_target_pairs={{0,6},{1,7},{2,4},{3,5},{4,2},{5,3},{6,0},{7,1},{8,14},{9,15},{10,... | collective-permute-start | bytes 368648 | tf_op jit(solution)/shard_map/ppermute | solution.py:29
  20.3 0.1 collective-permute-start.15
  20.4 0.0 copy-start.1
  20.5 1.9 %collective-permute-done.5.refs_1_ = bf16[10,48,128]{2,1,0:T(8,128)(2,1)S(1)} collective-permute-done((bf16[10,48,128]{2,1,0:T(8,128)(2,1)S(1)}, bf16[10,48,128]{2,1,0:T(8,128)(2,1)S(1)}, u32[]{:S(2)}, u32[]{:S(2)}) %collective-permute-start.5) | collective-permute-done | bytes 122912 | tf_op jit(solution)/shard_map/ppermute | solution.py:29
  22.4 2.6 %collective-permute-done.6.refs_2_ = bf16[10,48,128]{2,1,0:T(8,128)(2,1)S(1)} collective-permute-done((bf16[10,48,128]{2,1,0:T(8,128)(2,1)S(1)}, bf16[10,48,128]{2,1,0:T(8,128)(2,1)S(1)}, u32[]{:S(2)}, u32[]{:S(2)}) %collective-permute-start.6) | collective-permute-done | bytes 122912 | tf_op jit(solution)/shard_map/ppermute | solution.py:29
  25.0 1.3 %collective-permute-done.7.refs_3_ = bf16[10,48,128]{2,1,0:T(8,128)(2,1)S(1)} collective-permute-done((bf16[10,48,128]{2,1,0:T(8,128)(2,1)S(1)}, bf16[10,48,128]{2,1,0:T(8,128)(2,1)S(1)}, u32[]{:S(2)}, u32[]{:S(2)}) %collective-permute-start.7) | collective-permute-done | bytes 122912 | tf_op jit(solution)/shard_map/ppermute | solution.py:29
  26.3 3.5 %shard_map.163 = bf16[40,48,128]{2,1,0:T(8,128)(2,1)S(1)} custom-call(bf16[40,48,128]{2,1,0:T(8,128)(2,1)S(1)} %shard_map.162.rows, bf16[6144,128]{1,0:T(8,128)(2,1)S(1)} %copy-done.1, bf16[6144,128]{1,0:T(8,128)(2,1)S(1)} %collective-permute-done.2.refs_2_.rest_1_, bf16[6144,128]{1,0:T(8,128)(2,1)S(1)} %copy-done.2, ...), custom_call_target="tpu_custom_call" | custom-call | flops 400000000 | bytes 10485760 | tf_op jit(solution)/shard_map/pallas_call | solution.py:347
  29.8 1.6 %collective-permute-start.10 = (bf16[5,48,128]{2,1,0:T(8,128)(2,1)S(1)}, bf16[5,48,128]{2,1,0:T(8,128)(2,1)S(1)}, u32[]{:S(2)}, u32[]{:S(2)}) collective-permute-start(bf16[5,48,128]{2,1,0:T(8,128)(2,1)S(1)} %get-tuple-element.43), channel_id=1, source_target_pairs={{0,6},{1,7},{2,4},{3,5},{4,2},{5,3},{6,0},{7,1},{8,14},{9,15},{10,... | collective-permute-start | bytes 184328 | tf_op jit(solution)/shard_map/ppermute | solution.py:29
  31.4 1.7 %collective-permute-start.8 = (bf16[5,48,128]{2,1,0:T(8,128)(2,1)S(1)}, bf16[5,48,128]{2,1,0:T(8,128)(2,1)S(1)}, u32[]{:S(2)}, u32[]{:S(2)}) collective-permute-start(bf16[5,48,128]{2,1,0:T(8,128)(2,1)S(1)} %get-tuple-element.45), channel_id=1, source_target_pairs={{0,2},{1,3},{2,0},{3,1},{4,6},{5,7},{6,4},{7,5},{8,10},{9,11},{10,... | collective-permute-start | bytes 184328 | tf_op jit(solution)/shard_map/ppermute | solution.py:29
  33.1 0.3 collective-permute-start.9
  33.4 1.8 %collective-permute-start.12 = (bf16[5,48,128]{2,1,0:T(8,128)(2,1)S(1)}, bf16[5,48,128]{2,1,0:T(8,128)(2,1)S(1)}, u32[]{:S(2)}, u32[]{:S(2)}) collective-permute-start(bf16[5,48,128]{2,1,0:T(8,128)(2,1)S(1)} %get-tuple-element.41), channel_id=1, source_target_pairs={{0,2},{1,3},{2,0},{3,1},{4,6},{5,7},{6,4},{7,5},{8,10},{9,11},{10,... | collective-permute-start | bytes 184328 | tf_op jit(solution)/shard_map/ppermute | solution.py:29
  35.2 0.2 select_reduce_fusion.1
  35.4 1.8 %collective-permute-done.10 = bf16[5,48,128]{2,1,0:T(8,128)(2,1)S(1)} collective-permute-done((bf16[5,48,128]{2,1,0:T(8,128)(2,1)S(1)}, bf16[5,48,128]{2,1,0:T(8,128)(2,1)S(1)}, u32[]{:S(2)}, u32[]{:S(2)}) %collective-permute-start.10) | collective-permute-done | bytes 61472 | tf_op jit(solution)/shard_map/ppermute | solution.py:29
  37.2 1.3 %collective-permute-done.8 = bf16[5,48,128]{2,1,0:T(8,128)(2,1)S(1)} collective-permute-done((bf16[5,48,128]{2,1,0:T(8,128)(2,1)S(1)}, bf16[5,48,128]{2,1,0:T(8,128)(2,1)S(1)}, u32[]{:S(2)}, u32[]{:S(2)}) %collective-permute-start.8) | collective-permute-done | bytes 61472 | tf_op jit(solution)/shard_map/ppermute | solution.py:29
  38.5 2.2 %collective-permute-start.11 = (bf16[5,48,128]{2,1,0:T(8,128)(2,1)S(1)}, bf16[5,48,128]{2,1,0:T(8,128)(2,1)S(1)}, u32[]{:S(2)}, u32[]{:S(2)}) collective-permute-start(bf16[5,48,128]{2,1,0:T(8,128)(2,1)S(1)} %get-tuple-element.37), channel_id=1, source_target_pairs={{0,8},{1,9},{2,10},{3,11},{4,12},{5,13},{6,14},{7,15},{8,0},{9,1},... | collective-permute-start | bytes 184328 | tf_op jit(solution)/shard_map/ppermute | solution.py:29
  40.8 1.0 %shard_map.164 = (bf16[2,128,1024]{2,1,0:T(8,128)(2,1)}, bf16[2,128,1024]{2,1,0:T(8,128)(2,1)}) custom-call(bf16[1,128,1024]{2,1,0:T(8,128)(2,1)S(1)} %collective-permute-done.1.rest_0_.refs_0_, bf16[3,128,1024]{2,1,0:T(8,128)(2,1)S(1)} %collective-permute-done.15.refs_1_, f32[5,48,128]{2,1,0:T(8,128)S(1)} %get-tuple-element.38.refs_2_), custom_call_target="tpu_custom_call" | custom-call | tf_op jit(solution)/shard_map/pallas_call | solution.py:462
  41.8 0.1 collective-permute-done.13.rest_2_
  41.9 2.4 %collective-permute-done.14.rest_3_ = bf16[5,48,128]{2,1,0:T(8,128)(2,1)S(1)} collective-permute-done((bf16[5,48,128]{2,1,0:T(8,128)(2,1)S(1)}, bf16[5,48,128]{2,1,0:T(8,128)(2,1)S(1)}, u32[]{:S(2)}, u32[]{:S(2)}) %collective-permute-start.14) | collective-permute-done | bytes 61472 | tf_op jit(solution)/shard_map/ppermute | solution.py:29
  44.2 0.6 %collective-permute-done.11.away = bf16[5,48,128]{2,1,0:T(8,128)(2,1)S(1)} collective-permute-done((bf16[5,48,128]{2,1,0:T(8,128)(2,1)S(1)}, bf16[5,48,128]{2,1,0:T(8,128)(2,1)S(1)}, u32[]{:S(2)}, u32[]{:S(2)}) %collective-permute-start.11) | collective-permute-done | bytes 61472 | tf_op jit(solution)/shard_map/ppermute | solution.py:29
  44.9 1.6 %shard_map.165 = bf16[12,6144]{1,0:T(8,128)(2,1)} custom-call(s32[13,12]{1,0:T(8,128)S(1)} %get-tuple-element.19.plan, s32[1]{0:T(128)} %bitcast.2.mine, f32[2,12]{1,0:T(2,128)S(1)} %fusion.2.weights, f32[12,48,128]{2,1,0:T(8,128)S(1)} %get-tuple-element.31.state, bf16[5,48,128]{2,1,0:T(8,128)(2,1)S(1)} %collective-permute-done.11.away, ...), custom_call_target="tpu_custom_call" | custom-call | tf_op jit(solution)/shard_map/pallas_call | solution.py:436
  (25 shorter events, 0.2 us)
Async XLA Ops:
  0.6 34.5 %copy-start = (bf16[6144,8]{0,1:T(8,128)(2,1)S(1)}, bf16[6144,8]{0,1:T(8,128)(2,1)}, u32[]{:S(2)}) copy-start(bf16[6144,8]{0,1:T(8,128)(2,1)} %param.24) | copy-start | bytes 294916
  0.6 18.1 %collective-permute-start.2 = (bf16[6144,128]{1,0:T(8,128)(2,1)}, bf16[6144,128]{1,0:T(8,128)(2,1)S(1)}, u32[]{:S(2)}, u32[]{:S(2)}) collective-permute-start(bf16[6144,128]{1,0:T(8,128)(2,1)} %rest_0_.1), channel_id=1, source_target_pairs={{0,1},{1,0},{2,3},{3,2},{4,5},{5,4},{6,7},{7,6},{8,9},{9,8},{10,11... | collective-permute-start | bytes 4718600 | tf_op jit(solution)/shard_map/ppermute | solution.py:29
  1.2 19.2 %collective-permute-start.3 = (bf16[6144,128]{1,0:T(8,128)(2,1)}, bf16[6144,128]{1,0:T(8,128)(2,1)S(1)}, u32[]{:S(2)}, u32[]{:S(2)}) collective-permute-start(bf16[6144,128]{1,0:T(8,128)(2,1)} %rest_2_.1), channel_id=1, source_target_pairs={{0,1},{1,0},{2,3},{3,2},{4,5},{5,4},{6,7},{7,6},{8,9},{9,8},{10,11... | collective-permute-start | bytes 4718600 | tf_op jit(solution)/shard_map/ppermute | solution.py:29
  1.2 19.2 %collective-permute-start.4 = (bf16[128,6144]{1,0:T(8,128)(2,1)}, bf16[128,6144]{1,0:T(8,128)(2,1)}, u32[]{:S(2)}, u32[]{:S(2)}) collective-permute-start(bf16[128,6144]{1,0:T(8,128)(2,1)} %rest_4_.1), channel_id=1, source_target_pairs={{0,1},{1,0},{2,3},{3,2},{4,5},{5,4},{6,7},{7,6},{8,9},{9,8},{10,11... | collective-permute-start | bytes 4718600 | tf_op jit(solution)/shard_map/ppermute | solution.py:29
  5.7 9.9 %collective-permute-start.1 = (bf16[1,128,1024]{2,1,0:T(8,128)(2,1)S(1)}, bf16[1,128,1024]{2,1,0:T(8,128)(2,1)S(1)}, u32[]{:S(2)}, u32[]{:S(2)}) collective-permute-start(bf16[1,128,1024]{2,1,0:T(8,128)(2,1)S(1)} %get-tuple-element.30), channel_id=1, source_target_pairs={{0,1},{1,2},{2,3},{3,4},{4,5},{5,6},{6,7},{7,8},{8,9},{9,10},{10,1... | collective-permute-start | bytes 786440 | tf_op jit(solution)/shard_map/ppermute | solution.py:516
  7.7 6.4 %collective-permute-start = (bf16[5,48,128]{2,1,0:T(8,128)(2,1)S(1)}, bf16[5,48,128]{2,1,0:T(8,128)(2,1)S(1)}, u32[]{:S(2)}, u32[]{:S(2)}) collective-permute-start(bf16[5,48,128]{2,1,0:T(8,128)(2,1)S(1)} %get-tuple-element.29), channel_id=1, source_target_pairs={{0,8},{1,9},{2,10},{3,11},{4,12},{5,13},{6,14},{7,15},{8,0},{9,1},... | collective-permute-start | bytes 184328 | tf_op jit(solution)/shard_map/ppermute | solution.py:29
  11.8 8.5 %copy-start.4 = (s32[12,2]{0,1:T(2,128)S(1)}, s32[12,2]{0,1:T(2,128)}, u32[]{:S(2)}) copy-start(s32[12,2]{0,1:T(2,128)} %param.23) | copy-start | bytes 292
  15.6 6.8 %collective-permute-start.5 = (bf16[10,48,128]{2,1,0:T(8,128)(2,1)S(1)}, bf16[10,48,128]{2,1,0:T(8,128)(2,1)S(1)}, u32[]{:S(2)}, u32[]{:S(2)}) collective-permute-start(bf16[10,48,128]{2,1,0:T(8,128)(2,1)S(1)} %shard_map.160.refs_1_.refs_0_), channel_id=1, source_target_pairs={{0,2},{1,3},{2,0},{3,1},{4,6},{5,7},{6,4},{7,5},{8,10},{9,11},{10,... | collective-permute-start | bytes 368648 | tf_op jit(solution)/shard_map/ppermute | solution.py:29
  18.8 6.2 %collective-permute-start.6 = (bf16[10,48,128]{2,1,0:T(8,128)(2,1)S(1)}, bf16[10,48,128]{2,1,0:T(8,128)(2,1)S(1)}, u32[]{:S(2)}, u32[]{:S(2)}) collective-permute-start(bf16[10,48,128]{2,1,0:T(8,128)(2,1)S(1)} %shard_map.160.refs_1_.refs_0_), channel_id=1, source_target_pairs={{0,4},{1,5},{2,6},{3,7},{4,0},{5,1},{6,2},{7,3},{8,12},{9,13},{10,... | collective-permute-start | bytes 368648 | tf_op jit(solution)/shard_map/ppermute | solution.py:29
  18.8 7.5 %collective-permute-start.7 = (bf16[10,48,128]{2,1,0:T(8,128)(2,1)S(1)}, bf16[10,48,128]{2,1,0:T(8,128)(2,1)S(1)}, u32[]{:S(2)}, u32[]{:S(2)}) collective-permute-start(bf16[10,48,128]{2,1,0:T(8,128)(2,1)S(1)} %shard_map.160.refs_1_.refs_0_), channel_id=1, source_target_pairs={{0,6},{1,7},{2,4},{3,5},{4,2},{5,3},{6,0},{7,1},{8,14},{9,15},{10,... | collective-permute-start | bytes 368648 | tf_op jit(solution)/shard_map/ppermute | solution.py:29
  20.3 20.4 %collective-permute-start.15 = (bf16[3,128,1024]{2,1,0:T(8,128)(2,1)S(1)}, bf16[3,128,1024]{2,1,0:T(8,128)(2,1)S(1)}, u32[]{:S(2)}, u32[]{:S(2)}) collective-permute-start(bf16[3,128,1024]{2,1,0:T(8,128)(2,1)S(1)} %get-tuple-element.32), channel_id=1, source_target_pairs={{0,1},{1,2},{2,3},{3,4},{4,5},{5,6},{6,7},{7,8},{8,9},{9,10},{10,1... | collective-permute-start | bytes 2359304 | tf_op jit(solution)/shard_map/ppermute | solution.py:517
  20.4 5.9 %copy-start.1 = (bf16[6144,128]{1,0:T(8,128)(2,1)S(1)}, bf16[6144,128]{1,0:T(8,128)(2,1)}, u32[]{:S(2)}) copy-start(bf16[6144,128]{1,0:T(8,128)(2,1)} %rest_0_.1) | copy-start | bytes 4718596
  20.4 5.9 %copy-start.2 = (bf16[6144,128]{1,0:T(8,128)(2,1)S(1)}, bf16[6144,128]{1,0:T(8,128)(2,1)}, u32[]{:S(2)}) copy-start(bf16[6144,128]{1,0:T(8,128)(2,1)} %rest_2_.1) | copy-start | bytes 4718596
  20.4 5.9 %copy-start.3 = (bf16[128,6144]{1,0:T(8,128)(2,1)S(1)}, bf16[128,6144]{1,0:T(8,128)(2,1)}, u32[]{:S(2)}) copy-start(bf16[128,6144]{1,0:T(8,128)(2,1)} %rest_4_.1) | copy-start | bytes 4718596
  29.8 7.4 %collective-permute-start.10 = (bf16[5,48,128]{2,1,0:T(8,128)(2,1)S(1)}, bf16[5,48,128]{2,1,0:T(8,128)(2,1)S(1)}, u32[]{:S(2)}, u32[]{:S(2)}) collective-permute-start(bf16[5,48,128]{2,1,0:T(8,128)(2,1)S(1)} %get-tuple-element.43), channel_id=1, source_target_pairs={{0,6},{1,7},{2,4},{3,5},{4,2},{5,3},{6,0},{7,1},{8,14},{9,15},{10,... | collective-permute-start | bytes 184328 | tf_op jit(solution)/shard_map/ppermute | solution.py:29
  31.4 7.1 %collective-permute-start.8 = (bf16[5,48,128]{2,1,0:T(8,128)(2,1)S(1)}, bf16[5,48,128]{2,1,0:T(8,128)(2,1)S(1)}, u32[]{:S(2)}, u32[]{:S(2)}) collective-permute-start(bf16[5,48,128]{2,1,0:T(8,128)(2,1)S(1)} %get-tuple-element.45), channel_id=1, source_target_pairs={{0,2},{1,3},{2,0},{3,1},{4,6},{5,7},{6,4},{7,5},{8,10},{9,11},{10,... | collective-permute-start | bytes 184328 | tf_op jit(solution)/shard_map/ppermute | solution.py:29
  33.1 5.4 %collective-permute-start.9 = (bf16[5,48,128]{2,1,0:T(8,128)(2,1)S(1)}, bf16[5,48,128]{2,1,0:T(8,128)(2,1)S(1)}, u32[]{:S(2)}, u32[]{:S(2)}) collective-permute-start(bf16[5,48,128]{2,1,0:T(8,128)(2,1)S(1)} %get-tuple-element.44), channel_id=1, source_target_pairs={{0,4},{1,5},{2,6},{3,7},{4,0},{5,1},{6,2},{7,3},{8,12},{9,13},{10,... | collective-permute-start | bytes 184328 | tf_op jit(solution)/shard_map/ppermute | solution.py:29
  33.4 8.4 %collective-permute-start.12 = (bf16[5,48,128]{2,1,0:T(8,128)(2,1)S(1)}, bf16[5,48,128]{2,1,0:T(8,128)(2,1)S(1)}, u32[]{:S(2)}, u32[]{:S(2)}) collective-permute-start(bf16[5,48,128]{2,1,0:T(8,128)(2,1)S(1)} %get-tuple-element.41), channel_id=1, source_target_pairs={{0,2},{1,3},{2,0},{3,1},{4,6},{5,7},{6,4},{7,5},{8,10},{9,11},{10,... | collective-permute-start | bytes 184328 | tf_op jit(solution)/shard_map/ppermute | solution.py:29
  37.2 4.7 %collective-permute-start.13 = (bf16[5,48,128]{2,1,0:T(8,128)(2,1)S(1)}, bf16[5,48,128]{2,1,0:T(8,128)(2,1)S(1)}, u32[]{:S(2)}, u32[]{:S(2)}) collective-permute-start(bf16[5,48,128]{2,1,0:T(8,128)(2,1)S(1)} %get-tuple-element.40), channel_id=1, source_target_pairs={{0,4},{1,5},{2,6},{3,7},{4,0},{5,1},{6,2},{7,3},{8,12},{9,13},{10,... | collective-permute-start | bytes 184328 | tf_op jit(solution)/shard_map/ppermute | solution.py:29
  38.5 5.8 %collective-permute-start.14 = (bf16[5,48,128]{2,1,0:T(8,128)(2,1)S(1)}, bf16[5,48,128]{2,1,0:T(8,128)(2,1)S(1)}, u32[]{:S(2)}, u32[]{:S(2)}) collective-permute-start(bf16[5,48,128]{2,1,0:T(8,128)(2,1)S(1)} %get-tuple-element.39), channel_id=1, source_target_pairs={{0,6},{1,7},{2,4},{3,5},{4,2},{5,3},{6,0},{7,1},{8,14},{9,15},{10,... | collective-permute-start | bytes 184328 | tf_op jit(solution)/shard_map/ppermute | solution.py:29
  38.5 6.4 %collective-permute-start.11 = (bf16[5,48,128]{2,1,0:T(8,128)(2,1)S(1)}, bf16[5,48,128]{2,1,0:T(8,128)(2,1)S(1)}, u32[]{:S(2)}, u32[]{:S(2)}) collective-permute-start(bf16[5,48,128]{2,1,0:T(8,128)(2,1)S(1)} %get-tuple-element.37), channel_id=1, source_target_pairs={{0,8},{1,9},{2,10},{3,11},{4,12},{5,13},{6,14},{7,15},{8,0},{9,1},... | collective-permute-start | bytes 184328 | tf_op jit(solution)/shard_map/ppermute | solution.py:29

commit v6 on v5

--- a/solution.py
+++ b/solution.py
@@ -531,10 +531,13 @@
     parts = [sums[i * CAP:(i + 1) * CAP] for i in range(2 * len(blocks))]
     own_parts, away_parts = parts[0::2], parts[1::2]
     back = away_parts[0].astype(F32)
-    for part, mask in zip(away_parts[1:], masks):
+    for part, mask in zip(away_parts[1:][1:] + away_parts[1:][:1], masks[1:] + masks[:1]):
         back = back + exchanged(part, mask).astype(F32)
     own_sums = [own_parts[0]]
-    own_sums += [exchanged(part, mask) for part, mask in zip(own_parts[1:], masks)]
+    own_sums += [
+        exchanged(part, mask)
+        for part, mask in zip(own_parts[1:][1:] + own_parts[1:][:1], masks[1:] + masks[:1])
+    ]
     away_sums = exchanged(back.astype(BF16), swap)
     moved_keys, moved_values = delivered(arrived, back)
     mixed = finished(plan, mine, weights, state, away_sums, own_sums, in_hbm(moved_keys))

time: 46.6 us -> 46.1 us (0.989)
  waiting for transfers between devices: 13.8 us -> 11.3 us
  starting transfers between devices: 17.6 us -> 19.5 us
    ppermute x14, waiting for transfers between devices: 12.4 us -> 9.86 us  [exchanged(): return lax.ppermute(array, 'attn', [(i, i ^ mask) for i in range(length)])]
    ppermute x14, starting transfers between devices: 17.4 us -> 19.3 us  [exchanged(): return lax.ppermute(array, 'attn', [(i, i ^ mask) for i in range(length)])]
  transfers between devices with their start and end apart: 16 -> 16, of which waited for: 10 -> 9; matrix products, arithmetic and copies ran while one was open for 1% -> 1% of each run, Pallas kernels for 27% -> 27%
where the time goes in v6:
time: 46.1 us; the launch traced here: 45.9 us
  starting transfers between devices  19.5 us (42%)
  Pallas kernels  14 us (30%)
  waiting for transfers between devices  11.3 us (25%)
  between operations  0.81 us (2%)
    ppermute x14, starting transfers between devices, exchanged(): return lax.ppermute(array, 'attn', [(i, i ^ mask) for i in range(length)])  19.3 us
    ppermute x14, waiting for transfers between devices, exchanged(): return lax.ppermute(array, 'attn', [(i, i ^ mask) for i in range(length)])  9.86 us
    pallas_call x1, Pallas kernels, staged(): pl.pallas_call(stage_kernel, out_shape=(jax.ShapeDtypeStruct((pages + 5,...  4.05 us
    pallas_call x2, Pallas kernels, attended(): pl.pallas_call(kernel, out_shape=attend_shapes(rows, heads)[:outs], in_sp...  3.82 us
    pallas_call x1, Pallas kernels, expert_parts(): pl.pallas_call(functools.partial(expert_kernel, block), out_shape=jax.Sha...  3.46 us
    pallas_call x1, Pallas kernels, finished(): pl.pallas_call(functools.partial(finish_kernel, len(owns)), out_shape=jax...  1.57 us
    ppermute x1, waiting for transfers between devices, body(): arrived[0] = lax.ppermute(leave[0], 'attn', along)  1.45 us
    pallas_call x1, Pallas kernels, delivered(): pl.pallas_call(functools.partial(deliver_kernel, len(arrived)), out_shape...  1 us
  transfers between devices with their start and end apart: 16, of which 9 were waited for; matrix products, arithmetic and copies ran while one was open for 1% of the time, Pallas kernels for 27%

profile of v6, /device:TPU:0, one launch (start us, length us, event | category | flops | bytes accessed | tf_op | source)
XLA Modules:
  0.0 45.9 jit_solution(7536115153113287334)
XLA Ops:
  0.6 0.0 copy-start
  0.6 0.5 %collective-permute-start.2 = (bf16[6144,128]{1,0:T(8,128)(2,1)}, bf16[6144,128]{1,0:T(8,128)(2,1)S(1)}, u32[]{:S(2)}, u32[]{:S(2)}) collective-permute-start(bf16[6144,128]{1,0:T(8,128)(2,1)} %rest_0_.1), channel_id=1, source_target_pairs={{0,1},{1,0},{2,3},{3,2},{4,5},{5,4},{6,7},{7,6},{8,9},{9,8},{10,11... | collective-permute-start | bytes 4718600 | tf_op jit(solution)/shard_map/ppermute | solution.py:29
  1.2 0.1 collective-permute-start.3
  1.2 0.4 collective-permute-start.4
  1.7 4.1 %shard_map.157 = (s32[13,12]{1,0:T(8,128)S(1)}, bf16[96,16,1024]{2,1,0:T(8,128)(2,1)S(1)}, bf16[96,16,1024]{2,1,0:T(8,128)(2,1)S(1)}, f32[576,128]{1,0:T(8,128)S...) custom-call(s32[8,12]{1,0:T(8,128)} %bitcast.15, s32[12]{0:T(128)} %lengths_at.1, ...), custom_call_target="tpu_custom_call" | custom-call | bytes 8388608 | tf_op jit(solution)/shard_map/pallas_call | solution.py:151
  5.7 0.1 collective-permute-start.1
  5.9 1.8 %shard_map.158 = (f32[12,48,128]{2,1,0:T(8,128)S(1)}, bf16[12,48,128]{2,1,0:T(8,128)(2,1)S(1)}, bf16[5,48,128]{2,1,0:T(8,128)(2,1)S(1)}, bf16[5,48,128]{2,1,0:T(8,128)(2,1)S(1)}) custom-call(s32[13,12]{1,0:T(8,128)S(1)} %get-tuple-element.19.plan, bf16[96,16,1024]{2,1,0:T(8,128)(2,1)S(1)} %get-tuple-element.20.key_pool, ...), custom_call_target="tpu_custom_call" | custom-call | flops 1048576 | bytes 65536 | tf_op jit(solution)/shard_map/pallas_call | solution.py:291
  7.7 4.1 %collective-permute-start = (bf16[5,48,128]{2,1,0:T(8,128)(2,1)S(1)}, bf16[5,48,128]{2,1,0:T(8,128)(2,1)S(1)}, u32[]{:S(2)}, u32[]{:S(2)}) collective-permute-start(bf16[5,48,128]{2,1,0:T(8,128)(2,1)S(1)} %get-tuple-element.29), channel_id=1, source_target_pairs={{0,8},{1,9},{2,10},{3,11},{4,12},{5,13},{6,14},{7,15},{8,0},{9,1},... | collective-permute-start | bytes 184328 | tf_op jit(solution)/shard_map/ppermute | solution.py:29
  11.8 2.0 %shard_map.159 = (f32[12,48,128]{2,1,0:T(8,128)S(1)}, bf16[12,48,128]{2,1,0:T(8,128)(2,1)S(1)}, bf16[5,48,128]{2,1,0:T(8,128)(2,1)S(1)}) custom-call(s32[13,12]{1,0:T(8,128)S(1)} %get-tuple-element.19.plan, bf16[96,16,1024]{2,1,0:T(8,128)(2,1)S(1)} %get-tuple-element.20.key_pool, bf16[96,16,1024]{2,1,0:T(8,128)(2,1)S(1)} %get-tuple-element.21.value_pool, ...), custom_call_target="tpu_custom_call" | custom-call | flops 1048576 | bytes 65536 | tf_op jit(solution)/shard_map/pallas_call | solution.py:291
  13.8 0.4 collective-permute-done.away
  14.2 1.5 %collective-permute-done.1.rest_0_.refs_0_ = bf16[1,128,1024]{2,1,0:T(8,128)(2,1)S(1)} collective-permute-done((bf16[1,128,1024]{2,1,0:T(8,128)(2,1)S(1)}, bf16[1,128,1024]{2,1,0:T(8,128)(2,1)S(1)}, u32[]{:S(2)}, u32[]{:S(2)}) %collective-permute-start.1) | collective-permute-done | bytes 262176 | tf_op jit(solution)/shard_map/ppermute | solution.py:516
  15.6 3.2 %collective-permute-start.5 = (bf16[10,48,128]{2,1,0:T(8,128)(2,1)S(1)}, bf16[10,48,128]{2,1,0:T(8,128)(2,1)S(1)}, u32[]{:S(2)}, u32[]{:S(2)}) collective-permute-start(bf16[10,48,128]{2,1,0:T(8,128)(2,1)S(1)} %shard_map.160.refs_1_.refs_0_), channel_id=1, source_target_pairs={{0,2},{1,3},{2,0},{3,1},{4,6},{5,7},{6,4},{7,5},{8,10},{9,11},{10,... | collective-permute-start | bytes 368648 | tf_op jit(solution)/shard_map/ppermute | solution.py:29
  18.8 1.5 %collective-permute-start.7 = (bf16[10,48,128]{2,1,0:T(8,128)(2,1)S(1)}, bf16[10,48,128]{2,1,0:T(8,128)(2,1)S(1)}, u32[]{:S(2)}, u32[]{:S(2)}) collective-permute-start(bf16[10,48,128]{2,1,0:T(8,128)(2,1)S(1)} %shard_map.160.refs_1_.refs_0_), channel_id=1, source_target_pairs={{0,6},{1,7},{2,4},{3,5},{4,2},{5,3},{6,0},{7,1},{8,14},{9,15},{10,... | collective-permute-start | bytes 368648 | tf_op jit(solution)/shard_map/ppermute | solution.py:29
  20.3 0.1 collective-permute-start.15
  20.4 0.0 copy-start.3
  20.5 1.9 %collective-permute-done.5.refs_1_ = bf16[10,48,128]{2,1,0:T(8,128)(2,1)S(1)} collective-permute-done((bf16[10,48,128]{2,1,0:T(8,128)(2,1)S(1)}, bf16[10,48,128]{2,1,0:T(8,128)(2,1)S(1)}, u32[]{:S(2)}, u32[]{:S(2)}) %collective-permute-start.5) | collective-permute-done | bytes 122912 | tf_op jit(solution)/shard_map/ppermute | solution.py:29
  22.4 2.6 %collective-permute-done.6.refs_2_ = bf16[10,48,128]{2,1,0:T(8,128)(2,1)S(1)} collective-permute-done((bf16[10,48,128]{2,1,0:T(8,128)(2,1)S(1)}, bf16[10,48,128]{2,1,0:T(8,128)(2,1)S(1)}, u32[]{:S(2)}, u32[]{:S(2)}) %collective-permute-start.6) | collective-permute-done | bytes 122912 | tf_op jit(solution)/shard_map/ppermute | solution.py:29
  25.0 1.3 %collective-permute-done.7.refs_3_ = bf16[10,48,128]{2,1,0:T(8,128)(2,1)S(1)} collective-permute-done((bf16[10,48,128]{2,1,0:T(8,128)(2,1)S(1)}, bf16[10,48,128]{2,1,0:T(8,128)(2,1)S(1)}, u32[]{:S(2)}, u32[]{:S(2)}) %collective-permute-start.7) | collective-permute-done | bytes 122912 | tf_op jit(solution)/shard_map/ppermute | solution.py:29
  26.3 3.5 %shard_map.163 = bf16[40,48,128]{2,1,0:T(8,128)(2,1)S(1)} custom-call(bf16[40,48,128]{2,1,0:T(8,128)(2,1)S(1)} %shard_map.162.rows, bf16[6144,128]{1,0:T(8,128)(2,1)S(1)} %copy-done.1, bf16[6144,128]{1,0:T(8,128)(2,1)S(1)} %collective-permute-done.2.refs_2_.rest_1_, bf16[6144,128]{1,0:T(8,128)(2,1)S(1)} %copy-done.2, ...), custom_call_target="tpu_custom_call" | custom-call | flops 400000000 | bytes 10485760 | tf_op jit(solution)/shard_map/pallas_call | solution.py:347
  29.8 1.8 %collective-permute-start.10 = (bf16[5,48,128]{2,1,0:T(8,128)(2,1)S(1)}, bf16[5,48,128]{2,1,0:T(8,128)(2,1)S(1)}, u32[]{:S(2)}, u32[]{:S(2)}) collective-permute-start(bf16[5,48,128]{2,1,0:T(8,128)(2,1)S(1)} %get-tuple-element.43), channel_id=1, source_target_pairs={{0,2},{1,3},{2,0},{3,1},{4,6},{5,7},{6,4},{7,5},{8,10},{9,11},{10,... | collective-permute-start | bytes 184328 | tf_op jit(solution)/shard_map/ppermute | solution.py:29
  31.7 0.3 collective-permute-start.8
  32.0 1.4 %collective-permute-start.9 = (bf16[5,48,128]{2,1,0:T(8,128)(2,1)S(1)}, bf16[5,48,128]{2,1,0:T(8,128)(2,1)S(1)}, u32[]{:S(2)}, u32[]{:S(2)}) collective-permute-start(bf16[5,48,128]{2,1,0:T(8,128)(2,1)S(1)} %get-tuple-element.44), channel_id=1, source_target_pairs={{0,6},{1,7},{2,4},{3,5},{4,2},{5,3},{6,0},{7,1},{8,14},{9,15},{10,... | collective-permute-start | bytes 184328 | tf_op jit(solution)/shard_map/ppermute | solution.py:29
  33.4 1.7 %collective-permute-start.12 = (bf16[5,48,128]{2,1,0:T(8,128)(2,1)S(1)}, bf16[5,48,128]{2,1,0:T(8,128)(2,1)S(1)}, u32[]{:S(2)}, u32[]{:S(2)}) collective-permute-start(bf16[5,48,128]{2,1,0:T(8,128)(2,1)S(1)} %get-tuple-element.41), channel_id=1, source_target_pairs={{0,4},{1,5},{2,6},{3,7},{4,0},{5,1},{6,2},{7,3},{8,12},{9,13},{10,... | collective-permute-start | bytes 184328 | tf_op jit(solution)/shard_map/ppermute | solution.py:29
  35.1 0.2 select_reduce_fusion.1
  35.3 1.9 %collective-permute-done.10 = bf16[5,48,128]{2,1,0:T(8,128)(2,1)S(1)} collective-permute-done((bf16[5,48,128]{2,1,0:T(8,128)(2,1)S(1)}, bf16[5,48,128]{2,1,0:T(8,128)(2,1)S(1)}, u32[]{:S(2)}, u32[]{:S(2)}) %collective-permute-start.10) | collective-permute-done | bytes 61472 | tf_op jit(solution)/shard_map/ppermute | solution.py:29
  37.2 1.3 %collective-permute-start.14 = (bf16[5,48,128]{2,1,0:T(8,128)(2,1)S(1)}, bf16[5,48,128]{2,1,0:T(8,128)(2,1)S(1)}, u32[]{:S(2)}, u32[]{:S(2)}) collective-permute-start(bf16[5,48,128]{2,1,0:T(8,128)(2,1)S(1)} %get-tuple-element.39), channel_id=1, source_target_pairs={{0,2},{1,3},{2,0},{3,1},{4,6},{5,7},{6,4},{7,5},{8,10},{9,11},{10,... | collective-permute-start | bytes 184328 | tf_op jit(solution)/shard_map/ppermute | solution.py:29
  38.4 0.1 collective-permute-done.9
  38.5 3.0 %collective-permute-start.11 = (bf16[5,48,128]{2,1,0:T(8,128)(2,1)S(1)}, bf16[5,48,128]{2,1,0:T(8,128)(2,1)S(1)}, u32[]{:S(2)}, u32[]{:S(2)}) collective-permute-start(bf16[5,48,128]{2,1,0:T(8,128)(2,1)S(1)} %get-tuple-element.37), channel_id=1, source_target_pairs={{0,8},{1,9},{2,10},{3,11},{4,12},{5,13},{6,14},{7,15},{8,0},{9,1},... | collective-permute-start | bytes 184328 | tf_op jit(solution)/shard_map/ppermute | solution.py:29
  41.6 1.0 %shard_map.164 = (bf16[2,128,1024]{2,1,0:T(8,128)(2,1)}, bf16[2,128,1024]{2,1,0:T(8,128)(2,1)}) custom-call(bf16[1,128,1024]{2,1,0:T(8,128)(2,1)S(1)} %collective-permute-done.1.rest_0_.refs_0_, bf16[3,128,1024]{2,1,0:T(8,128)(2,1)S(1)} %collective-permute-done.15.refs_1_, f32[5,48,128]{2,1,0:T(8,128)S(1)} %get-tuple-element.38.refs_2_), custom_call_target="tpu_custom_call" | custom-call | tf_op jit(solution)/shard_map/pallas_call | solution.py:462
  42.6 0.4 collective-permute-done.13.rest_2_
  42.9 1.4 %collective-permute-done.11.away = bf16[5,48,128]{2,1,0:T(8,128)(2,1)S(1)} collective-permute-done((bf16[5,48,128]{2,1,0:T(8,128)(2,1)S(1)}, bf16[5,48,128]{2,1,0:T(8,128)(2,1)S(1)}, u32[]{:S(2)}, u32[]{:S(2)}) %collective-permute-start.11) | collective-permute-done | bytes 61472 | tf_op jit(solution)/shard_map/ppermute | solution.py:29
  44.4 1.6 %shard_map.165 = bf16[12,6144]{1,0:T(8,128)(2,1)} custom-call(s32[13,12]{1,0:T(8,128)S(1)} %get-tuple-element.19.plan, s32[1]{0:T(128)} %bitcast.2.mine, f32[2,12]{1,0:T(2,128)S(1)} %fusion.2.weights, f32[12,48,128]{2,1,0:T(8,128)S(1)} %get-tuple-element.31.state, bf16[5,48,128]{2,1,0:T(8,128)(2,1)S(1)} %collective-permute-done.11.away, ...), custom_call_target="tpu_custom_call" | custom-call | tf_op jit(solution)/shard_map/pallas_call | solution.py:436
  (25 shorter events, 0.2 us)
Async XLA Ops:
  0.6 34.5 %copy-start = (bf16[6144,8]{0,1:T(8,128)(2,1)S(1)}, bf16[6144,8]{0,1:T(8,128)(2,1)}, u32[]{:S(2)}) copy-start(bf16[6144,8]{0,1:T(8,128)(2,1)} %param.24) | copy-start | bytes 294916
  0.6 18.1 %collective-permute-start.2 = (bf16[6144,128]{1,0:T(8,128)(2,1)}, bf16[6144,128]{1,0:T(8,128)(2,1)S(1)}, u32[]{:S(2)}, u32[]{:S(2)}) collective-permute-start(bf16[6144,128]{1,0:T(8,128)(2,1)} %rest_0_.1), channel_id=1, source_target_pairs={{0,1},{1,0},{2,3},{3,2},{4,5},{5,4},{6,7},{7,6},{8,9},{9,8},{10,11... | collective-permute-start | bytes 4718600 | tf_op jit(solution)/shard_map/ppermute | solution.py:29
  1.2 19.2 %collective-permute-start.3 = (bf16[6144,128]{1,0:T(8,128)(2,1)}, bf16[6144,128]{1,0:T(8,128)(2,1)S(1)}, u32[]{:S(2)}, u32[]{:S(2)}) collective-permute-start(bf16[6144,128]{1,0:T(8,128)(2,1)} %rest_2_.1), channel_id=1, source_target_pairs={{0,1},{1,0},{2,3},{3,2},{4,5},{5,4},{6,7},{7,6},{8,9},{9,8},{10,11... | collective-permute-start | bytes 4718600 | tf_op jit(solution)/shard_map/ppermute | solution.py:29
  1.2 19.2 %collective-permute-start.4 = (bf16[128,6144]{1,0:T(8,128)(2,1)}, bf16[128,6144]{1,0:T(8,128)(2,1)}, u32[]{:S(2)}, u32[]{:S(2)}) collective-permute-start(bf16[128,6144]{1,0:T(8,128)(2,1)} %rest_4_.1), channel_id=1, source_target_pairs={{0,1},{1,0},{2,3},{3,2},{4,5},{5,4},{6,7},{7,6},{8,9},{9,8},{10,11... | collective-permute-start | bytes 4718600 | tf_op jit(solution)/shard_map/ppermute | solution.py:29
  5.7 9.9 %collective-permute-start.1 = (bf16[1,128,1024]{2,1,0:T(8,128)(2,1)S(1)}, bf16[1,128,1024]{2,1,0:T(8,128)(2,1)S(1)}, u32[]{:S(2)}, u32[]{:S(2)}) collective-permute-start(bf16[1,128,1024]{2,1,0:T(8,128)(2,1)S(1)} %get-tuple-element.30), channel_id=1, source_target_pairs={{0,1},{1,2},{2,3},{3,4},{4,5},{5,6},{6,7},{7,8},{8,9},{9,10},{10,1... | collective-permute-start | bytes 786440 | tf_op jit(solution)/shard_map/ppermute | solution.py:516
  7.7 6.4 %collective-permute-start = (bf16[5,48,128]{2,1,0:T(8,128)(2,1)S(1)}, bf16[5,48,128]{2,1,0:T(8,128)(2,1)S(1)}, u32[]{:S(2)}, u32[]{:S(2)}) collective-permute-start(bf16[5,48,128]{2,1,0:T(8,128)(2,1)S(1)} %get-tuple-element.29), channel_id=1, source_target_pairs={{0,8},{1,9},{2,10},{3,11},{4,12},{5,13},{6,14},{7,15},{8,0},{9,1},... | collective-permute-start | bytes 184328 | tf_op jit(solution)/shard_map/ppermute | solution.py:29
  11.8 8.5 %copy-start.4 = (s32[12,2]{0,1:T(2,128)S(1)}, s32[12,2]{0,1:T(2,128)}, u32[]{:S(2)}) copy-start(s32[12,2]{0,1:T(2,128)} %param.23) | copy-start | bytes 292
  15.6 6.8 %collective-permute-start.5 = (bf16[10,48,128]{2,1,0:T(8,128)(2,1)S(1)}, bf16[10,48,128]{2,1,0:T(8,128)(2,1)S(1)}, u32[]{:S(2)}, u32[]{:S(2)}) collective-permute-start(bf16[10,48,128]{2,1,0:T(8,128)(2,1)S(1)} %shard_map.160.refs_1_.refs_0_), channel_id=1, source_target_pairs={{0,2},{1,3},{2,0},{3,1},{4,6},{5,7},{6,4},{7,5},{8,10},{9,11},{10,... | collective-permute-start | bytes 368648 | tf_op jit(solution)/shard_map/ppermute | solution.py:29
  18.8 6.2 %collective-permute-start.6 = (bf16[10,48,128]{2,1,0:T(8,128)(2,1)S(1)}, bf16[10,48,128]{2,1,0:T(8,128)(2,1)S(1)}, u32[]{:S(2)}, u32[]{:S(2)}) collective-permute-start(bf16[10,48,128]{2,1,0:T(8,128)(2,1)S(1)} %shard_map.160.refs_1_.refs_0_), channel_id=1, source_target_pairs={{0,4},{1,5},{2,6},{3,7},{4,0},{5,1},{6,2},{7,3},{8,12},{9,13},{10,... | collective-permute-start | bytes 368648 | tf_op jit(solution)/shard_map/ppermute | solution.py:29
  18.8 7.5 %collective-permute-start.7 = (bf16[10,48,128]{2,1,0:T(8,128)(2,1)S(1)}, bf16[10,48,128]{2,1,0:T(8,128)(2,1)S(1)}, u32[]{:S(2)}, u32[]{:S(2)}) collective-permute-start(bf16[10,48,128]{2,1,0:T(8,128)(2,1)S(1)} %shard_map.160.refs_1_.refs_0_), channel_id=1, source_target_pairs={{0,6},{1,7},{2,4},{3,5},{4,2},{5,3},{6,0},{7,1},{8,14},{9,15},{10,... | collective-permute-start | bytes 368648 | tf_op jit(solution)/shard_map/ppermute | solution.py:29
  20.3 21.2 %collective-permute-start.15 = (bf16[3,128,1024]{2,1,0:T(8,128)(2,1)S(1)}, bf16[3,128,1024]{2,1,0:T(8,128)(2,1)S(1)}, u32[]{:S(2)}, u32[]{:S(2)}) collective-permute-start(bf16[3,128,1024]{2,1,0:T(8,128)(2,1)S(1)} %get-tuple-element.32), channel_id=1, source_target_pairs={{0,1},{1,2},{2,3},{3,4},{4,5},{5,6},{6,7},{7,8},{8,9},{9,10},{10,1... | collective-permute-start | bytes 2359304 | tf_op jit(solution)/shard_map/ppermute | solution.py:517
  20.4 5.9 %copy-start.1 = (bf16[6144,128]{1,0:T(8,128)(2,1)S(1)}, bf16[6144,128]{1,0:T(8,128)(2,1)}, u32[]{:S(2)}) copy-start(bf16[6144,128]{1,0:T(8,128)(2,1)} %rest_0_.1) | copy-start | bytes 4718596
  20.4 5.9 %copy-start.2 = (bf16[6144,128]{1,0:T(8,128)(2,1)S(1)}, bf16[6144,128]{1,0:T(8,128)(2,1)}, u32[]{:S(2)}) copy-start(bf16[6144,128]{1,0:T(8,128)(2,1)} %rest_2_.1) | copy-start | bytes 4718596
  20.4 5.9 %copy-start.3 = (bf16[128,6144]{1,0:T(8,128)(2,1)S(1)}, bf16[128,6144]{1,0:T(8,128)(2,1)}, u32[]{:S(2)}) copy-start(bf16[128,6144]{1,0:T(8,128)(2,1)} %rest_4_.1) | copy-start | bytes 4718596
  29.8 7.3 %collective-permute-start.10 = (bf16[5,48,128]{2,1,0:T(8,128)(2,1)S(1)}, bf16[5,48,128]{2,1,0:T(8,128)(2,1)S(1)}, u32[]{:S(2)}, u32[]{:S(2)}) collective-permute-start(bf16[5,48,128]{2,1,0:T(8,128)(2,1)S(1)} %get-tuple-element.43), channel_id=1, source_target_pairs={{0,2},{1,3},{2,0},{3,1},{4,6},{5,7},{6,4},{7,5},{8,10},{9,11},{10,... | collective-permute-start | bytes 184328 | tf_op jit(solution)/shard_map/ppermute | solution.py:29
  31.7 5.5 %collective-permute-start.8 = (bf16[5,48,128]{2,1,0:T(8,128)(2,1)S(1)}, bf16[5,48,128]{2,1,0:T(8,128)(2,1)S(1)}, u32[]{:S(2)}, u32[]{:S(2)}) collective-permute-start(bf16[5,48,128]{2,1,0:T(8,128)(2,1)S(1)} %get-tuple-element.45), channel_id=1, source_target_pairs={{0,4},{1,5},{2,6},{3,7},{4,0},{5,1},{6,2},{7,3},{8,12},{9,13},{10,... | collective-permute-start | bytes 184328 | tf_op jit(solution)/shard_map/ppermute | solution.py:29
  32.0 6.5 %collective-permute-start.9 = (bf16[5,48,128]{2,1,0:T(8,128)(2,1)S(1)}, bf16[5,48,128]{2,1,0:T(8,128)(2,1)S(1)}, u32[]{:S(2)}, u32[]{:S(2)}) collective-permute-start(bf16[5,48,128]{2,1,0:T(8,128)(2,1)S(1)} %get-tuple-element.44), channel_id=1, source_target_pairs={{0,6},{1,7},{2,4},{3,5},{4,2},{5,3},{6,0},{7,1},{8,14},{9,15},{10,... | collective-permute-start | bytes 184328 | tf_op jit(solution)/shard_map/ppermute | solution.py:29
  33.4 9.2 %collective-permute-start.12 = (bf16[5,48,128]{2,1,0:T(8,128)(2,1)S(1)}, bf16[5,48,128]{2,1,0:T(8,128)(2,1)S(1)}, u32[]{:S(2)}, u32[]{:S(2)}) collective-permute-start(bf16[5,48,128]{2,1,0:T(8,128)(2,1)S(1)} %get-tuple-element.41), channel_id=1, source_target_pairs={{0,4},{1,5},{2,6},{3,7},{4,0},{5,1},{6,2},{7,3},{8,12},{9,13},{10,... | collective-permute-start | bytes 184328 | tf_op jit(solution)/shard_map/ppermute | solution.py:29
  37.2 5.8 %collective-permute-start.13 = (bf16[5,48,128]{2,1,0:T(8,128)(2,1)S(1)}, bf16[5,48,128]{2,1,0:T(8,128)(2,1)S(1)}, u32[]{:S(2)}, u32[]{:S(2)}) collective-permute-start(bf16[5,48,128]{2,1,0:T(8,128)(2,1)S(1)} %get-tuple-element.40), channel_id=1, source_target_pairs={{0,6},{1,7},{2,4},{3,5},{4,2},{5,3},{6,0},{7,1},{8,14},{9,15},{10,... | collective-permute-start | bytes 184328 | tf_op jit(solution)/shard_map/ppermute | solution.py:29
  37.2 5.8 %collective-permute-start.14 = (bf16[5,48,128]{2,1,0:T(8,128)(2,1)S(1)}, bf16[5,48,128]{2,1,0:T(8,128)(2,1)S(1)}, u32[]{:S(2)}, u32[]{:S(2)}) collective-permute-start(bf16[5,48,128]{2,1,0:T(8,128)(2,1)S(1)} %get-tuple-element.39), channel_id=1, source_target_pairs={{0,2},{1,3},{2,0},{3,1},{4,6},{5,7},{6,4},{7,5},{8,10},{9,11},{10,... | collective-permute-start | bytes 184328 | tf_op jit(solution)/shard_map/ppermute | solution.py:29
  38.5 5.9 %collective-permute-start.11 = (bf16[5,48,128]{2,1,0:T(8,128)(2,1)S(1)}, bf16[5,48,128]{2,1,0:T(8,128)(2,1)S(1)}, u32[]{:S(2)}, u32[]{:S(2)}) collective-permute-start(bf16[5,48,128]{2,1,0:T(8,128)(2,1)S(1)} %get-tuple-element.37), channel_id=1, source_target_pairs={{0,8},{1,9},{2,10},{3,11},{4,12},{5,13},{6,14},{7,15},{8,0},{9,1},... | collective-permute-start | bytes 184328 | tf_op jit(solution)/shard_map/ppermute | solution.py:29

commit v7 on v6

--- a/solution.py
+++ b/solution.py
@@ -52,17 +52,20 @@
              (new_keys_at, new_keys), (new_values_at, new_values))
         )
     ]
-    pool = []
     cut = key_pool.shape[0] // POOL_CUTS
-    for c in range(POOL_CUTS):
-        part = pl.ds(c * cut, cut)
+    pools = [
+        [
+            pltpu.make_async_copy(
+                source.at[pl.ds(c * cut, cut)], target.at[pl.ds(c * cut, cut)],
+                pool_sems.at[side, c],
+            )
+            for c in range(POOL_CUTS)
+        ]
         for side, (source, target) in enumerate(
             ((key_pool_at, key_pool), (value_pool_at, value_pool))
-        ):
-            pool.append(
-                pltpu.make_async_copy(source.at[part], target.at[part], pool_sems.at[side, c])
-            )
-    for copy in wide[:2] + small + wide[2:] + pool:
+        )
+    ]
+    for copy in wide[:2] + small + wide[2:] + pools[0] + pools[1]:
         copy.start()
     for copy, target, source in zip(wide[:2], (heads_q, heads_r), (queries, residual)):
         copy.wait()
@@ -106,26 +109,23 @@
     for copy, side in zip(wide[2:], (0, 1)):
         copy.wait()
         fresh[side] = (new_keys, new_values)[side][...].astype(F32)
-    for copy in pool:
-        copy.wait()
     inside = lax.broadcasted_iota(jnp.int32, (page, key_pool.shape[2]), 0)
-    for r in range(rows):
-        length = lengths[r]
-        last = length // page
-        number = table[last, r]
-        here = inside == length - last * page
-        for side, buffer in enumerate((key_pool, value_pool)):
+    for side, buffer in enumerate((key_pool, value_pool)):
+        for copy in pools[side]:
+            copy.wait()
+        for r in range(rows):
+            length = lengths[r]
+            last = length // page
+            number = table[last, r]
+            here = inside == length - last * page
             block = buffer[number].astype(F32)
             buffer[number] = jnp.where(here, fresh[side, r:r + 1, :], block).astype(BF16)
-    for m in range(moves):
-        request = migrate[m]
-        length = lengths[request]
-        for p in range(pages):
-            number = table[p, request]
-            kept = inside + p * page <= length
-            for side, buffer in enumerate((key_pool, value_pool)):
-                group, place = PLACES[side * moves + m]
-                block = jnp.where(kept, buffer[number].astype(F32), 0.0)
+        for m in range(moves):
+            request = migrate[m]
+            group, place = PLACES[side * moves + m]
+            for p in range(pages):
+                kept = inside + p * page <= lengths[request]
+                block = jnp.where(kept, buffer[table[p, request]].astype(F32), 0.0)
                 moved[group][place, p * page:(p + 1) * page, :] = block.astype(BF16)
 
 

time: 46.1 us -> 46 us (level)
  transfers between devices with their start and end apart: 16 -> 16, of which waited for: 9 -> 8; matrix products, arithmetic and copies ran while one was open for 1% -> 1% of each run, Pallas kernels for 27% -> 27%
where the time goes in v7:
time: 46 us; the launch traced here: 45.8 us
  starting transfers between devices  19.5 us (42%)
  Pallas kernels  13.8 us (30%)
  waiting for transfers between devices  11.3 us (25%)
  between operations  0.81 us (2%)
    ppermute x14, starting transfers between devices, exchanged(): return lax.ppermute(array, 'attn', [(i, i ^ mask) for i in range(length)])  19.3 us
    ppermute x14, waiting for transfers between devices, exchanged(): return lax.ppermute(array, 'attn', [(i, i ^ mask) for i in range(length)])  9.86 us
    pallas_call x1, Pallas kernels, staged(): pl.pallas_call(stage_kernel, out_shape=(jax.ShapeDtypeStruct((pages + 5,...  3.92 us
    pallas_call x2, Pallas kernels, attended(): pl.pallas_call(kernel, out_shape=attend_shapes(rows, heads)[:outs], in_sp...  3.82 us
    pallas_call x1, Pallas kernels, expert_parts(): pl.pallas_call(functools.partial(expert_kernel, block), out_shape=jax.Sha...  3.46 us
    pallas_call x1, Pallas kernels, finished(): pl.pallas_call(functools.partial(finish_kernel, len(owns)), out_shape=jax...  1.57 us
    ppermute x1, waiting for transfers between devices, body(): arrived[0] = lax.ppermute(leave[0], 'attn', along)  1.47 us
    pallas_call x1, Pallas kernels, delivered(): pl.pallas_call(functools.partial(deliver_kernel, len(arrived)), out_shape...  1 us
  transfers between devices with their start and end apart: 16, of which 8 were waited for; matrix products, arithmetic and copies ran while one was open for 1% of the time, Pallas kernels for 27%

profile of v7, /device:TPU:0, one launch (start us, length us, event | category | flops | bytes accessed | tf_op | source)
XLA Modules:
  0.0 45.8 jit_solution(3408375766093504050)
XLA Ops:
  0.6 0.0 copy-start
  0.6 0.5 %collective-permute-start.2 = (bf16[6144,128]{1,0:T(8,128)(2,1)}, bf16[6144,128]{1,0:T(8,128)(2,1)S(1)}, u32[]{:S(2)}, u32[]{:S(2)}) collective-permute-start(bf16[6144,128]{1,0:T(8,128)(2,1)} %rest_0_.1), channel_id=1, source_target_pairs={{0,1},{1,0},{2,3},{3,2},{4,5},{5,4},{6,7},{7,6},{8,9},{9,8},{10,11... | collective-permute-start | bytes 4718600 | tf_op jit(solution)/shard_map/ppermute | solution.py:29
  1.2 0.1 collective-permute-start.3
  1.2 0.4 collective-permute-start.4
  1.7 3.9 %shard_map.157 = (s32[13,12]{1,0:T(8,128)S(1)}, bf16[96,16,1024]{2,1,0:T(8,128)(2,1)S(1)}, bf16[96,16,1024]{2,1,0:T(8,128)(2,1)S(1)}, f32[576,128]{1,0:T(8,128)S...) custom-call(s32[8,12]{1,0:T(8,128)} %bitcast.15, s32[12]{0:T(128)} %lengths_at.1, ...), custom_call_target="tpu_custom_call" | custom-call | bytes 8388608 | tf_op jit(solution)/shard_map/pallas_call | solution.py:151
  5.6 0.1 collective-permute-start.1
  5.7 1.8 %shard_map.158 = (f32[12,48,128]{2,1,0:T(8,128)S(1)}, bf16[12,48,128]{2,1,0:T(8,128)(2,1)S(1)}, bf16[5,48,128]{2,1,0:T(8,128)(2,1)S(1)}, bf16[5,48,128]{2,1,0:T(8,128)(2,1)S(1)}) custom-call(s32[13,12]{1,0:T(8,128)S(1)} %get-tuple-element.19.plan, bf16[96,16,1024]{2,1,0:T(8,128)(2,1)S(1)} %get-tuple-element.20.key_pool, ...), custom_call_target="tpu_custom_call" | custom-call | flops 1048576 | bytes 65536 | tf_op jit(solution)/shard_map/pallas_call | solution.py:291
  7.6 4.1 %collective-permute-start = (bf16[5,48,128]{2,1,0:T(8,128)(2,1)S(1)}, bf16[5,48,128]{2,1,0:T(8,128)(2,1)S(1)}, u32[]{:S(2)}, u32[]{:S(2)}) collective-permute-start(bf16[5,48,128]{2,1,0:T(8,128)(2,1)S(1)} %get-tuple-element.29), channel_id=1, source_target_pairs={{0,8},{1,9},{2,10},{3,11},{4,12},{5,13},{6,14},{7,15},{8,0},{9,1},... | collective-permute-start | bytes 184328 | tf_op jit(solution)/shard_map/ppermute | solution.py:29
  11.7 2.0 %shard_map.159 = (f32[12,48,128]{2,1,0:T(8,128)S(1)}, bf16[12,48,128]{2,1,0:T(8,128)(2,1)S(1)}, bf16[5,48,128]{2,1,0:T(8,128)(2,1)S(1)}) custom-call(s32[13,12]{1,0:T(8,128)S(1)} %get-tuple-element.19.plan, bf16[96,16,1024]{2,1,0:T(8,128)(2,1)S(1)} %get-tuple-element.20.key_pool, bf16[96,16,1024]{2,1,0:T(8,128)(2,1)S(1)} %get-tuple-element.21.value_pool, ...), custom_call_target="tpu_custom_call" | custom-call | flops 1048576 | bytes 65536 | tf_op jit(solution)/shard_map/pallas_call | solution.py:291
  13.7 0.4 collective-permute-done.away
  14.0 1.5 %collective-permute-done.1.rest_0_.refs_0_ = bf16[1,128,1024]{2,1,0:T(8,128)(2,1)S(1)} collective-permute-done((bf16[1,128,1024]{2,1,0:T(8,128)(2,1)S(1)}, bf16[1,128,1024]{2,1,0:T(8,128)(2,1)S(1)}, u32[]{:S(2)}, u32[]{:S(2)}) %collective-permute-start.1) | collective-permute-done | bytes 262176 | tf_op jit(solution)/shard_map/ppermute | solution.py:516
  15.5 3.2 %collective-permute-start.5 = (bf16[10,48,128]{2,1,0:T(8,128)(2,1)S(1)}, bf16[10,48,128]{2,1,0:T(8,128)(2,1)S(1)}, u32[]{:S(2)}, u32[]{:S(2)}) collective-permute-start(bf16[10,48,128]{2,1,0:T(8,128)(2,1)S(1)} %shard_map.160.refs_1_.refs_0_), channel_id=1, source_target_pairs={{0,2},{1,3},{2,0},{3,1},{4,6},{5,7},{6,4},{7,5},{8,10},{9,11},{10,... | collective-permute-start | bytes 368648 | tf_op jit(solution)/shard_map/ppermute | solution.py:29
  18.6 1.5 %collective-permute-start.7 = (bf16[10,48,128]{2,1,0:T(8,128)(2,1)S(1)}, bf16[10,48,128]{2,1,0:T(8,128)(2,1)S(1)}, u32[]{:S(2)}, u32[]{:S(2)}) collective-permute-start(bf16[10,48,128]{2,1,0:T(8,128)(2,1)S(1)} %shard_map.160.refs_1_.refs_0_), channel_id=1, source_target_pairs={{0,6},{1,7},{2,4},{3,5},{4,2},{5,3},{6,0},{7,1},{8,14},{9,15},{10,... | collective-permute-start | bytes 368648 | tf_op jit(solution)/shard_map/ppermute | solution.py:29
  20.2 0.1 collective-permute-start.15
  20.3 0.0 copy-start.1
  20.3 1.9 %collective-permute-done.5.refs_1_ = bf16[10,48,128]{2,1,0:T(8,128)(2,1)S(1)} collective-permute-done((bf16[10,48,128]{2,1,0:T(8,128)(2,1)S(1)}, bf16[10,48,128]{2,1,0:T(8,128)(2,1)S(1)}, u32[]{:S(2)}, u32[]{:S(2)}) %collective-permute-start.5) | collective-permute-done | bytes 122912 | tf_op jit(solution)/shard_map/ppermute | solution.py:29
  22.2 2.6 %collective-permute-done.6.refs_2_ = bf16[10,48,128]{2,1,0:T(8,128)(2,1)S(1)} collective-permute-done((bf16[10,48,128]{2,1,0:T(8,128)(2,1)S(1)}, bf16[10,48,128]{2,1,0:T(8,128)(2,1)S(1)}, u32[]{:S(2)}, u32[]{:S(2)}) %collective-permute-start.6) | collective-permute-done | bytes 122912 | tf_op jit(solution)/shard_map/ppermute | solution.py:29
  24.9 1.3 %collective-permute-done.7.refs_3_ = bf16[10,48,128]{2,1,0:T(8,128)(2,1)S(1)} collective-permute-done((bf16[10,48,128]{2,1,0:T(8,128)(2,1)S(1)}, bf16[10,48,128]{2,1,0:T(8,128)(2,1)S(1)}, u32[]{:S(2)}, u32[]{:S(2)}) %collective-permute-start.7) | collective-permute-done | bytes 122912 | tf_op jit(solution)/shard_map/ppermute | solution.py:29
  26.2 3.5 %shard_map.163 = bf16[40,48,128]{2,1,0:T(8,128)(2,1)S(1)} custom-call(bf16[40,48,128]{2,1,0:T(8,128)(2,1)S(1)} %shard_map.162.rows, bf16[6144,128]{1,0:T(8,128)(2,1)S(1)} %copy-done.1, bf16[6144,128]{1,0:T(8,128)(2,1)S(1)} %collective-permute-done.2.refs_2_.rest_1_, bf16[6144,128]{1,0:T(8,128)(2,1)S(1)} %copy-done.2, ...), custom_call_target="tpu_custom_call" | custom-call | flops 400000000 | bytes 10485760 | tf_op jit(solution)/shard_map/pallas_call | solution.py:347
  29.7 1.8 %collective-permute-start.10 = (bf16[5,48,128]{2,1,0:T(8,128)(2,1)S(1)}, bf16[5,48,128]{2,1,0:T(8,128)(2,1)S(1)}, u32[]{:S(2)}, u32[]{:S(2)}) collective-permute-start(bf16[5,48,128]{2,1,0:T(8,128)(2,1)S(1)} %get-tuple-element.43), channel_id=1, source_target_pairs={{0,2},{1,3},{2,0},{3,1},{4,6},{5,7},{6,4},{7,5},{8,10},{9,11},{10,... | collective-permute-start | bytes 184328 | tf_op jit(solution)/shard_map/ppermute | solution.py:29
  31.5 0.3 collective-permute-start.8
  31.8 1.4 %collective-permute-start.9 = (bf16[5,48,128]{2,1,0:T(8,128)(2,1)S(1)}, bf16[5,48,128]{2,1,0:T(8,128)(2,1)S(1)}, u32[]{:S(2)}, u32[]{:S(2)}) collective-permute-start(bf16[5,48,128]{2,1,0:T(8,128)(2,1)S(1)} %get-tuple-element.44), channel_id=1, source_target_pairs={{0,6},{1,7},{2,4},{3,5},{4,2},{5,3},{6,0},{7,1},{8,14},{9,15},{10,... | collective-permute-start | bytes 184328 | tf_op jit(solution)/shard_map/ppermute | solution.py:29
  33.3 1.7 %collective-permute-start.12 = (bf16[5,48,128]{2,1,0:T(8,128)(2,1)S(1)}, bf16[5,48,128]{2,1,0:T(8,128)(2,1)S(1)}, u32[]{:S(2)}, u32[]{:S(2)}) collective-permute-start(bf16[5,48,128]{2,1,0:T(8,128)(2,1)S(1)} %get-tuple-element.41), channel_id=1, source_target_pairs={{0,4},{1,5},{2,6},{3,7},{4,0},{5,1},{6,2},{7,3},{8,12},{9,13},{10,... | collective-permute-start | bytes 184328 | tf_op jit(solution)/shard_map/ppermute | solution.py:29
  35.0 0.2 select_reduce_fusion.1
  35.2 1.9 %collective-permute-done.10 = bf16[5,48,128]{2,1,0:T(8,128)(2,1)S(1)} collective-permute-done((bf16[5,48,128]{2,1,0:T(8,128)(2,1)S(1)}, bf16[5,48,128]{2,1,0:T(8,128)(2,1)S(1)}, u32[]{:S(2)}, u32[]{:S(2)}) %collective-permute-start.10) | collective-permute-done | bytes 61472 | tf_op jit(solution)/shard_map/ppermute | solution.py:29
  37.0 1.3 %collective-permute-start.14 = (bf16[5,48,128]{2,1,0:T(8,128)(2,1)S(1)}, bf16[5,48,128]{2,1,0:T(8,128)(2,1)S(1)}, u32[]{:S(2)}, u32[]{:S(2)}) collective-permute-start(bf16[5,48,128]{2,1,0:T(8,128)(2,1)S(1)} %get-tuple-element.39), channel_id=1, source_target_pairs={{0,2},{1,3},{2,0},{3,1},{4,6},{5,7},{6,4},{7,5},{8,10},{9,11},{10,... | collective-permute-start | bytes 184328 | tf_op jit(solution)/shard_map/ppermute | solution.py:29
  38.3 0.0 collective-permute-done.9
  38.4 3.0 %collective-permute-start.11 = (bf16[5,48,128]{2,1,0:T(8,128)(2,1)S(1)}, bf16[5,48,128]{2,1,0:T(8,128)(2,1)S(1)}, u32[]{:S(2)}, u32[]{:S(2)}) collective-permute-start(bf16[5,48,128]{2,1,0:T(8,128)(2,1)S(1)} %get-tuple-element.37), channel_id=1, source_target_pairs={{0,8},{1,9},{2,10},{3,11},{4,12},{5,13},{6,14},{7,15},{8,0},{9,1},... | collective-permute-start | bytes 184328 | tf_op jit(solution)/shard_map/ppermute | solution.py:29
  41.4 1.0 %shard_map.164 = (bf16[2,128,1024]{2,1,0:T(8,128)(2,1)}, bf16[2,128,1024]{2,1,0:T(8,128)(2,1)}) custom-call(bf16[1,128,1024]{2,1,0:T(8,128)(2,1)S(1)} %collective-permute-done.1.rest_0_.refs_0_, bf16[3,128,1024]{2,1,0:T(8,128)(2,1)S(1)} %collective-permute-done.15.refs_1_, f32[5,48,128]{2,1,0:T(8,128)S(1)} %get-tuple-element.38.refs_2_), custom_call_target="tpu_custom_call" | custom-call | tf_op jit(solution)/shard_map/pallas_call | solution.py:462
  42.5 0.4 collective-permute-done.13.rest_2_
  42.8 1.4 %collective-permute-done.11.away = bf16[5,48,128]{2,1,0:T(8,128)(2,1)S(1)} collective-permute-done((bf16[5,48,128]{2,1,0:T(8,128)(2,1)S(1)}, bf16[5,48,128]{2,1,0:T(8,128)(2,1)S(1)}, u32[]{:S(2)}, u32[]{:S(2)}) %collective-permute-start.11) | collective-permute-done | bytes 61472 | tf_op jit(solution)/shard_map/ppermute | solution.py:29
  44.2 1.6 %shard_map.165 = bf16[12,6144]{1,0:T(8,128)(2,1)} custom-call(s32[13,12]{1,0:T(8,128)S(1)} %get-tuple-element.19.plan, s32[1]{0:T(128)} %bitcast.2.mine, f32[2,12]{1,0:T(2,128)S(1)} %fusion.2.weights, f32[12,48,128]{2,1,0:T(8,128)S(1)} %get-tuple-element.31.state, bf16[5,48,128]{2,1,0:T(8,128)(2,1)S(1)} %collective-permute-done.11.away, ...), custom_call_target="tpu_custom_call" | custom-call | tf_op jit(solution)/shard_map/pallas_call | solution.py:436
  (25 shorter events, 0.2 us)
Async XLA Ops:
  0.6 34.3 %copy-start = (bf16[6144,8]{0,1:T(8,128)(2,1)S(1)}, bf16[6144,8]{0,1:T(8,128)(2,1)}, u32[]{:S(2)}) copy-start(bf16[6144,8]{0,1:T(8,128)(2,1)} %param.24) | copy-start | bytes 294916
  0.6 18.0 %collective-permute-start.2 = (bf16[6144,128]{1,0:T(8,128)(2,1)}, bf16[6144,128]{1,0:T(8,128)(2,1)S(1)}, u32[]{:S(2)}, u32[]{:S(2)}) collective-permute-start(bf16[6144,128]{1,0:T(8,128)(2,1)} %rest_0_.1), channel_id=1, source_target_pairs={{0,1},{1,0},{2,3},{3,2},{4,5},{5,4},{6,7},{7,6},{8,9},{9,8},{10,11... | collective-permute-start | bytes 4718600 | tf_op jit(solution)/shard_map/ppermute | solution.py:29
  1.2 19.0 %collective-permute-start.3 = (bf16[6144,128]{1,0:T(8,128)(2,1)}, bf16[6144,128]{1,0:T(8,128)(2,1)S(1)}, u32[]{:S(2)}, u32[]{:S(2)}) collective-permute-start(bf16[6144,128]{1,0:T(8,128)(2,1)} %rest_2_.1), channel_id=1, source_target_pairs={{0,1},{1,0},{2,3},{3,2},{4,5},{5,4},{6,7},{7,6},{8,9},{9,8},{10,11... | collective-permute-start | bytes 4718600 | tf_op jit(solution)/shard_map/ppermute | solution.py:29
  1.2 19.0 %collective-permute-start.4 = (bf16[128,6144]{1,0:T(8,128)(2,1)}, bf16[128,6144]{1,0:T(8,128)(2,1)}, u32[]{:S(2)}, u32[]{:S(2)}) collective-permute-start(bf16[128,6144]{1,0:T(8,128)(2,1)} %rest_4_.1), channel_id=1, source_target_pairs={{0,1},{1,0},{2,3},{3,2},{4,5},{5,4},{6,7},{7,6},{8,9},{9,8},{10,11... | collective-permute-start | bytes 4718600 | tf_op jit(solution)/shard_map/ppermute | solution.py:29
  5.6 9.9 %collective-permute-start.1 = (bf16[1,128,1024]{2,1,0:T(8,128)(2,1)S(1)}, bf16[1,128,1024]{2,1,0:T(8,128)(2,1)S(1)}, u32[]{:S(2)}, u32[]{:S(2)}) collective-permute-start(bf16[1,128,1024]{2,1,0:T(8,128)(2,1)S(1)} %get-tuple-element.30), channel_id=1, source_target_pairs={{0,1},{1,2},{2,3},{3,4},{4,5},{5,6},{6,7},{7,8},{8,9},{9,10},{10,1... | collective-permute-start | bytes 786440 | tf_op jit(solution)/shard_map/ppermute | solution.py:516
  7.6 6.4 %collective-permute-start = (bf16[5,48,128]{2,1,0:T(8,128)(2,1)S(1)}, bf16[5,48,128]{2,1,0:T(8,128)(2,1)S(1)}, u32[]{:S(2)}, u32[]{:S(2)}) collective-permute-start(bf16[5,48,128]{2,1,0:T(8,128)(2,1)S(1)} %get-tuple-element.29), channel_id=1, source_target_pairs={{0,8},{1,9},{2,10},{3,11},{4,12},{5,13},{6,14},{7,15},{8,0},{9,1},... | collective-permute-start | bytes 184328 | tf_op jit(solution)/shard_map/ppermute | solution.py:29
  11.7 8.5 %copy-start.4 = (s32[12,2]{0,1:T(2,128)S(1)}, s32[12,2]{0,1:T(2,128)}, u32[]{:S(2)}) copy-start(s32[12,2]{0,1:T(2,128)} %param.23) | copy-start | bytes 292
  15.5 6.8 %collective-permute-start.5 = (bf16[10,48,128]{2,1,0:T(8,128)(2,1)S(1)}, bf16[10,48,128]{2,1,0:T(8,128)(2,1)S(1)}, u32[]{:S(2)}, u32[]{:S(2)}) collective-permute-start(bf16[10,48,128]{2,1,0:T(8,128)(2,1)S(1)} %shard_map.160.refs_1_.refs_0_), channel_id=1, source_target_pairs={{0,2},{1,3},{2,0},{3,1},{4,6},{5,7},{6,4},{7,5},{8,10},{9,11},{10,... | collective-permute-start | bytes 368648 | tf_op jit(solution)/shard_map/ppermute | solution.py:29
  18.6 6.2 %collective-permute-start.6 = (bf16[10,48,128]{2,1,0:T(8,128)(2,1)S(1)}, bf16[10,48,128]{2,1,0:T(8,128)(2,1)S(1)}, u32[]{:S(2)}, u32[]{:S(2)}) collective-permute-start(bf16[10,48,128]{2,1,0:T(8,128)(2,1)S(1)} %shard_map.160.refs_1_.refs_0_), channel_id=1, source_target_pairs={{0,4},{1,5},{2,6},{3,7},{4,0},{5,1},{6,2},{7,3},{8,12},{9,13},{10,... | collective-permute-start | bytes 368648 | tf_op jit(solution)/shard_map/ppermute | solution.py:29
  18.6 7.5 %collective-permute-start.7 = (bf16[10,48,128]{2,1,0:T(8,128)(2,1)S(1)}, bf16[10,48,128]{2,1,0:T(8,128)(2,1)S(1)}, u32[]{:S(2)}, u32[]{:S(2)}) collective-permute-start(bf16[10,48,128]{2,1,0:T(8,128)(2,1)S(1)} %shard_map.160.refs_1_.refs_0_), channel_id=1, source_target_pairs={{0,6},{1,7},{2,4},{3,5},{4,2},{5,3},{6,0},{7,1},{8,14},{9,15},{10,... | collective-permute-start | bytes 368648 | tf_op jit(solution)/shard_map/ppermute | solution.py:29
  20.2 21.2 %collective-permute-start.15 = (bf16[3,128,1024]{2,1,0:T(8,128)(2,1)S(1)}, bf16[3,128,1024]{2,1,0:T(8,128)(2,1)S(1)}, u32[]{:S(2)}, u32[]{:S(2)}) collective-permute-start(bf16[3,128,1024]{2,1,0:T(8,128)(2,1)S(1)} %get-tuple-element.32), channel_id=1, source_target_pairs={{0,1},{1,2},{2,3},{3,4},{4,5},{5,6},{6,7},{7,8},{8,9},{9,10},{10,1... | collective-permute-start | bytes 2359304 | tf_op jit(solution)/shard_map/ppermute | solution.py:517
  20.3 5.9 %copy-start.1 = (bf16[6144,128]{1,0:T(8,128)(2,1)S(1)}, bf16[6144,128]{1,0:T(8,128)(2,1)}, u32[]{:S(2)}) copy-start(bf16[6144,128]{1,0:T(8,128)(2,1)} %rest_0_.1) | copy-start | bytes 4718596
  20.3 5.9 %copy-start.2 = (bf16[6144,128]{1,0:T(8,128)(2,1)S(1)}, bf16[6144,128]{1,0:T(8,128)(2,1)}, u32[]{:S(2)}) copy-start(bf16[6144,128]{1,0:T(8,128)(2,1)} %rest_2_.1) | copy-start | bytes 4718596
  20.3 5.9 %copy-start.3 = (bf16[128,6144]{1,0:T(8,128)(2,1)S(1)}, bf16[128,6144]{1,0:T(8,128)(2,1)}, u32[]{:S(2)}) copy-start(bf16[128,6144]{1,0:T(8,128)(2,1)} %rest_4_.1) | copy-start | bytes 4718596
  29.7 7.3 %collective-permute-start.10 = (bf16[5,48,128]{2,1,0:T(8,128)(2,1)S(1)}, bf16[5,48,128]{2,1,0:T(8,128)(2,1)S(1)}, u32[]{:S(2)}, u32[]{:S(2)}) collective-permute-start(bf16[5,48,128]{2,1,0:T(8,128)(2,1)S(1)} %get-tuple-element.43), channel_id=1, source_target_pairs={{0,2},{1,3},{2,0},{3,1},{4,6},{5,7},{6,4},{7,5},{8,10},{9,11},{10,... | collective-permute-start | bytes 184328 | tf_op jit(solution)/shard_map/ppermute | solution.py:29
  31.5 5.5 %collective-permute-start.8 = (bf16[5,48,128]{2,1,0:T(8,128)(2,1)S(1)}, bf16[5,48,128]{2,1,0:T(8,128)(2,1)S(1)}, u32[]{:S(2)}, u32[]{:S(2)}) collective-permute-start(bf16[5,48,128]{2,1,0:T(8,128)(2,1)S(1)} %get-tuple-element.45), channel_id=1, source_target_pairs={{0,4},{1,5},{2,6},{3,7},{4,0},{5,1},{6,2},{7,3},{8,12},{9,13},{10,... | collective-permute-start | bytes 184328 | tf_op jit(solution)/shard_map/ppermute | solution.py:29
  31.8 6.5 %collective-permute-start.9 = (bf16[5,48,128]{2,1,0:T(8,128)(2,1)S(1)}, bf16[5,48,128]{2,1,0:T(8,128)(2,1)S(1)}, u32[]{:S(2)}, u32[]{:S(2)}) collective-permute-start(bf16[5,48,128]{2,1,0:T(8,128)(2,1)S(1)} %get-tuple-element.44), channel_id=1, source_target_pairs={{0,6},{1,7},{2,4},{3,5},{4,2},{5,3},{6,0},{7,1},{8,14},{9,15},{10,... | collective-permute-start | bytes 184328 | tf_op jit(solution)/shard_map/ppermute | solution.py:29
  33.3 9.2 %collective-permute-start.12 = (bf16[5,48,128]{2,1,0:T(8,128)(2,1)S(1)}, bf16[5,48,128]{2,1,0:T(8,128)(2,1)S(1)}, u32[]{:S(2)}, u32[]{:S(2)}) collective-permute-start(bf16[5,48,128]{2,1,0:T(8,128)(2,1)S(1)} %get-tuple-element.41), channel_id=1, source_target_pairs={{0,4},{1,5},{2,6},{3,7},{4,0},{5,1},{6,2},{7,3},{8,12},{9,13},{10,... | collective-permute-start | bytes 184328 | tf_op jit(solution)/shard_map/ppermute | solution.py:29
  37.0 5.8 %collective-permute-start.13 = (bf16[5,48,128]{2,1,0:T(8,128)(2,1)S(1)}, bf16[5,48,128]{2,1,0:T(8,128)(2,1)S(1)}, u32[]{:S(2)}, u32[]{:S(2)}) collective-permute-start(bf16[5,48,128]{2,1,0:T(8,128)(2,1)S(1)} %get-tuple-element.40), channel_id=1, source_target_pairs={{0,6},{1,7},{2,4},{3,5},{4,2},{5,3},{6,0},{7,1},{8,14},{9,15},{10,... | collective-permute-start | bytes 184328 | tf_op jit(solution)/shard_map/ppermute | solution.py:29
  37.0 5.8 %collective-permute-start.14 = (bf16[5,48,128]{2,1,0:T(8,128)(2,1)S(1)}, bf16[5,48,128]{2,1,0:T(8,128)(2,1)S(1)}, u32[]{:S(2)}, u32[]{:S(2)}) collective-permute-start(bf16[5,48,128]{2,1,0:T(8,128)(2,1)S(1)} %get-tuple-element.39), channel_id=1, source_target_pairs={{0,2},{1,3},{2,0},{3,1},{4,6},{5,7},{6,4},{7,5},{8,10},{9,11},{10,... | collective-permute-start | bytes 184328 | tf_op jit(solution)/shard_map/ppermute | solution.py:29
  38.4 5.9 %collective-permute-start.11 = (bf16[5,48,128]{2,1,0:T(8,128)(2,1)S(1)}, bf16[5,48,128]{2,1,0:T(8,128)(2,1)S(1)}, u32[]{:S(2)}, u32[]{:S(2)}) collective-permute-start(bf16[5,48,128]{2,1,0:T(8,128)(2,1)S(1)} %get-tuple-element.37), channel_id=1, source_target_pairs={{0,8},{1,9},{2,10},{3,11},{4,12},{5,13},{6,14},{7,15},{8,0},{9,1},... | collective-permute-start | bytes 184328 | tf_op jit(solution)/shard_map/ppermute | solution.py:29
